TPU v7x, 32 devices: a whole 2x2x4 slice. The times are simulated.
32 devices in a mesh: batch: 4 (over y, core), space: 8 (over z, x).
Axes of the slice: x: 2, y: 2, z: 4, core: 2. Of those that a mesh axis runs over, the one named last changes fastest.
Arguments:
- features: bfloat16 [3, 32, 8, 16, 1024], P(None, 'batch', 'space'), may hold values from -30 to 30
- view_ids: int32 [3, 32], P(None, 'batch'), may hold values from 0 to 1, as said below
- w_reduce: bfloat16 [1024, 256], replicated, may hold values from -0.1875 to 0.1875
- w_spatial: bfloat16 [2304, 256], replicated, may hold values from -0.125 to 0.125
- w_expand: bfloat16 [256, 1024], replicated, may hold values from -0.375 to 0.375
- w_narrow: bfloat16 [1024, 512], replicated, may hold values from -0.1875 to 0.1875
- w_stride: bfloat16 [4608, 512], replicated, may hold values from -0.09375 to 0.09375
- w_widen: bfloat16 [512, 2048], replicated, may hold values from -0.25 to 0.25
- w_shortcut: bfloat16 [1024, 2048], replicated, may hold values from -0.1875 to 0.1875
- gain_reduce: float32 [256], replicated, may hold values from 0.5 to 1.5
- offset_reduce: float32 [256], replicated, may hold values from -3 to 3
- gain_spatial: float32 [256], replicated, may hold values from 0.5 to 1.5
- offset_spatial: float32 [256], replicated, may hold values from -3 to 3
- gain_expand: float32 [1024], replicated, may hold values from 0.5 to 1.5
- offset_expand: float32 [1024], replicated, may hold values from -3 to 3
- gain_narrow: float32 [512], replicated, may hold values from 0.5 to 1.5
- offset_narrow: float32 [512], replicated, may hold values from -3 to 3
- gain_stride: float32 [512], replicated, may hold values from 0.5 to 1.5
- offset_stride: float32 [512], replicated, may hold values from -3 to 3
- gain_widen: float32 [2048], replicated, may hold values from 0.5 to 1.5
- offset_widen: float32 [2048], replicated, may hold values from -3 to 3
- gain_shortcut: float32 [2048], replicated, may hold values from 0.5 to 1.5
- offset_shortcut: float32 [2048], replicated, may hold values from -3 to 3
- cotangent: bfloat16 [3, 32, 4, 8, 2048], P(None, ('batch', 'space')), may hold values from -6 to 6
Outputs:
- mapped: bfloat16 [3, 32, 4, 8, 2048], P(None, ('batch', 'space'))
- grad_features: bfloat16 [3, 32, 8, 16, 1024], P(None, 'batch', 'space')
- grad_w_reduce: float32 [1024, 256], P('space')
- grad_w_spatial: float32 [2304, 256], P('space')
- grad_w_expand: float32 [256, 1024], P('space')
- grad_w_narrow: float32 [1024, 512], P('space')
- grad_w_stride: float32 [4608, 512], P('space')
- grad_w_widen: float32 [512, 2048], P('space')
- grad_w_shortcut: float32 [1024, 2048], P('space')
- grad_gain_reduce: float32 [256], replicated
- grad_offset_reduce: float32 [256], replicated
- grad_gain_spatial: float32 [256], replicated
- grad_offset_spatial: float32 [256], replicated
- grad_gain_expand: float32 [1024], replicated
- grad_offset_expand: float32 [1024], replicated
- grad_gain_narrow: float32 [512], replicated
- grad_offset_narrow: float32 [512], replicated
- grad_gain_stride: float32 [512], replicated
- grad_offset_stride: float32 [512], replicated
- grad_gain_widen: float32 [2048], replicated
- grad_offset_widen: float32 [2048], replicated
- grad_gain_shortcut: float32 [2048], replicated
- grad_offset_shortcut: float32 [2048], replicated
Inputs may be any that keep to these rules, and one draw needn't show every extreme that they name: `view_ids`: in every micro-batch exactly 16 maps carry each view.
All inputs are finite; a program needn't handle non-finite values.
Results may differ from a plain program's by a relative error of at most 0.025.
Values may be sent and summed in bfloat16 or wider, within the bound.
No kernel may reach another device: no remote copies, remote signals or barrier semaphores. Data moves between devices by JAX's collectives and lax.ppermute only.
A program may use at most 256 MiB of HBM per device.

v0:
```python
import functools
import math

import jax
import jax.numpy as jnp
from jax import lax
from jax.experimental import pallas as pl
from jax.experimental.pallas import tpu as pltpu
from jax.sharding import Mesh
from jax.sharding import PartitionSpec as P

NVIEW = 2
MICRO = 3
EPSILON = 1e-05
BF = jnp.bfloat16
F32 = jnp.float32
BATCH, SPACE = ("bhi", "core"), ("shi", "slo")
ALL = BATCH + SPACE
LANES = 128
ROOT = math.sqrt(2.0 / math.pi)
CUBE = 0.044715


def dot(a, b, dims=((1,), (0,))):
    return lax.dot_general(a, b, (dims, ((), ())), preferred_element_type=F32)


def dot_nt(a, b):
    return dot(a, b, ((1,), (1,)))


def dot_tn(a, b):
    return dot(a, b, ((0,), (0,)))


def gelu(v):
    return 0.5 * v * (1.0 + jnp.tanh(ROOT * (v + CUBE * (v * v * v))))


def gelu_slope(v):
    square = v * v
    t = jnp.tanh(ROOT * (v + CUBE * (square * v)))
    return 0.5 * (1.0 + t) + (0.5 * ROOT) * v * (1.0 - t * t) * (1.0 + (3.0 * CUBE) * square)


def cols(c):
    return pl.ds(c * LANES, LANES)


def row(ref, r):
    return ref[pl.ds(r, 1), :]


class Kernel:
    def __init__(self, i, w, o, raw, scalars, stacks, extra, starts, sems):
        self.i, self.w, self.o, self.raw, self.s, self.st, self.x = i, w, o, raw, scalars, stacks, extra
        self.w_copies, self.out_pairs, self.sems = starts, {}, sems
        self.flying, self.sent = [], set()

    def wait_w(self, n=0):
        self.w_copies[n].wait()

    def send(self, n):
        src, dst, sem = self.out_pairs[n]
        copy = pltpu.make_async_copy(src, dst, sem)
        copy.start()
        self.flying.append(copy)
        self.sent.add(n)

    def copy(self, src, dst):
        copy = pltpu.make_async_copy(src, dst, self.sems.pop())
        copy.start()
        self.flying.append(copy)


def kernel_call(body, outs, args, weights=(), scratch=(), flops=0, raw=(), n_raw=0, scalars=(), passes=(), stacks=()):
    n_s, n_in, n_w, n_p = len(scalars), len(args), len(weights), len(passes)
    n_k = sum(map(len, stacks))
    n_out, n_r = len(outs), len(raw)

    def run(*refs):
        refs = list(refs)

        def take(n):
            part = refs[:n]
            del refs[:n]
            return part

        s, ins, w_any = take(n_s), take(n_in), take(n_w)
        piles = [take(len(g)) for g in stacks]
        take(n_p)
        out, raw_refs, _ = take(n_out), take(n_r), take(n_p)
        v_in, v_w, v_out, v_k = take(n_in), take(n_w), take(n_out), take(len(stacks))
        (sems,) = take(1)
        sem = [sems.at[j] for j in range(n_in + n_w + n_k + n_out + n_raw)]
        in_copies = [pltpu.make_async_copy(a, v, sem.pop(0)) for a, v in zip(ins, v_in)]
        for pile, v in zip(piles, v_k):
            for j, a in enumerate(pile):
                rows = a.shape[0]
                in_copies.append(pltpu.make_async_copy(a, v.at[pl.ds(j * rows, rows)], sem.pop(0)))
        w_copies = [pltpu.make_async_copy(a, v, sem.pop(0)) for a, v in zip(w_any, v_w)]
        for copy in in_copies + w_copies:
            copy.start()
        k = Kernel(v_in, v_w, v_out, raw_refs, s, v_k, refs, w_copies, sem[n_out:])
        k.out_pairs = {j: (v_out[j], out[j], sem[j]) for j in range(n_out)}
        for copy in in_copies:
            copy.wait()
        body(k)
        for j in range(n_out):
            if j not in k.sent:
                k.send(j)
        for copy in k.flying:
            copy.wait()

    def size(a):
        return math.prod(a.shape) * jnp.dtype(a.dtype).itemsize

    outside = pl.BlockSpec(memory_space=pl.ANY)
    piled = [arr(len(g) * g[0].shape[0], *g[0].shape[1:], dtype=g[0].dtype) for g in stacks]
    held = sum(map(size, (*args, *weights, *outs, *piled)))
    total = held + sum(size(a) for a in scratch if hasattr(a, "dtype"))
    first = n_s + n_in + n_w + n_k
    results = pl.pallas_call(
        run,
        out_shape=tuple(jax.ShapeDtypeStruct(o.shape, o.dtype) for o in (*outs, *raw, *passes)),
        in_specs=[pl.BlockSpec(memory_space=pltpu.SMEM)] * n_s + [outside] * (n_in + n_w + n_k + n_p),
        out_specs=tuple([outside] * (n_out + n_r + n_p)),
        scratch_shapes=[pltpu.VMEM(a.shape, a.dtype) for a in (*args, *weights, *outs, *piled)]
        + [pltpu.SemaphoreType.DMA((n_in + n_w + n_k + n_out + n_raw,))]
        + list(scratch),
        input_output_aliases={first + j: n_out + n_r + j for j in range(n_p)},
        cost_estimate=pl.CostEstimate(flops=flops, bytes_accessed=held, transcendentals=0),
        compiler_params=pltpu.CompilerParams(vmem_limit_bytes=max(60 * 2**20, total)),
    )(*scalars, *args, *weights, *(a for g in stacks for a in g), *passes)
    return tuple(results)


def arr(*shape, dtype=F32):
    return jax.ShapeDtypeStruct(shape, dtype)


def fill(pay_ref, rows_ref):
    block = rows_ref[...].astype(pay_ref.dtype)

    def step(j, _):
        pay_ref[j] = block
        return 0

    lax.fori_loop(0, pay_ref.shape[0], step, 0, unroll=8)


def stats_rows(value, rows_ref, r, size, offset):
    mean = jnp.sum(value, axis=0, keepdims=True) * (1.0 / size)
    away = value - mean
    rows_ref[pl.ds(r, 1), :] = mean
    rows_ref[pl.ds(r + offset, 1), :] = jnp.sum(away * away, axis=0, keepdims=True)


def stats_shape(q):
    return (6 * q, F32) if q < 4 else (9 * q, BF)


def stats_arr(n, q):
    rows, dtype = stats_shape(q)
    return arr(n, rows, LANES, dtype=dtype)


def fill_stats(pay_ref, rows_ref, q):
    k = MICRO * q
    if pay_ref.dtype == BF:
        mean, square = rows_ref[:k], rows_ref[k : 2 * k]
        high = mean.astype(BF).astype(F32)
        rows_ref[:k] = high
        rows_ref[k : 2 * k] = mean - high
        rows_ref[2 * k :] = square
    fill(pay_ref, rows_ref)


def merge_stats(got_ref, mates_ref, st_ref, q, size):
    n = got_ref.shape[0]
    k = MICRO * q
    mates = n // NVIEW
    step = 8

    def parts(at):
        got = got_ref[at].astype(F32)
        if got_ref.dtype == BF:
            return got[:, :k] + got[:, k : 2 * k], got[:, 2 * k : 3 * k]
        return got[:, :k], got[:, k : 2 * k]

    def one(i, acc):
        at = pl.ds(i * step, step)
        return acc + jnp.sum(mates_ref[at] * parts(at)[0], axis=0)

    mean = lax.fori_loop(0, n // step, one, jnp.zeros((k, LANES), F32), unroll=4) * (1.0 / mates)

    def two(i, acc):
        at = pl.ds(i * step, step)
        means, squares = parts(at)
        away = means - mean[None]
        return acc + jnp.sum(mates_ref[at] * (squares + size * (away * away)), axis=0)

    total = lax.fori_loop(0, n // step, two, jnp.zeros((k, LANES), F32), unroll=4)
    st_ref[:k] = mean
    st_ref[k : 2 * k] = lax.rsqrt(total * (1.0 / (mates * size)) + EPSILON)


def merge_sums(got_ref, mates_ref, sum_ref, q, size, total_refs):
    n = got_ref.shape[0]
    k = MICRO * q
    scale = 1.0 / (n // NVIEW * size)
    step = 8

    def one(i, carry):
        at = pl.ds(i * step, step)
        both = got_ref[at].astype(F32)
        first, second = both[:, :k], both[:, k : 2 * k]
        w = mates_ref[at]
        return (
            carry[0] + jnp.sum(w * first, axis=0),
            carry[1] + jnp.sum(w * second, axis=0),
            carry[2] + jnp.sum(first, axis=0),
            carry[3] + jnp.sum(second, axis=0),
        )

    zero = jnp.zeros((k, LANES), F32)
    a, b, ta, tb = lax.fori_loop(0, n // step, one, (zero,) * 4, unroll=4)
    sum_ref[:k] = a * scale
    sum_ref[k : 2 * k] = b * scale
    for ref, t in zip(total_refs, (ta, tb)):
        ref[...] = t[:q] + t[q : 2 * q] + t[2 * q :]


def shift_y(v, offset):
    if offset == 0:
        return v
    zero = jnp.zeros((8, v.shape[1]), v.dtype)
    if offset > 0:
        return jnp.concatenate([v[8:], zero], axis=0)
    return jnp.concatenate([zero, v[:-8]], axis=0)


def shift_x(v, offset):
    if offset == 0:
        return v
    place = lax.broadcasted_iota(jnp.int32, v.shape, 0) % 8
    if offset > 0:
        return jnp.where(place == 7, 0.0, pltpu.roll(v, v.shape[0] - 1, axis=0))
    return jnp.where(place == 0, 0.0, pltpu.roll(v, 1, axis=0))


def write_patches(phase, patch_ref, m, half, c, width, sign, out_phases=((0, 0), (0, 1), (1, 0), (1, 1))):
    moved = {}

    def get(sy, sx, ox):
        if (sy, sx, ox) not in moved:
            moved[sy, sx, ox] = shift_x(phase[sy, sx], ox)
        return moved[sy, sx, ox]

    for i, (py, px) in enumerate(out_phases):
        for r in range(3):
            for k in range(3):
                at_y, at_x = py + sign * (r - 1), px + sign * (k - 1)
                piece = shift_y(get(at_y % 2, at_x % 2, at_x // 2), at_y // 2)
                rows = pl.ds((m * len(out_phases) + i) * half, half)
                patch_ref[rows, pl.ds((r * 3 + k) * width + c * LANES, LANES)] = piece.astype(BF)


PHASES = ((0, 0), (0, 1), (1, 0), (1, 1))


class Sizes:
    pass


def k_reduce(x, ids, w, z):
    q = z.q1

    def body(k):
        (x_ref,), (map_ref, pay_ref), (tmp, rows_ref) = k.i, k.o, k.x
        k.wait_w()
        for y in range(z.height):
            product = dot(x_ref[y].reshape(MICRO * z.cols, z.c_in), k.w[0][...])
            for c in range(q):
                tmp[c, pl.ds(y * MICRO * z.cols, MICRO * z.cols), :] = product[:, c * LANES : (c + 1) * LANES]
        for m in range(MICRO):
            for y in range(z.height):
                for px in range(2):
                    at = m * z.rows + (2 * (y % 2) + px) * z.half + (y // 2) * 8
                    for c in range(q):
                        map_ref[pl.ds(at, 8), cols(c)] = tmp[
                            c, pl.ds((y * MICRO + m) * z.cols + px, 8, stride=2), :
                        ]
        rows_ref[...] = jnp.zeros(rows_ref.shape, F32)
        for m in range(MICRO):
            for c in range(q):
                stats_rows(map_ref[pl.ds(m * z.rows, z.rows), cols(c)], rows_ref, m * q + c, z.rows, MICRO * q)
        for m in range(MICRO):
            rows_ref[pl.ds(6 * q + m, 1), :] = jnp.full((1, LANES), k.s[0][m], F32)
        fill(pay_ref, rows_ref)

    rows, pad = MICRO * z.rows, 16
    return kernel_call(
        body,
        [arr(rows, z.c_mid), arr(z.n, pad, LANES)],
        [x],
        [w],
        [pltpu.VMEM((q, rows, LANES), F32), pltpu.VMEM((pad, LANES), F32)],
        flops=2 * rows * z.c_in * z.c_mid,
        scalars=[ids],
    )


def k_spatial(got, ids, pre, gain, offset, w, z):
    q = z.q1

    def body(k):
        got_ref, pre_ref, g_ref, o_ref = k.i
        patch_ref, next_ref, pay_ref, st_ref, mates_ref = k.o
        (rows_ref,) = k.x
        same = []
        for m in range(MICRO):
            view = got_ref[:, pl.ds(6 * q + m, 1), :]
            same += [(view == k.s[0][m]).astype(F32)] * q
        mates_ref[...] = jnp.concatenate(same, axis=1)
        merge_stats(got_ref, mates_ref, st_ref, q, z.rows)
        for m in range(MICRO):
            for c in range(q):
                mean, inverse = row(st_ref, m * q + c), row(st_ref, (MICRO + m) * q + c)
                phase = {}
                for i, p in enumerate(PHASES):
                    x = pre_ref[pl.ds(m * z.rows + i * z.half, z.half), cols(c)]
                    phase[p] = gelu(g_ref[:, cols(c)] * ((x - mean) * inverse) + o_ref[:, cols(c)])
                write_patches(phase, patch_ref, m, z.half, c, z.c_mid, 1)
        k.send(0)
        k.wait_w()
        next_ref[...] = dot(patch_ref[...], k.w[0][...])
        k.send(1)
        for m in range(MICRO):
            for c in range(q):
                stats_rows(next_ref[pl.ds(m * z.rows, z.rows), cols(c)], rows_ref, m * q + c, z.rows, MICRO * q)
        fill_stats(pay_ref, rows_ref, q)

    rows = MICRO * z.rows
    return kernel_call(
        body,
        [arr(rows, 9 * z.c_mid, dtype=BF), arr(rows, z.c_mid), stats_arr(z.n, q), arr(6 * q, LANES), arr(z.n, 3 * q, LANES)],
        [got, pre, gain, offset],
        [w],
        [pltpu.VMEM((stats_shape(q)[0], LANES), F32)],
        flops=2 * rows * 9 * z.c_mid * z.c_mid,
        scalars=[ids],
    )


def k_expand(got, mates, pre, gain, offset, w, z):
    q, qo = z.q1, z.q3

    def body(k):
        got_ref, mates_ref, pre_ref, g_ref, o_ref = k.i
        act_ref, next_ref, pay_ref, st_ref = k.o
        (rows_ref,) = k.x
        merge_stats(got_ref, mates_ref, st_ref, q, z.rows)
        for m in range(MICRO):
            for c in range(q):
                mean, inverse = row(st_ref, m * q + c), row(st_ref, (MICRO + m) * q + c)
                at = pl.ds(m * z.rows, z.rows)
                x = pre_ref[at, cols(c)]
                act_ref[at, cols(c)] = gelu(g_ref[:, cols(c)] * ((x - mean) * inverse) + o_ref[:, cols(c)]).astype(BF)
        k.send(0)
        k.wait_w()
        next_ref[...] = dot(act_ref[...], k.w[0][...])
        k.send(1)
        for m in range(MICRO):
            for c in range(qo):
                stats_rows(next_ref[pl.ds(m * z.rows, z.rows), cols(c)], rows_ref, m * qo + c, z.rows, MICRO * qo)
        fill_stats(pay_ref, rows_ref, qo)

    rows = MICRO * z.rows
    return kernel_call(
        body,
        [arr(rows, z.c_mid, dtype=BF), arr(rows, z.c_in), stats_arr(z.n, qo), arr(6 * q, LANES)],
        [got, mates, pre, gain, offset],
        [w],
        [pltpu.VMEM((stats_shape(qo)[0], LANES), F32)],
        flops=2 * rows * z.c_in * z.c_mid,
    )


def k_narrow(got, mates, pre, gain, offset, maps_in, w, z):
    q, qo = z.q3, z.q4

    def body(k):
        got_ref, mates_ref, pre_ref, g_ref, o_ref, in_ref = k.i
        res_ref, join_ref, even_ref, next_ref, pay_ref, st_ref = k.o
        (rows_ref,) = k.x
        merge_stats(got_ref, mates_ref, st_ref, q, z.rows)
        for m in range(MICRO):
            for c in range(q):
                mean, inverse = row(st_ref, m * q + c), row(st_ref, (MICRO + m) * q + c)
                at = pl.ds(m * z.rows, z.rows)
                x = pre_ref[at, cols(c)]
                res = g_ref[:, cols(c)] * ((x - mean) * inverse) + o_ref[:, cols(c)] + in_ref[at, cols(c)].astype(F32)
                res_ref[at, cols(c)] = res
                joined = gelu(res).astype(BF)
                join_ref[at, cols(c)] = joined
                even_ref[pl.ds(m * z.half, z.half), cols(c)] = joined[: z.half]
        for j in range(3):
            k.send(j)
        k.wait_w()
        next_ref[...] = dot(join_ref[...], k.w[0][...])
        k.send(3)
        for m in range(MICRO):
            for c in range(qo):
                stats_rows(next_ref[pl.ds(m * z.rows, z.rows), cols(c)], rows_ref, m * qo + c, z.rows, MICRO * qo)
        fill_stats(pay_ref, rows_ref, qo)

    rows = MICRO * z.rows
    return kernel_call(
        body,
        [
            arr(rows, z.c_in),
            arr(rows, z.c_in, dtype=BF),
            arr(MICRO * z.half, z.c_in, dtype=BF),
            arr(rows, z.c_wide),
            stats_arr(z.n, qo),
            arr(6 * q, LANES),
        ],
        [got, mates, pre, gain, offset, maps_in],
        [w],
        [pltpu.VMEM((stats_shape(qo)[0], LANES), F32)],
        flops=2 * rows * z.c_in * z.c_wide,
    )


def k_stride(got, mates, pre, gain, offset, w, z, passes=()):
    q = z.q4

    def body(k):
        got_ref, mates_ref, pre_ref, g_ref, o_ref = k.i
        act_ref, next_ref, pay_ref, st_ref = k.o
        patch_ref, rows_ref = k.x
        merge_stats(got_ref, mates_ref, st_ref, q, z.rows)
        for m in range(MICRO):
            for c in range(q):
                mean, inverse = row(st_ref, m * q + c), row(st_ref, (MICRO + m) * q + c)
                phase = {}
                for i, p in enumerate(PHASES):
                    x = pre_ref[pl.ds(m * z.rows + i * z.half, z.half), cols(c)]
                    phase[p] = gelu(g_ref[:, cols(c)] * ((x - mean) * inverse) + o_ref[:, cols(c)])
                    act_ref[pl.ds(m * z.rows + i * z.half, z.half), cols(c)] = phase[p].astype(BF)
                write_patches(phase, patch_ref, m, z.half, c, z.c_wide, 1, ((0, 0),))
        k.send(0)
        k.wait_w()
        next_ref[...] = dot(patch_ref[...], k.w[0][...])
        k.send(1)
        for m in range(MICRO):
            for c in range(q):
                stats_rows(next_ref[pl.ds(m * z.half, z.half), cols(c)], rows_ref, m * q + c, z.half, MICRO * q)
        fill_stats(pay_ref, rows_ref, q)

    rows = MICRO * z.half
    return kernel_call(
        body,
        [arr(MICRO * z.rows, z.c_wide, dtype=BF), arr(rows, z.c_wide), stats_arr(z.n, q), arr(6 * q, LANES)],
        [got, mates, pre, gain, offset],
        [w],
        [pltpu.VMEM((rows, 9 * z.c_wide), BF), pltpu.VMEM((stats_shape(q)[0], LANES), F32)],
        flops=2 * rows * 9 * z.c_wide * z.c_wide,
        passes=passes,
    )


def k_shortcut(even, w, z):
    def body(k):
        (e_ref,), (next_ref, st_ref) = k.i, k.o
        k.wait_w()
        next_ref[...] = dot(e_ref[...], k.w[0][...])
        for c in range(z.q6):
            for m in range(MICRO):
                stats_rows(next_ref[pl.ds(m * z.half, z.half), cols(c)], st_ref.at[c], m, z.half, MICRO)

    rows = MICRO * z.half
    return kernel_call(
        body, [arr(rows, z.c_out), arr(z.q6, 8, LANES)], [even], [w], flops=2 * rows * z.c_in * z.c_out
    )


def k_widen(got, mates, pre, gain, offset, short_st, w, z, passes=()):
    q = z.q4

    def body(k):
        got_ref, mates_ref, pre_ref, g_ref, o_ref, short_ref = k.i
        act_ref, next_ref, pay_ref, st_ref = k.o
        merge_stats(got_ref, mates_ref, st_ref, q, z.half)
        for m in range(MICRO):
            for c in range(q):
                mean, inverse = row(st_ref, m * q + c), row(st_ref, (MICRO + m) * q + c)
                at = pl.ds(m * z.half, z.half)
                x = pre_ref[at, cols(c)]
                act_ref[at, cols(c)] = gelu(g_ref[:, cols(c)] * ((x - mean) * inverse) + o_ref[:, cols(c)]).astype(BF)
        k.send(0)
        k.wait_w()
        next_ref[...] = dot(act_ref[...], k.w[0][...])
        k.send(1)
        for c in range(z.q6):
            for m in range(MICRO):
                stats_rows(next_ref[pl.ds(m * z.half, z.half), cols(c)], pay_ref.at[c], m, z.half, MICRO)
            pay_ref[z.q6 + c] = short_ref[c]
        chunks = 2 * z.q6
        for j in range(chunks, z.n):
            pay_ref[j] = pay_ref[j % chunks]

    rows = MICRO * z.half
    return kernel_call(
        body,
        [arr(rows, z.c_wide, dtype=BF), arr(rows, z.c_out), arr(z.n, 8, LANES), arr(6 * q, LANES)],
        [got, mates, pre, gain, offset, short_st],
        [w],
        flops=2 * rows * z.c_wide * z.c_out,
        passes=passes,
    )


def k_views(got, ids, z):
    def body(k):
        (got_ref, id_ref), (pay_ref,), (lo, hi) = k.i, k.o, k.x
        mates = z.n // NVIEW
        g, ids = got_ref[...], id_ref[...]
        for view, ref in ((0, lo), (1, hi)):
            w = (ids == float(view)).astype(F32)
            mean = jnp.sum(w * g, axis=0)[:MICRO] * (1.0 / mates)
            away = g[:, :MICRO] - mean[None]
            total = jnp.sum(w[:, :MICRO] * (g[:, MICRO : 2 * MICRO] + z.half * (away * away)), axis=0)
            ref[...] = jnp.zeros(ref.shape, F32)
            ref[:MICRO] = mean
            ref[MICRO : 2 * MICRO] = lax.rsqrt(total * (1.0 / (mates * z.half)) + EPSILON)
        pay_ref[...] = jnp.where(ids > 0.5, hi[...][None], lo[...][None])

    return kernel_call(
        body, [arr(z.n, 8, LANES)], [got, ids], scratch=[pltpu.VMEM((8, LANES), F32)] * 2
    )[0]


def k_mapped(whole, pre_w, pre_s, cot, gains, z, passes=()):
    def body(k):
        st_ref, w_ref, s_ref, cot_ref, gw, ow, gs, os = k.i
        map_ref, d_ref, pay_ref = k.o
        n_c = z.q6
        pay_ref[...] = jnp.zeros(pay_ref.shape, F32)
        for c in range(n_c):
            for m in range(MICRO):
                at = pl.ds(m * z.half, z.half)
                sw, ss = st_ref.at[c], st_ref.at[n_c + c]
                hat_w = (w_ref[at, cols(c)] - row(sw, m)) * row(sw, MICRO + m)
                hat_s = (s_ref[at, cols(c)] - row(ss, m)) * row(ss, MICRO + m)
                res = gw[:, cols(c)] * hat_w + ow[:, cols(c)] + (gs[:, cols(c)] * hat_s + os[:, cols(c)])
                map_ref[at, cols(c)] = gelu(res).astype(BF)
                d = gelu_slope(res) * cot_ref[at, cols(c)].astype(F32)
                d_ref[at, cols(c)] = d
                first, second = pay_ref.at[c], pay_ref.at[n_c + c]
                first[pl.ds(m, 1), :] = jnp.sum(d, axis=0, keepdims=True)
                first[pl.ds(MICRO + m, 1), :] = jnp.sum(d * hat_w, axis=0, keepdims=True)
                second[pl.ds(m, 1), :] = jnp.sum(d * hat_s, axis=0, keepdims=True)
        for j in range(2 * n_c, z.n):
            pay_ref[j] = pay_ref[j % (2 * n_c)]

    rows = MICRO * z.half
    return kernel_call(
        body,
        [arr(rows, z.c_out, dtype=BF), arr(rows, z.c_out), arr(z.n, 8, LANES)],
        [whole, pre_w, pre_s, cot, *gains],
        flops=rows * z.c_out * 60,
        passes=passes,
    )


def k_view_sums(got, ids, z):
    def body(k):
        (got_ref, id_ref), (pay_ref,), (both,) = k.i, k.o, k.x
        g, ids = got_ref[...], id_ref[...]
        lo = jnp.sum((ids == 0.0).astype(F32) * g, axis=0)
        hi = jnp.sum((ids == 1.0).astype(F32) * g, axis=0)
        both[0], both[1] = lo, hi
        all_views = lo + hi
        totals = []
        for k in range(2):
            totals.append(jnp.sum(all_views[k * MICRO : (k + 1) * MICRO], axis=0, keepdims=True))
        for v in range(2):
            for k in range(2):
                both[v, pl.ds(2 * MICRO + k, 1), :] = totals[k]
        pay_ref[...] = jnp.where(ids > 0.5, both[1][None], both[0][None])

    return kernel_call(body, [arr(z.n, 8, LANES)], [got, ids], scratch=[pltpu.VMEM((2, 8, LANES), F32)])[0]


def back_rows(x, d, st_ref, sum_ref, m, q, c, gain):
    inverse = row(st_ref, (MICRO + m) * q + c)
    hat = (x - row(st_ref, m * q + c)) * inverse
    return gain * inverse * (d - row(sum_ref, m * q + c) - hat * row(sum_ref, (MICRO + m) * q + c))


def sum_rows(d, hat, rows_ref, r, offset):
    rows_ref[pl.ds(r, 1), :] = jnp.sum(d, axis=0, keepdims=True)
    rows_ref[pl.ds(r + offset, 1), :] = jnp.sum(d * hat, axis=0, keepdims=True)


def slope_and_sums(d_out, pre_ref, at, st_ref, m, q, c, g_ref, o_ref, d_ref, rows_ref):
    hat = (pre_ref[at, cols(c)] - row(st_ref, m * q + c)) * row(st_ref, (MICRO + m) * q + c)
    d = gelu_slope(g_ref[:, cols(c)] * hat + o_ref[:, cols(c)]) * d_out
    d_ref[at, cols(c)] = d
    sum_rows(d, hat, rows_ref, m * q + c, MICRO * q)


def k_back_widen(whole, sums, d_two, pre_w, pre_s, gain_w, gain_s, pre, st, gain, offset, place, w, z, passes=()):
    q, n_c = z.q4, z.q6

    def body(k):
        st2, sum_ref, d_ref, w_ref, s_ref, gw, gs, pre_ref, st_ref, g_ref, o_ref = k.i
        ds_ref, t_off, t_gw, t_gs, d_next, pay_ref = k.o
        dw_ref, rows_ref, tmp = k.x
        scale = 1.0 / (z.n // NVIEW * z.half)
        for c in range(n_c):
            first, second = sum_ref.at[c], sum_ref.at[n_c + c]
            t_off[pl.ds(c, 1), :] = row(first, 2 * MICRO)
            t_gw[pl.ds(c, 1), :] = row(first, 2 * MICRO + 1)
            t_gs[pl.ds(c, 1), :] = row(second, 2 * MICRO)
            sw, ss = st2.at[c], st2.at[n_c + c]
            for m in range(MICRO):
                at = pl.ds(m * z.half, z.half)
                inv_w, inv_s = row(sw, MICRO + m), row(ss, MICRO + m)
                hat_w = (w_ref[at, cols(c)] - row(sw, m)) * inv_w
                hat_s = (s_ref[at, cols(c)] - row(ss, m)) * inv_s
                d = d_ref[at, cols(c)] - row(first, m) * scale
                dw_ref[at, cols(c)] = (
                    gw[:, cols(c)] * inv_w * (d - hat_w * (row(first, MICRO + m) * scale))
                ).astype(BF)
                ds_ref[at, cols(c)] = (gs[:, cols(c)] * inv_s * (d - hat_s * (row(second, m) * scale))).astype(BF)
        k.send(0)
        some = z.c_out // z.g
        for j in range(z.g):
            at = pl.ds(pl.multiple_of(((k.s[0][0] & (z.g - 1)) ^ j) * some, some), some)
            k.copy(dw_ref.at[:, at], k.raw[j].at[:, pl.ds(0, some)])
            k.copy(ds_ref.at[:, at], k.raw[j].at[:, pl.ds(some, some)])
        k.wait_w()
        tmp[...] = dot_nt(dw_ref[...], k.w[0][...])
        for m in range(MICRO):
            at = pl.ds(m * z.half, z.half)
            for c in range(q):
                slope_and_sums(tmp[at, cols(c)], pre_ref, at, st_ref, m, q, c, g_ref, o_ref, d_next, rows_ref)
        fill(pay_ref, rows_ref)

    rows = MICRO * z.half
    return kernel_call(
        body,
        [arr(rows, z.c_out, dtype=BF)]
        + [arr(n_c, LANES)] * 3
        + [arr(rows, z.c_wide), arr(z.n, 6 * q, LANES, dtype=BF)],
        [whole, sums, d_two, pre_w, pre_s, gain_w, gain_s, pre, st, gain, offset],
        [w],
        [
            pltpu.VMEM((rows, z.c_out), BF),
            pltpu.VMEM((6 * q, LANES), F32),
            pltpu.VMEM((rows, z.c_wide), F32),
        ],
        flops=2 * rows * z.c_wide * z.c_out,
        raw=[arr(rows, 2 * z.c_out // z.g, dtype=BF)] * z.g,
        n_raw=2 * z.g,
        scalars=[place],
        passes=passes,
    )


def back_start(refs, mates_ref, sum_ref, out_ref, q, n_rows, totals):
    got_ref, d_ref, pre_ref, st_ref, g_ref = refs
    merge_sums(got_ref, mates_ref, sum_ref, q, n_rows, totals)
    for m in range(MICRO):
        at = pl.ds(m * n_rows, n_rows)
        for c in range(q):
            out_ref[at, cols(c)] = back_rows(
                pre_ref[at, cols(c)], d_ref[at, cols(c)], st_ref, sum_ref, m, q, c, g_ref[:, cols(c)]
            ).astype(BF)


def k_back_stride(got, mates, d, pre_s, st_s, gain_s, pre, st, gain, offset, place, w, z, passes=()):
    q = z.q4

    def body(k):
        got_ref, mates_ref, d_ref, ps_ref, ss_ref, gs_ref, pre_ref, st_ref, g_ref, o_ref = k.i
        t_off, t_gain, d_next, pay_ref = k.o
        delta_ref, rows_ref, sum_ref, contrib = k.x
        back_start((got_ref, d_ref, ps_ref, ss_ref, gs_ref), mates_ref, sum_ref, delta_ref, q, z.half, (t_off, t_gain))
        some = z.c_wide // z.g
        for j in range(z.g):
            at = pl.ds(pl.multiple_of(((k.s[0][0] & (z.g - 1)) ^ j) * some, some), some)
            k.copy(delta_ref.at[:, at], k.raw[j])
        k.wait_w()
        contrib[...] = dot_nt(delta_ref[...], k.w[0][...])
        for m in range(MICRO):
            for c in range(q):
                phase = {}
                for r in range(3):
                    for k in range(3):
                        piece = contrib[pl.ds(m * z.half, z.half), pl.ds((r * 3 + k) * z.c_wide + c * LANES, LANES)]
                        piece = shift_x(shift_y(piece, 1 if r == 0 else 0), 1 if k == 0 else 0)
                        p = ((r + 1) % 2, (k + 1) % 2)
                        phase[p] = piece if p not in phase else phase[p] + piece
                first = second = 0.0
                mean, inverse = row(st_ref, m * q + c), row(st_ref, (MICRO + m) * q + c)
                for i, p in enumerate(PHASES):
                    at = pl.ds(m * z.rows + i * z.half, z.half)
                    hat = (pre_ref[at, cols(c)] - mean) * inverse
                    grad = gelu_slope(g_ref[:, cols(c)] * hat + o_ref[:, cols(c)]) * phase[p]
                    d_next[at, cols(c)] = grad
                    first = first + jnp.sum(grad, axis=0, keepdims=True)
                    second = second + jnp.sum(grad * hat, axis=0, keepdims=True)
                rows_ref[pl.ds(m * q + c, 1), :] = first
                rows_ref[pl.ds((MICRO + m) * q + c, 1), :] = second
        fill(pay_ref, rows_ref)

    rows = MICRO * z.half
    return kernel_call(
        body,
        [arr(q, LANES)] * 2
        + [arr(MICRO * z.rows, z.c_wide), arr(z.n, 6 * q, LANES, dtype=BF)],
        [got, mates, d, pre_s, st_s, gain_s, pre, st, gain, offset],
        [w],
        [
            pltpu.VMEM((rows, z.c_wide), BF),
            pltpu.VMEM((6 * q, LANES), F32),
            pltpu.VMEM((6 * q, LANES), F32),
            pltpu.VMEM((rows, 9 * z.c_wide), F32),
        ],
        flops=2 * rows * 9 * z.c_wide * z.c_wide,
        passes=passes,
        raw=[arr(rows, z.c_wide // z.g, dtype=BF)] * z.g,
        n_raw=z.g,
        scalars=[place],
    )


def k_back_narrow(got, mates, d, pre_n, st_n, gain_n, even, res, pre, st, w, z, passes=()):
    q, qo = z.q4, z.q3

    def body(k):
        got_ref, mates_ref, d_ref, pn_ref, sn_ref, gn_ref, even_ref, res_ref, pre_ref, st_ref = k.i
        delta_ref, t_off, t_gain, d_next, pay_ref = k.o
        rows_ref, sum_ref, tmp = k.x
        back_start((got_ref, d_ref, pn_ref, sn_ref, gn_ref), mates_ref, sum_ref, delta_ref, q, z.rows, (t_off, t_gain))
        k.send(0)
        k.wait_w()
        tmp[...] = dot_nt(delta_ref[...], k.w[0][...])
        for m in range(MICRO):
            at = pl.ds(m * z.rows, z.rows)
            some = pl.ds(m * z.rows, z.half)
            for c in range(qo):
                tmp[some, cols(c)] = tmp[some, cols(c)] + even_ref[pl.ds(m * z.half, z.half), cols(c)]
                d_join = tmp[at, cols(c)].astype(BF).astype(F32)
                one = gelu_slope(res_ref[at, cols(c)]) * d_join
                hat = (pre_ref[at, cols(c)] - row(st_ref, m * qo + c)) * row(st_ref, (MICRO + m) * qo + c)
                d_next[at, cols(c)] = one
                sum_rows(one, hat, rows_ref, m * qo + c, MICRO * qo)
        fill(pay_ref, rows_ref)

    rows = MICRO * z.rows
    return kernel_call(
        body,
        [arr(rows, z.c_wide, dtype=BF)] + [arr(q, LANES)] * 2 + [arr(rows, z.c_in), arr(z.n, 6 * qo, LANES, dtype=BF)],
        [got, mates, d, pre_n, st_n, gain_n, even, res, pre, st],
        [w],
        [
            pltpu.VMEM((6 * qo, LANES), F32),
            pltpu.VMEM((6 * q, LANES), F32),
            pltpu.VMEM((rows, z.c_in), F32),
        ],
        flops=2 * rows * z.c_in * z.c_wide,
        passes=passes,
    )


def k_back_expand(got, mates, d, pre_e, st_e, gain_e, pre, st, gain, offset, w, z, passes=()):
    q, qo = z.q3, z.q1

    def body(k):
        got_ref, mates_ref, d_ref, pe_ref, se_ref, ge_ref, pre_ref, st_ref, g_ref, o_ref = k.i
        delta_ref, t_off, t_gain, d_next, pay_ref = k.o
        rows_ref, sum_ref, tmp = k.x
        back_start((got_ref, d_ref, pe_ref, se_ref, ge_ref), mates_ref, sum_ref, delta_ref, q, z.rows, (t_off, t_gain))
        k.send(0)
        k.wait_w()
        tmp[...] = dot_nt(delta_ref[...], k.w[0][...])
        for m in range(MICRO):
            at = pl.ds(m * z.rows, z.rows)
            for c in range(qo):
                slope_and_sums(tmp[at, cols(c)], pre_ref, at, st_ref, m, qo, c, g_ref, o_ref, d_next, rows_ref)
        fill(pay_ref, rows_ref)

    rows = MICRO * z.rows
    return kernel_call(
        body,
        [arr(rows, z.c_in, dtype=BF)] + [arr(q, LANES)] * 2 + [arr(rows, z.c_mid), arr(z.n, 6 * qo, LANES, dtype=BF)],
        [got, mates, d, pre_e, st_e, gain_e, pre, st, gain, offset],
        [w],
        [
            pltpu.VMEM((6 * qo, LANES), F32),
            pltpu.VMEM((6 * q, LANES), F32),
            pltpu.VMEM((rows, z.c_mid), F32),
        ],
        flops=2 * rows * z.c_in * z.c_mid,
        passes=passes,
    )


def k_back_spatial(got, mates, d, pre_s, st_s, gain_s, pre, st, gain, offset, w, z, passes=()):
    q = z.q1

    def body(k):
        got_ref, mates_ref, d_ref, ps_ref, ss_ref, gs_ref, pre_ref, st_ref, g_ref, o_ref = k.i
        delta_ref, t_off, t_gain, d_next, pay_ref = k.o
        rows_ref, sum_ref, patch_ref, tmp = k.x
        merge_sums(got_ref, mates_ref, sum_ref, q, z.rows, (t_off, t_gain))
        for m in range(MICRO):
            for c in range(q):
                phase = {}
                for i, p in enumerate(PHASES):
                    at = pl.ds(m * z.rows + i * z.half, z.half)
                    phase[p] = back_rows(
                        ps_ref[at, cols(c)], d_ref[at, cols(c)], ss_ref, sum_ref, m, q, c, gs_ref[:, cols(c)]
                    )
                    delta_ref[at, cols(c)] = phase[p].astype(BF)
                write_patches(phase, patch_ref, m, z.half, c, z.c_mid, -1)
        k.send(0)
        k.wait_w()
        tmp[...] = dot(patch_ref[...], k.w[0][...])
        for m in range(MICRO):
            at = pl.ds(m * z.rows, z.rows)
            for c in range(q):
                slope_and_sums(tmp[at, cols(c)], pre_ref, at, st_ref, m, q, c, g_ref, o_ref, d_next, rows_ref)
        fill(pay_ref, rows_ref)

    rows = MICRO * z.rows
    return kernel_call(
        body,
        [arr(rows, z.c_mid, dtype=BF)] + [arr(q, LANES)] * 2 + [arr(rows, z.c_mid), arr(z.n, 6 * q, LANES, dtype=BF)],
        [got, mates, d, pre_s, st_s, gain_s, pre, st, gain, offset],
        [w],
        [
            pltpu.VMEM((6 * q, LANES), F32),
            pltpu.VMEM((6 * q, LANES), F32),
            pltpu.VMEM((rows, 9 * z.c_mid), BF),
            pltpu.VMEM((rows, z.c_mid), F32),
        ],
        flops=2 * rows * 9 * z.c_mid * z.c_mid,
        passes=passes,
    )


def k_back_reduce(got, mates, d, pre_r, st_r, gain_r, z, passes=()):
    q = z.q1

    def body(k):
        got_ref, mates_ref, d_ref, pr_ref, sr_ref, gr_ref = k.i
        delta_ref, t_off, t_gain = k.o
        (sum_ref,) = k.x
        back_start((got_ref, d_ref, pr_ref, sr_ref, gr_ref), mates_ref, sum_ref, delta_ref, q, z.rows, (t_off, t_gain))

    rows = MICRO * z.rows
    return kernel_call(
        body,
        [arr(rows, z.c_mid, dtype=BF)] + [arr(q, LANES)] * 2,
        [got, mates, d, pre_r, st_r, gain_r],
        scratch=[pltpu.VMEM((6 * q, LANES), F32)],
        passes=passes,
    )


def k_input(delta, d_one, w, z, passes=()):
    def body(k):
        (delta_ref, one_ref), (out_ref,), (tmp, line) = k.i, k.o, k.x
        k.wait_w()
        tmp[...] = dot_nt(delta_ref[...], k.w[0][...])
        for m in range(MICRO):
            for y in range(z.height):
                for c in range(z.q3):
                    for px in range(2):
                        at = pl.ds(m * z.rows + (2 * (y % 2) + px) * z.half + (y // 2) * 8, 8)
                        line[c, pl.ds((y * MICRO + m) * z.cols + px, 8, stride=2), :] = (
                            one_ref[at, cols(c)] + tmp[at, cols(c)]
                        )
                    out_ref[y, m, :, cols(c)] = line[c, pl.ds((y * MICRO + m) * z.cols, z.cols), :].astype(BF)

    rows = MICRO * z.rows
    return kernel_call(
        body,
        [arr(z.height, MICRO, z.cols, z.c_in, dtype=BF)],
        [delta, d_one],
        [w],
        [pltpu.VMEM((rows, z.c_in), F32), pltpu.VMEM((z.q3, rows, LANES), F32)],
        flops=2 * rows * z.c_in * z.c_mid,
        passes=passes,
    )


def k_even(delta, w, z):
    def body(k):
        k.wait_w()
        k.o[0][...] = dot_nt(k.i[0][...], k.w[0][...])

    rows = delta.shape[0]
    return kernel_call(body, [arr(rows, z.c_in)], [delta], [w], flops=2 * rows * z.c_in * z.c_out)[0]


def k_first_grads(outs, evens, pieces, z):
    some = z.c_out // z.g
    a, b = z.c_wide // z.ns, z.c_in // z.ns

    def body(k):
        lhs_w, lhs_s, rhs = k.st
        held_w, held_s = k.x
        held_w[...] = dot_tn(lhs_w[...], rhs[:, :some]).astype(BF)
        for s in range(z.ns):
            k.copy(held_w.at[pl.ds(s * a, a)], k.raw[0].at[s % z.slo, s // z.slo, pl.ds(0, a)])
        held_s[...] = dot_tn(lhs_s[...], rhs[:, some:]).astype(BF)
        for s in range(z.ns):
            k.copy(held_s.at[pl.ds(s * b, b)], k.raw[0].at[s % z.slo, s // z.slo, pl.ds(a, b)])

    return kernel_call(
        body,
        [],
        [],
        scratch=[pltpu.VMEM((z.c_wide, some), BF), pltpu.VMEM((z.c_in, some), BF)],
        stacks=[outs, evens, pieces],
        raw=[arr(z.slo, z.ns // z.slo, a + b, some, dtype=BF)],
        n_raw=2 * z.ns,
        flops=2 * z.g * outs[0].shape[0] * (z.c_in + z.c_wide) * some,
    )[0]


def k_stride_grads(maps, pieces, z):
    few = z.c_wide // z.g
    c = 9 * z.c_wide // z.ns
    rows = z.g * pieces[0].shape[0]

    def body(k):
        map_ref, rhs = k.st
        held, lhs = k.x
        for m in range(z.g * MICRO):
            for col in range(z.q4):
                phase = {}
                for i, p in enumerate(PHASES):
                    phase[p] = map_ref[pl.ds(m * z.rows + i * z.half, z.half), cols(col)].astype(F32)
                write_patches(phase, lhs, m, z.half, col, z.c_wide, 1, ((0, 0),))
        for t in range(9):
            at = pl.ds(t * z.c_wide, z.c_wide)
            held[at] = dot_tn(lhs[:, at], rhs[...]).astype(BF)
        for s in range(z.ns):
            k.copy(held.at[pl.ds(s * c, c)], k.raw[0].at[s % z.slo, s // z.slo])

    return kernel_call(
        body,
        [],
        [],
        scratch=[pltpu.VMEM((9 * z.c_wide, few), BF), pltpu.VMEM((rows, 9 * z.c_wide), BF)],
        stacks=[maps, pieces],
        raw=[arr(z.slo, z.ns // z.slo, c, few, dtype=BF)],
        n_raw=z.ns,
        flops=2 * rows * 9 * z.c_wide * few,
    )[0]


def k_products(pairs, place, z):
    hi = z.ns // z.slo
    widths = [(o.shape[1], g.shape[1]) for o, g in pairs]
    rows = [r // z.n * c // 256 for r, c in widths]
    total = sum(rows)

    def body(k):
        (held,) = k.x
        at = 0
        for j, (r, c) in enumerate(widths):
            product = dot_tn(k.i[2 * j][...], k.i[2 * j + 1][...])
            blocks = product.reshape(hi, z.slo, z.nb // 2, 2, r // z.n, c).astype(BF)
            for part in range(c // 256):
                held[:, :, :, :, pl.ds(at, r // z.n), :] = blocks[..., part * 256 : (part + 1) * 256]
                at += r // z.n
        core = k.s[0][0] & 1
        k.copy(held.at[:, :, :, core], k.raw[0])
        k.copy(held.at[:, :, :, 1 - core], k.raw[1])

    return kernel_call(
        body,
        [],
        [a for pair in pairs for a in pair],
        scratch=[pltpu.VMEM((hi, z.slo, z.nb // 2, 2, total, 256), BF)],
        raw=[arr(hi, z.slo, z.nb // 2, total, 256, dtype=BF)] * 2,
        n_raw=2,
        scalars=[place],
        flops=sum(2 * pairs[j][0].shape[0] * r * c for j, (r, c) in enumerate(widths)),
    )


def k_sum_plane(groups, where, z, passes=()):
    hi, high = z.ns // z.slo, z.nb // 2
    rows = [g[0].shape[3] for g in groups]

    def body(k):
        (held,) = k.x
        at = 0
        for j, r in enumerate(rows):
            both = k.i[2 * j][...].astype(F32) + k.i[2 * j + 1][...].astype(F32)
            held[:, :, :, pl.ds(at, r), :] = both.astype(BF)
            at += r
        for i in range(high):
            for j in range(z.slo):
                k.copy(held.at[:, k.s[0][0] ^ j, k.s[0][1] ^ i], k.raw[z.slo * i + j])

    total = sum(rows)
    return kernel_call(
        body,
        [],
        [a for g in groups for a in g],
        scratch=[pltpu.VMEM((hi, z.slo, high, total, 256), BF)],
        raw=[arr(hi, total, 256, dtype=BF)] * (z.slo * high),
        n_raw=z.slo * high,
        scalars=[where],
        passes=passes,
    )


def k_sum_line(groups, where, z, passes=()):
    hi = z.ns // z.slo
    rows = [g[0].shape[1] for g in groups]
    n = len(groups[0])

    def body(k):
        (held,) = k.x
        at = 0
        for j, r in enumerate(rows):
            value = k.i[j * n][...].astype(F32)
            for other in range(1, n):
                value = value + k.i[j * n + other][...].astype(F32)
            held[:, pl.ds(at, r), :] = value.astype(BF)
            at += r
        for j in range(hi):
            k.copy(held.at[k.s[0][2] ^ j], k.raw[j])

    total = sum(rows)
    return kernel_call(
        body,
        [],
        [a for g in groups for a in g],
        scratch=[pltpu.VMEM((hi, total, 256), BF)],
        raw=[arr(total, 256, dtype=BF)] * hi,
        n_raw=hi,
        scalars=[where],
        passes=passes,
    )


def k_sum_last(parts, passes=()):
    def body(k):
        value = k.i[0][...].astype(F32)
        for other in k.i[1:]:
            value = value + other[...].astype(F32)
        k.o[0][...] = value.astype(BF)

    return kernel_call(body, [arr(*parts[0].shape, dtype=BF)], parts, passes=passes)


def k_late_shares(pieces, place, shapes, z):
    n = z.nb
    total = pieces[0].shape[0]

    def body(k):
        (held,) = k.x
        for j in range(n):
            held[k.s[0][0] ^ j] = k.i[j][...]
        for j in range(n):
            value = held[j].astype(F32)
            at = 0
            for g, (r, c) in enumerate(shapes):
                r = r // z.n
                for part in range(c // 256):
                    k.o[g][pl.ds(j * r, r), pl.ds(part * 256, 256)] = value[at : at + r]
                    at += r

    return kernel_call(
        body,
        [arr(r // z.ns, c) for r, c in shapes],
        list(pieces),
        scratch=[pltpu.VMEM((n, total, 256), BF)],
        scalars=[place],
    )


def k_early_shares(first, second, place, z):
    n = z.g
    some, few = z.c_out // n, z.c_wide // n
    a, b, c = z.c_wide // z.ns, z.c_in // z.ns, 9 * z.c_wide // z.ns

    def body(k):
        one, two = k.x
        for j in range(n):
            one[(k.s[0][0] & (n - 1)) ^ j] = k.i[j][...]
            two[(k.s[0][0] & (n - 1)) ^ j] = k.i[n + j][...]
        for j in range(n):
            value = one[j].astype(F32)
            k.o[0][:, pl.ds(j * some, some)] = value[:a]
            k.o[1][:, pl.ds(j * some, some)] = value[a:]
            k.o[2][:, pl.ds(j * few, few)] = two[j].astype(F32)

    return kernel_call(
        body,
        [arr(a, z.c_out), arr(b, z.c_out), arr(c, z.c_wide)],
        [*first, *second],
        scratch=[pltpu.VMEM((n, a + b, some), BF), pltpu.VMEM((n, c, few), BF)],
        scalars=[place],
    )


def on_device(
    features,
    view_ids,
    w_reduce,
    w_spatial,
    w_expand,
    w_narrow,
    w_stride,
    w_widen,
    w_shortcut,
    gain_reduce,
    offset_reduce,
    gain_spatial,
    offset_spatial,
    gain_expand,
    offset_expand,
    gain_narrow,
    offset_narrow,
    gain_stride,
    offset_stride,
    gain_widen,
    offset_widen,
    gain_shortcut,
    offset_shortcut,
    cotangent,
):
    z = Sizes()
    z.ns, z.nb = lax.axis_size(SPACE), lax.axis_size(BATCH)
    z.slo = lax.axis_size("slo")
    z.g = min(z.nb, 4)
    z.n = z.ns * z.nb
    z.maps, z.cols = features.shape[1], features.shape[3]
    z.height = z.ns
    z.rows = z.height * z.cols
    z.half = z.rows // 4
    z.c_in, z.c_mid = w_reduce.shape
    z.c_wide, z.c_out = w_widen.shape
    z.q1, z.q3, z.q4, z.q6 = (c // LANES for c in (z.c_mid, z.c_in, z.c_wide, z.c_out))
    assert features.shape[2] == 1 and cotangent.shape[1] == 1 and z.maps == z.ns and z.cols == 16
    yh, xh = z.height // 2, z.cols // 2
    n, ns, nb = z.n, z.ns, z.nb
    s, b = lax.axis_index(SPACE), lax.axis_index(BATCH)
    place = b.astype(jnp.int32).reshape(1)

    def share(pay):
        return lax.all_to_all(pay, ALL, 0, 0, tiled=True)

    def exchange(block):
        return lax.all_to_all(block, SPACE, 0, 0, tiled=True)

    def swap(block, axis, distance):
        return lax.ppermute(block, axis, [(i, i ^ distance) for i in range(lax.axis_size(axis))])

    def trade(pieces):
        pairs = [(i, i ^ j) for j in range(z.g) for i in range(nb)]
        return [p if j == 0 else lax.ppermute(p, BATCH, pairs[j * nb : (j + 1) * nb]) for j, p in enumerate(pieces)]

    def everywhere(block, places):
        pieces = []
        for high in range(places // 2):
            other = swap(block, "bhi", high) if high else block
            pieces += [other, swap(other, "core", 1)]
        return pieces

    def over_groups(product):
        distance = z.g // 2
        while distance < nb // 2:
            product = (product.astype(F32) + swap(product, "bhi", distance).astype(F32)).astype(BF)
            distance *= 2
        return product

    def lines(vector):
        return vector.reshape(1, -1)

    vectors = {
        "reduce": (lines(gain_reduce), lines(offset_reduce)),
        "spatial": (lines(gain_spatial), lines(offset_spatial)),
        "expand": (lines(gain_expand), lines(offset_expand)),
        "narrow": (lines(gain_narrow), lines(offset_narrow)),
        "stride": (lines(gain_stride), lines(offset_stride)),
        "widen": (lines(gain_widen), lines(offset_widen)),
        "shortcut": (lines(gain_shortcut), lines(offset_shortcut)),
    }

    my_ids = lax.dynamic_slice_in_dim(view_ids, s, 1, 1).astype(F32)
    arrived = exchange(features.reshape(MICRO, z.maps, z.cols, z.c_in).transpose(1, 0, 2, 3))
    pre_reduce, pay = k_reduce(arrived, my_ids.reshape(MICRO), w_reduce, z)
    got = share(pay)
    ids = got[:, 6 * z.q1 : 6 * z.q1 + MICRO]
    same = (ids == my_ids[None]).astype(F32)
    mates = {q: jnp.repeat(same, q, axis=1) for q in (z.q3, z.q4)}
    id_rows = jnp.concatenate([ids, ids, jnp.zeros((n, 2, LANES), F32)], axis=1)

    maps_in = arrived.reshape(yh, 2, MICRO, xh, 2, z.c_in).transpose(2, 1, 4, 0, 3, 5)
    maps_in = maps_in.reshape(MICRO * z.rows, z.c_in)

    patch_reduce, pre_spatial, pay, st_reduce, mates[z.q1] = k_spatial(
        got, my_ids.reshape(MICRO), pre_reduce, *vectors["reduce"], w_spatial, z
    )
    got = share(pay)
    out_spatial, pre_expand, pay, st_spatial = k_expand(got, mates[z.q1], pre_spatial, *vectors["spatial"], w_expand, z)
    got = share(pay)
    residual_one, joined, even, pre_narrow, pay, st_expand = k_narrow(
        got, mates[z.q3], pre_expand, *vectors["expand"], maps_in, w_narrow, z
    )
    evens = everywhere(even, z.g)
    got = share(pay)
    pre_shortcut, short_st = k_shortcut(even, w_shortcut, z)
    out_narrow, pre_stride, pay, st_narrow = k_stride(
        got, mates[z.q4], pre_narrow, *vectors["narrow"], w_stride, z
    )
    got = share(pay)
    outs_narrow = everywhere(out_narrow, z.g)
    out_stride, pre_widen, pay, st_stride, *evens = k_widen(
        got, mates[z.q4], pre_stride, *vectors["stride"], short_st, w_widen, z, evens
    )
    outs_stride = everywhere(out_stride, z.g)
    whole = share(k_views(share(pay), id_rows, z))
    mapped, d_two, pay = k_mapped(
        whole,
        pre_widen,
        pre_shortcut,
        cotangent.reshape(-1, z.c_out),
        (*vectors["widen"], *vectors["shortcut"]),
        z,
    )

    sums = share(k_view_sums(share(pay), id_rows, z))
    delta_shortcut, go_widen, gg_widen, gg_shortcut, d_stride, pay, *more = k_back_widen(
        whole, sums, d_two, pre_widen, pre_shortcut, vectors["widen"][0], vectors["shortcut"][0],
        pre_stride, st_stride, *vectors["stride"], place, w_widen, z, outs_narrow,
    )
    got = share(pay)
    pieces, outs_narrow = more[: z.g], more[z.g :]
    d_even = k_even(delta_shortcut, w_shortcut, z)
    first_pieces = trade(pieces)
    go_stride, gg_stride, d_narrow, pay, *more = k_back_stride(
        got, mates[z.q4], d_stride, pre_stride, st_stride, vectors["stride"][0],
        pre_narrow, st_narrow, *vectors["narrow"], place, w_stride, z, (*first_pieces, *outs_stride, d_even),
    )
    pieces, first_pieces, outs_stride, d_even = more[: z.g], more[z.g : 2 * z.g], more[2 * z.g : 3 * z.g], more[3 * z.g]
    got = share(pay)
    first = k_first_grads(outs_stride, evens, first_pieces, z)
    first = over_groups(first)
    pieces = trade(pieces)
    delta_narrow, go_narrow, gg_narrow, d_one, pay, first, *pieces = k_back_narrow(
        got, mates[z.q4], d_narrow, pre_narrow, st_narrow, vectors["narrow"][0],
        d_even, residual_one, pre_expand, st_expand, w_narrow, z, (first, *pieces),
    )
    got = share(pay)
    first = lax.psum_scatter(first, "slo", scatter_dimension=0, tiled=True)
    second = over_groups(k_stride_grads(outs_narrow, pieces, z))

    delta_expand, go_expand, gg_expand, d_spatial, pay, second = k_back_expand(
        got, mates[z.q3], d_one, pre_expand, st_expand, vectors["expand"][0],
        pre_spatial, st_spatial, *vectors["spatial"], w_expand, z, (second,),
    )
    got = share(pay)
    second = lax.psum_scatter(second, "slo", scatter_dimension=0, tiled=True)
    blocks = all(w.shape[0] % (8 * n) == 0 for w in (w_reduce, w_spatial, w_expand, w_narrow))
    pairs_some = [(joined, delta_narrow), (out_spatial, delta_expand)]
    kept_some, sent_some = k_products(pairs_some, place, z) if blocks else (None, delta_expand)
    flipped = w_spatial.reshape(9, z.c_mid, z.c_mid).transpose(0, 2, 1).reshape(9 * z.c_mid, z.c_mid)
    delta_spatial, go_spatial, gg_spatial, d_reduce, pay, sent_some = k_back_spatial(
        got, mates[z.q1], d_spatial, pre_spatial, st_spatial, vectors["spatial"][0],
        pre_reduce, st_reduce, *vectors["reduce"], flipped, z, (sent_some,),
    )
    got = share(pay)
    pairs_more = [(patch_reduce, delta_spatial)]
    kept_more, sent_more = k_products(pairs_more, place, z) if blocks else (None, delta_spatial)
    came_some = swap(sent_some, "core", 1) if blocks else sent_some
    delta_reduce, go_reduce, gg_reduce, sent_more, came_some, first = k_back_reduce(
        got, mates[z.q1], d_reduce, pre_reduce, st_reduce, vectors["reduce"][0], z, (sent_more, came_some, first)
    )
    where = jnp.stack([lax.axis_index("slo"), lax.axis_index("bhi"), lax.axis_index("shi")]).astype(jnp.int32)

    def over_plane(groups, passes=()):
        high = nb // 2
        parts = k_sum_plane(groups, where, z, passes)
        came = []
        for i in range(high):
            for j in range(z.slo):
                pairs = [(u * z.slo + v, (u ^ i) * z.slo + (v ^ j)) for u in range(high) for v in range(z.slo)]
                part = parts[i * z.slo + j]
                came.append(lax.ppermute(part, ("bhi", "slo"), pairs) if i or j else part)
        return came, parts[high * z.slo :]

    pairs_last = [(maps_in, delta_reduce)]
    if blocks:
        kept_last, sent_last = k_products(pairs_last, place, z)
        late, (sent_last,) = over_plane([(kept_some, came_some), (kept_more, swap(sent_more, "core", 1))], (sent_last,))
        came_last = swap(sent_last, "core", 1)
        left, second, came_last = k_input(delta_reduce, d_one, w_reduce, z, (second, came_last))
    else:
        (left,) = k_input(delta_reduce, d_one, w_reduce, z)
    grad_features = exchange(left).transpose(1, 0, 2, 3).reshape(features.shape)
    first, second = lax.psum_scatter(
        (first.reshape(first.shape[1:]), second.reshape(second.shape[1:])), "shi", scatter_dimension=0, tiled=True
    )
    if blocks:
        last, late = over_plane([(kept_last, came_last)], late)
        parts = k_sum_line([late, last], where, z)
        parts = [p if j == 0 else swap(p, "shi", j) for j, p in enumerate(parts)]
        late, first, second = k_sum_last(parts, (first, second))
        late = everywhere(late, nb)
        shapes = [w.shape for w in (w_narrow, w_expand, w_spatial, w_reduce)]
        grad_w_narrow, grad_w_expand, grad_w_spatial, grad_w_reduce = k_late_shares(late, place, shapes, z)
    else:
        late = [dot_tn(o, g).astype(BF) for o, g in pairs_some + pairs_more + pairs_last]
        late = [lax.psum_scatter(w, SPACE, scatter_dimension=0, tiled=True) for w in late]
        late = [w.astype(F32) for w in lax.psum(late, BATCH)]
        grad_w_narrow, grad_w_expand, grad_w_spatial, grad_w_reduce = late
    first = everywhere(first.reshape(first.shape[1:]), z.g)
    second = everywhere(second.reshape(second.shape[1:]), z.g)
    grad_w_widen, grad_w_shortcut, grad_w_stride = k_early_shares(first, second, place, z)

    flat = lambda block: block.reshape(-1)
    return (
        mapped.reshape(cotangent.shape),
        grad_features,
        grad_w_reduce,
        grad_w_spatial,
        grad_w_expand,
        grad_w_narrow,
        grad_w_stride,
        grad_w_widen,
        grad_w_shortcut,
        flat(gg_reduce),
        flat(go_reduce),
        flat(gg_spatial),
        flat(go_spatial),
        flat(gg_expand),
        flat(go_expand),
        flat(gg_narrow),
        flat(go_narrow),
        flat(gg_stride),
        flat(go_stride),
        flat(gg_widen),
        flat(go_widen),
        flat(gg_shortcut),
        flat(go_widen),
    )


def solution(mesh):
    nb, ns = mesh.shape["batch"], mesh.shape["space"]
    fine = Mesh(mesh.devices.reshape(nb // 2, 2, ns // 2, 2), ALL)
    maps = P(None, ALL, None, None, None)
    return jax.shard_map(
        on_device,
        mesh=fine,
        in_specs=(P(None, BATCH, SPACE, None, None), P(None, BATCH)) + (P(),) * 21 + (maps,),
        out_specs=(maps, P(None, BATCH, SPACE, None, None)) + (P(SPACE, None),) * 7 + (P(),) * 14,
        check_vma=False,
    )
```

profile of v0, /device:TPU:0, one launch (start us, length us, event | category | flops | bytes accessed | tf_op | source)
XLA Modules:
  0.0 395.8 jit_solution(1404981242494147907)
XLA Ops:
  9.3 7.3 %all-to-all-start = ((bf16[8,3,16,1024]{3,2,1,0:T(8,128)(2,1)}), bf16[8,3,16,1024]{3,2,1,0:T(8,128)(2,1)S(1)}, u32[]{:S(2)}, u32[]{:S(2)}) async-start(bf16[8,3,16,1024]{3,2,1,0:T(8,128)(2,1)} %bitcast.58), calls=%async_computation | async-start | bytes 1572864 | tf_op jit(solution)/shard_map/all_to_all | solution.py:1169
  17.3 19.5 %all-to-all-done.refs_1_ = bf16[8,3,16,1024]{3,2,1,0:T(8,128)(2,1)S(1)} async-done(((bf16[8,3,16,1024]{3,2,1,0:T(8,128)(2,1)}), bf16[8,3,16,1024]{3,2,1,0:T(8,128)(2,1)S(1)}, u32[]{:S(2)}, u32[]{:S(2)}) %all-to-all-start) | async-done | bytes 786464 | tf_op jit(solution)/shard_map/all_to_all | solution.py:1169
  37.6 3.8 shard_map.407
  41.4 14.4 %all_to_all.80.refs_1_ = f32[32,16,128]{2,1,0:T(8,128)} all-to-all(f32[32,16,128]{2,1,0:T(8,128)} %get-tuple-element.152), channel_id=1, replica_groups=mesh['bhi'=2,'core'=2,'shi'=4,'slo'=2] {'bhi','core','shi','slo'}, dimensions={0} | all-to-all | bytes 524288 | tf_op jit(solution)/shard_map/all_to_all | solution.py:1166
  55.7 3.8 shard_map.408
  59.6 14.1 %all_to_all.81.refs_0_ = f32[32,12,128]{2,1,0:T(8,128)} all-to-all(f32[32,12,128]{2,1,0:T(8,128)} %get-tuple-element.154), channel_id=1, replica_groups=mesh['bhi'=2,'core'=2,'shi'=4,'slo'=2] {'bhi','core','shi','slo'}, dimensions={0} | all-to-all | bytes 393216 | tf_op jit(solution)/shard_map/all_to_all | solution.py:1166
  73.6 3.2 shard_map.409
  81.8 15.5 %all-to-all-done.3.refs_0_ = bf16[32,72,128]{2,1,0:T(8,128)(2,1)S(1)} async-done(((bf16[32,72,128]{2,1,0:T(8,128)(2,1)}), bf16[32,72,128]{2,1,0:T(8,128)(2,1)S(1)}, u32[]{:S(2)}, u32[]{:S(2)}) %all-to-all-start.3) | async-done | bytes 589856 | tf_op jit(solution)/shard_map/all_to_all | solution.py:1166
  98.1 4.9 %shard_map.410 = (f32[384,1024]{1,0:T(8,128)}, bf16[384,1024]{1,0:T(8,128)(2,1)}, bf16[96,1024]{1,0:T(8,128)(2,1)}, f32[384,512]{1,0:T(8,128)}, bf16[32,36,128]{2,1,0:T(8,128)(2,1)}, /*index=5*/f32[48,128]{1,0:T(8,128)}) custom-call(bf16[32,72,128]{2,1,0:T(8,128)(2,1)} %copy-done.4, f32[32,24,128]{2,1,0:T(8,128)} %broadcast_bitcast_fusion.refs_1_, ...), custom_call_target="tpu_custom_call" | custom-call | flops 402653184 | bytes 8060928 | tf_op jit(solution)/shard_map/pallas_call | solution.py:123
  106.5 11.3 %all-to-all-done.4.refs_0_ = bf16[32,36,128]{2,1,0:T(8,128)(2,1)S(1)} async-done(((bf16[32,36,128]{2,1,0:T(8,128)(2,1)}), bf16[32,36,128]{2,1,0:T(8,128)(2,1)S(1)}, u32[]{:S(2)}, u32[]{:S(2)}) %all-to-all-start.4) | async-done | bytes 294944 | tf_op jit(solution)/shard_map/all_to_all | solution.py:1166
  118.5 4.6 %shard_map.411 = (bf16[384,512]{1,0:T(8,128)(2,1)}, f32[96,512]{1,0:T(8,128)}, bf16[32,36,128]{2,1,0:T(8,128)(2,1)}, f32[24,128]{1,0:T(8,128)}) custom-call(bf16[32,36,128]{2,1,0:T(8,128)(2,1)} %copy-done.16, f32[32,12,128]{2,1,0:T(8,128)} %copy.91.refs_1_.refs_2_, f32[384,512]{1,0:T(8,128)} %get-tuple-element.160.refs_2_.refs_7_.refs_3_, ...), custom_call_target="tpu_custom_call" | custom-call | flops 452984832 | bytes 6897664 | tf_op jit(solution)/shard_map/pallas_call | solution.py:123
  127.5 8.7 %collective-permute-done.1.refs_9_ = bf16[96,1024]{1,0:T(8,128)(2,1)S(1)} collective-permute-done((bf16[96,1024]{1,0:T(8,128)(2,1)S(1)}, bf16[96,1024]{1,0:T(8,128)(2,1)S(1)}, u32[]{:S(2)}, u32[]{:S(2)}) %collective-permute-start.1) | collective-permute-done | bytes 196640 | tf_op jit(solution)/shard_map/ppermute | solution.py:1172
  136.2 4.1 %shard_map.412 = (f32[96,2048]{1,0:T(8,128)}, f32[16,8,128]{2,1,0:T(8,128)}) custom-call(bf16[96,1024]{1,0:T(8,128)(2,1)} %get-tuple-element.163.refs_0_.refs_7_, bf16[1024,2048]{1,0:T(8,128)(2,1)} %refs_1_.3), custom_call_target="tpu_custom_call" | custom-call | flops 402653184 | bytes 5242880 | tf_op jit(solution)/shard_map/pallas_call | solution.py:123
  141.2 3.5 shard_map.413
  144.8 4.9 %all-to-all-start.6 = ((f32[32,8,128]{2,1,0:T(8,128)}), f32[32,8,128]{2,1,0:T(8,128)S(1)}, u32[]{:S(2)}, u32[]{:S(2)}) async-start(f32[32,8,128]{2,1,0:T(8,128)} %get-tuple-element.165), calls=%async_computation.6 | async-start | bytes 262144 | tf_op jit(solution)/shard_map/all_to_all | solution.py:1166
  152.4 5.1 %all-to-all-done.6.refs_0_ = f32[32,8,128]{2,1,0:T(8,128)S(1)} async-done(((f32[32,8,128]{2,1,0:T(8,128)}), f32[32,8,128]{2,1,0:T(8,128)S(1)}, u32[]{:S(2)}, u32[]{:S(2)}) %all-to-all-start.6) | async-done | bytes 131104 | tf_op jit(solution)/shard_map/all_to_all | solution.py:1166
  159.9 11.0 %all_to_all.82.refs_0_.refs_1_ = f32[32,8,128]{2,1,0:T(8,128)} all-to-all(f32[32,8,128]{2,1,0:T(8,128)} %shard_map.414), channel_id=1, replica_groups=mesh['bhi'=2,'core'=2,'shi'=4,'slo'=2] {'bhi','core','shi','slo'}, dimensions={0} | all-to-all | bytes 262144 | tf_op jit(solution)/shard_map/all_to_all | solution.py:1166
  170.9 3.5 shard_map.415
  177.6 7.2 %all-to-all-done.8.refs_0_ = f32[32,8,128]{2,1,0:T(8,128)S(1)} async-done(((f32[32,8,128]{2,1,0:T(8,128)}), f32[32,8,128]{2,1,0:T(8,128)S(1)}, u32[]{:S(2)}, u32[]{:S(2)}) %all-to-all-start.8) | async-done | bytes 131104 | tf_op jit(solution)/shard_map/all_to_all | solution.py:1166
  187.2 2.8 all-to-all-start.9
  190.0 7.5 %all-to-all-done.9.refs_2_ = f32[32,8,128]{2,1,0:T(8,128)S(1)} async-done(((f32[32,8,128]{2,1,0:T(8,128)}), f32[32,8,128]{2,1,0:T(8,128)S(1)}, u32[]{:S(2)}, u32[]{:S(2)}) %all-to-all-start.9) | async-done | bytes 131104 | tf_op jit(solution)/shard_map/all_to_all | solution.py:1166
  198.2 4.4 %shard_map.417 = (bf16[96,2048]{1,0:T(8,128)(2,1)}, f32[16,128]{1,0:T(8,128)}, f32[16,128]{1,0:T(8,128)}, f32[16,128]{1,0:T(8,128)}, f32[96,512]{1,0:T(8,128)}, ...) custom-call(s32[1]{0:T(128)} %bitcast.23.refs_0_, ...), custom_call_target="tpu_custom_call", output_to_operand_aliasing={{10}: (13, {}), {11}: (14, {}), {12}: (15, {}), {13}: (16, ... | custom-call | flops 201326592 | bytes 5758976 | tf_op jit(solution)/shard_map/pallas_call | solution.py:123
  209.1 3.2 collective-permute-done.10.refs_18_
  212.3 4.5 %shard_map.418.refs_20_ = f32[96,1024]{1,0:T(8,128)} custom-call(bf16[96,2048]{1,0:T(8,128)(2,1)} %get-tuple-element.181.refs_0_, bf16[1024,2048]{1,0:T(8,128)(2,1)} %refs_1_.3), custom_call_target="tpu_custom_call" | custom-call | flops 402653184 | bytes 4980736 | tf_op jit(solution)/shard_map/pallas_call | solution.py:123
  217.0 3.2 collective-permute-done.8.refs_15_
  220.9 6.0 %shard_map.419 = (f32[4,128]{1,0:T(4,128)}, f32[4,128]{1,0:T(4,128)}, f32[384,512]{1,0:T(8,128)}, bf16[32,24,128]{2,1,0:T(8,128)(2,1)}, bf16[96,128]{1,0:T(8,128...) custom-call(s32[1]{0:T(128)} %bitcast.23.refs_0_, ...), custom_call_target="tpu_custom_call", output_to_operand_aliasing={{8}: (12, {}), {9}: (13, {}), {10}: (14, {}), {11}: (15, {}... | custom-call | flops 452984832 | bytes 7309312 | tf_op jit(solution)/shard_map/pallas_call | solution.py:123
  226.9 5.0 %all-to-all-start.11 = ((bf16[32,24,128]{2,1,0:T(8,128)(2,1)}), bf16[32,24,128]{2,1,0:T(8,128)(2,1)S(1)}, u32[]{:S(2)}, u32[]{:S(2)}) async-start(bf16[32,24,128]{2,1,0:T(8,128)(2,1)} %get-tuple-element.182), calls=%async_computation.11 | async-start | bytes 393216 | tf_op jit(solution)/shard_map/all_to_all | solution.py:1166
  233.9 3.8 shard_map.420.refs_11_
  241.1 6.0 %shard_map.421 = (bf16[384,512]{1,0:T(8,128)(2,1)}, f32[4,128]{1,0:T(4,128)}, f32[4,128]{1,0:T(4,128)}, f32[384,1024]{1,0:T(8,128)}, bf16[32,48,128]{2,1,0:T(8,1...) custom-call(bf16[32,24,128]{2,1,0:T(8,128)(2,1)} %copy-done.25, ...), custom_call_target="tpu_custom_call", output_to_operand_aliasing={{5}: (11, {}), {6}: (12, {}), {7}: (13, {}), {8}: (14, {}),... | custom-call | flops 402653184 | bytes 8955904 | tf_op jit(solution)/shard_map/pallas_call | solution.py:123
  247.1 3.2 all-to-all-start.12
  250.4 3.9 shard_map.422.refs_11_
  254.3 9.6 %all-to-all-done.12.refs_0_ = bf16[32,48,128]{2,1,0:T(8,128)(2,1)S(1)} async-done(((bf16[32,48,128]{2,1,0:T(8,128)(2,1)}), bf16[32,48,128]{2,1,0:T(8,128)(2,1)S(1)}, u32[]{:S(2)}, u32[]{:S(2)}) %all-to-all-start.12) | async-done | bytes 393248 | tf_op jit(solution)/shard_map/all_to_all | solution.py:1166
  264.6 4.3 %shard_map.423 = (bf16[384,1024]{1,0:T(8,128)(2,1)}, f32[8,128]{1,0:T(8,128)}, f32[8,128]{1,0:T(8,128)}, f32[384,256]{1,0:T(8,128)}, bf16[32,12,128]{2,1,0:T(8,128)(2,1)}, /*index=5*/bf16[2,4,576,128]{3,2,1,0:T(8,128)(2,1)}) custom-call(bf16[32,48,128]{2,1,0:T(8,128)(2,1)} %copy-done.7, ...), custom_call_target="tpu_custom_call", output_to_operand_aliasing={{5}: (11, {})} | custom-call | flops 201326592 | bytes 6172672 | tf_op jit(solution)/shard_map/pallas_call | solution.py:123
  269.0 2.9 all-to-all-start.13
  273.5 3.8 shard_map.424
  280.1 3.6 shard_map.425
  283.9 3.6 all-to-all-start.14
  287.5 3.4 shard_map.426
  290.9 4.3 %all-to-all-done.14.refs_0_ = bf16[32,12,128]{2,1,0:T(8,128)(2,1)S(1)} async-done(((bf16[32,12,128]{2,1,0:T(8,128)(2,1)}), bf16[32,12,128]{2,1,0:T(8,128)(2,1)S(1)}, u32[]{:S(2)}, u32[]{:S(2)}) %all-to-all-start.14) | async-done | bytes 98336 | tf_op jit(solution)/shard_map/all_to_all | solution.py:1166
  302.4 3.9 shard_map.429
  308.8 3.2 shard_map.430
  312.1 3.7 all-to-all-start.15
  319.4 13.1 %collective-permute-done.18.refs_4_ = bf16[4,168,256]{2,1,0:T(8,128)(2,1)S(1)} collective-permute-done((bf16[4,168,256]{2,1,0:T(8,128)(2,1)S(1)}, bf16[4,168,256]{2,1,0:T(8,128)(2,1)S(1)}, u32[]{:S(2)}, u32[]{:S(2)}) %collective-permute-start.18) | collective-permute-done | bytes 344096 | tf_op jit(solution)/shard_map/ppermute | solution.py:1305
  332.5 9.9 %collective-permute-done.20.refs_6_ = bf16[4,168,256]{2,1,0:T(8,128)(2,1)S(1)} collective-permute-done((bf16[4,168,256]{2,1,0:T(8,128)(2,1)S(1)}, bf16[4,168,256]{2,1,0:T(8,128)(2,1)S(1)}, u32[]{:S(2)}, u32[]{:S(2)}) %collective-permute-start.20) | collective-permute-done | bytes 344096 | tf_op jit(solution)/shard_map/ppermute | solution.py:1305
  353.1 3.0 shard_map.432
  361.9 5.6 %collective-permute-done.25.refs_2_ = bf16[200,256]{1,0:T(8,128)(2,1)S(1)} collective-permute-done((bf16[200,256]{1,0:T(8,128)(2,1)}, bf16[200,256]{1,0:T(8,128)(2,1)S(1)}, u32[]{:S(2)}, u32[]{:S(2)}) %collective-permute-start.25) | collective-permute-done | bytes 102432 | tf_op jit(solution)/shard_map/ppermute | solution.py:1172
  373.4 3.2 collective-permute-done.31.refs_3_
  385.3 3.3 shard_map.435
  (231 shorter events, 92.8 us)
Async XLA Ops:
  9.3 27.4 %all-to-all-start = ((bf16[8,3,16,1024]{3,2,1,0:T(8,128)(2,1)}), bf16[8,3,16,1024]{3,2,1,0:T(8,128)(2,1)S(1)}, u32[]{:S(2)}, u32[]{:S(2)}) async-start(bf16[8,3,16,1024]{3,2,1,0:T(8,128)(2,1)} %bitcast.58), calls=%async_computation | async-start | bytes 1572864 | tf_op jit(solution)/shard_map/all_to_all | solution.py:1169
  76.9 20.4 %all-to-all-start.3 = ((bf16[32,72,128]{2,1,0:T(8,128)(2,1)}), bf16[32,72,128]{2,1,0:T(8,128)(2,1)S(1)}, u32[]{:S(2)}, u32[]{:S(2)}) async-start(bf16[32,72,128]{2,1,0:T(8,128)(2,1)} %get-tuple-element.157), calls=%async_computation.3 | async-start | bytes 1179648 | tf_op jit(solution)/shard_map/all_to_all | solution.py:1166
  103.0 14.8 %all-to-all-start.4 = ((bf16[32,36,128]{2,1,0:T(8,128)(2,1)}), bf16[32,36,128]{2,1,0:T(8,128)(2,1)S(1)}, u32[]{:S(2)}, u32[]{:S(2)}) async-start(bf16[32,36,128]{2,1,0:T(8,128)(2,1)} %get-tuple-element.159), calls=%async_computation.4 | async-start | bytes 655360 | tf_op jit(solution)/shard_map/all_to_all | solution.py:1166
  123.2 17.3 %all-to-all-start.5 = ((bf16[32,36,128]{2,1,0:T(8,128)(2,1)}), bf16[32,36,128]{2,1,0:T(8,128)(2,1)S(1)}, u32[]{:S(2)}, u32[]{:S(2)}) async-start(bf16[32,36,128]{2,1,0:T(8,128)(2,1)} %get-tuple-element.161), calls=%async_computation.5 | async-start | bytes 655360 | tf_op jit(solution)/shard_map/all_to_all | solution.py:1166
  125.8 10.4 %collective-permute-start.1 = (bf16[96,1024]{1,0:T(8,128)(2,1)S(1)}, bf16[96,1024]{1,0:T(8,128)(2,1)S(1)}, u32[]{:S(2)}, u32[]{:S(2)}) collective-permute-start(bf16[96,1024]{1,0:T(8,128)(2,1)S(1)} %copy-done.5), channel_id=1, source_target_pairs={{0,16},{16,0},{1,17},{17,1},{2,18},{18,2},{3,19},{19,3},{4,20},{20... | collective-permute-start | bytes 589832 | tf_op jit(solution)/shard_map/ppermute | solution.py:1172
  127.5 12.9 %collective-permute-start = (bf16[96,1024]{1,0:T(8,128)(2,1)S(1)}, bf16[96,1024]{1,0:T(8,128)(2,1)S(1)}, u32[]{:S(2)}, u32[]{:S(2)}) collective-permute-start(bf16[96,1024]{1,0:T(8,128)(2,1)S(1)} %copy-done.5), channel_id=1, source_target_pairs={{0,8},{8,0},{1,9},{9,1},{2,10},{10,2},{3,11},{11,3},{4,12},{12,4},... | collective-permute-start | bytes 589832 | tf_op jit(solution)/shard_map/ppermute | solution.py:1172
  144.8 12.7 %all-to-all-start.6 = ((f32[32,8,128]{2,1,0:T(8,128)}), f32[32,8,128]{2,1,0:T(8,128)S(1)}, u32[]{:S(2)}, u32[]{:S(2)}) async-start(f32[32,8,128]{2,1,0:T(8,128)} %get-tuple-element.165), calls=%async_computation.6 | async-start | bytes 262144 | tf_op jit(solution)/shard_map/all_to_all | solution.py:1166
  149.8 27.4 %collective-permute-start.4 = (bf16[384,512]{1,0:T(8,128)(2,1)S(1)}, bf16[384,512]{1,0:T(8,128)(2,1)S(1)}, u32[]{:S(2)}, u32[]{:S(2)}) collective-permute-start(bf16[384,512]{1,0:T(8,128)(2,1)S(1)} %copy-done.8), channel_id=1, source_target_pairs={{0,16},{16,0},{1,17},{17,1},{2,18},{18,2},{3,19},{19,3},{4,20},{20... | collective-permute-start | bytes 1179656 | tf_op jit(solution)/shard_map/ppermute | solution.py:1172
  174.5 10.3 %all-to-all-start.8 = ((f32[32,8,128]{2,1,0:T(8,128)}), f32[32,8,128]{2,1,0:T(8,128)S(1)}, u32[]{:S(2)}, u32[]{:S(2)}) async-start(f32[32,8,128]{2,1,0:T(8,128)} %get-tuple-element.169), calls=%async_computation.8 | async-start | bytes 262144 | tf_op jit(solution)/shard_map/all_to_all | solution.py:1166
  177.1 12.9 %collective-permute-start.3 = (bf16[384,512]{1,0:T(8,128)(2,1)S(1)}, bf16[384,512]{1,0:T(8,128)(2,1)S(1)}, u32[]{:S(2)}, u32[]{:S(2)}) collective-permute-start(bf16[384,512]{1,0:T(8,128)(2,1)S(1)} %copy-done.8), channel_id=1, source_target_pairs={{0,8},{8,0},{1,9},{9,1},{2,10},{10,2},{3,11},{11,3},{4,12},{12,4},... | collective-permute-start | bytes 1179656 | tf_op jit(solution)/shard_map/ppermute | solution.py:1172
  177.2 12.7 %collective-permute-start.5 = (bf16[384,512]{1,0:T(8,128)(2,1)S(1)}, bf16[384,512]{1,0:T(8,128)(2,1)S(1)}, u32[]{:S(2)}, u32[]{:S(2)}) collective-permute-start(bf16[384,512]{1,0:T(8,128)(2,1)S(1)} %collective-permute-done.4.refs_15_), channel_id=1, source_target_pairs={{0,8},{8,0},{1,9},{9,1},{2,10},{10,2},{3,11},{11,3},{4,12},{12,4},... | collective-permute-start | bytes 1179656 | tf_op jit(solution)/shard_map/ppermute | solution.py:1172
  187.2 10.3 %all-to-all-start.9 = ((f32[32,8,128]{2,1,0:T(8,128)}), f32[32,8,128]{2,1,0:T(8,128)S(1)}, u32[]{:S(2)}, u32[]{:S(2)}) async-start(f32[32,8,128]{2,1,0:T(8,128)} %shard_map.416), calls=%async_computation.9 | async-start | bytes 262144 | tf_op jit(solution)/shard_map/all_to_all | solution.py:1166
  202.6 17.6 %all-to-all-start.10 = ((bf16[32,24,128]{2,1,0:T(8,128)(2,1)}), bf16[32,24,128]{2,1,0:T(8,128)(2,1)S(1)}, u32[]{:S(2)}, u32[]{:S(2)}) async-start(bf16[32,24,128]{2,1,0:T(8,128)(2,1)} %get-tuple-element.173), calls=%async_computation.10 | async-start | bytes 393216 | tf_op jit(solution)/shard_map/all_to_all | solution.py:1166
  205.2 7.1 %collective-permute-start.10 = (bf16[96,512]{1,0:T(8,128)(2,1)S(1)}, bf16[96,512]{1,0:T(8,128)(2,1)S(1)}, u32[]{:S(2)}, u32[]{:S(2)}) collective-permute-start(bf16[96,512]{1,0:T(8,128)(2,1)S(1)} %copy-done.32), channel_id=1, source_target_pairs={{0,16},{16,0},{1,17},{17,1},{2,18},{18,2},{3,19},{19,3},{4,20},{20... | collective-permute-start | bytes 294920 | tf_op jit(solution)/shard_map/ppermute | solution.py:1172
  206.9 10.0 %collective-permute-start.6 = (bf16[96,1024]{1,0:T(8,128)(2,1)}, bf16[96,1024]{1,0:T(8,128)(2,1)S(1)}, u32[]{:S(2)}, u32[]{:S(2)}) collective-permute-start(bf16[96,1024]{1,0:T(8,128)(2,1)} %get-tuple-element.177), channel_id=1, source_target_pairs={{0,8},{8,0},{16,24},{24,16},{1,9},{9,1},{17,25},{25,17},{2,10},{10... | collective-permute-start | bytes 589832 | tf_op jit(solution)/shard_map/ppermute | solution.py:1176
  206.9 10.0 %collective-permute-start.7 = (bf16[96,1024]{1,0:T(8,128)(2,1)}, bf16[96,1024]{1,0:T(8,128)(2,1)S(1)}, u32[]{:S(2)}, u32[]{:S(2)}) collective-permute-start(bf16[96,1024]{1,0:T(8,128)(2,1)} %get-tuple-element.178), channel_id=1, source_target_pairs={{0,16},{8,24},{16,0},{24,8},{1,17},{9,25},{17,1},{25,9},{2,18},{10... | collective-permute-start | bytes 589832 | tf_op jit(solution)/shard_map/ppermute | solution.py:1176
  207.3 12.8 %collective-permute-start.8 = (bf16[96,1024]{1,0:T(8,128)(2,1)}, bf16[96,1024]{1,0:T(8,128)(2,1)S(1)}, u32[]{:S(2)}, u32[]{:S(2)}) collective-permute-start(bf16[96,1024]{1,0:T(8,128)(2,1)} %get-tuple-element.179), channel_id=1, source_target_pairs={{0,24},{8,16},{16,8},{24,0},{1,25},{9,17},{17,9},{25,1},{2,26},{10... | collective-permute-start | bytes 589832 | tf_op jit(solution)/shard_map/ppermute | solution.py:1176
  208.8 8.1 %collective-permute-start.9 = (bf16[96,512]{1,0:T(8,128)(2,1)S(1)}, bf16[96,512]{1,0:T(8,128)(2,1)S(1)}, u32[]{:S(2)}, u32[]{:S(2)}) collective-permute-start(bf16[96,512]{1,0:T(8,128)(2,1)S(1)} %copy-done.32), channel_id=1, source_target_pairs={{0,8},{8,0},{1,9},{9,1},{2,10},{10,2},{3,11},{11,3},{4,12},{12,4},... | collective-permute-start | bytes 294920 | tf_op jit(solution)/shard_map/ppermute | solution.py:1172
  212.3 4.6 %collective-permute-start.11 = (bf16[96,512]{1,0:T(8,128)(2,1)S(1)}, bf16[96,512]{1,0:T(8,128)(2,1)S(1)}, u32[]{:S(2)}, u32[]{:S(2)}) collective-permute-start(bf16[96,512]{1,0:T(8,128)(2,1)S(1)} %collective-permute-done.10.refs_18_), channel_id=1, source_target_pairs={{0,8},{8,0},{1,9},{9,1},{2,10},{10,2},{3,11},{11,3},{4,12},{12,4},... | collective-permute-start | bytes 294920 | tf_op jit(solution)/shard_map/ppermute | solution.py:1172
  226.9 13.5 %all-to-all-start.11 = ((bf16[32,24,128]{2,1,0:T(8,128)(2,1)}), bf16[32,24,128]{2,1,0:T(8,128)(2,1)S(1)}, u32[]{:S(2)}, u32[]{:S(2)}) async-start(bf16[32,24,128]{2,1,0:T(8,128)(2,1)} %get-tuple-element.182), calls=%async_computation.11 | async-start | bytes 393216 | tf_op jit(solution)/shard_map/all_to_all | solution.py:1166
  231.9 63.4 %reduce-scatter.5.cloned.1.call-start = ((), (), s32[]{:S(2)}) async-start(), calls=%async_computation.20 | async-start | bytes 2359296 | tf_op jit(solution)/shard_map/reduce_scatter | solution.py:1271
  231.9 5.8 %collective-permute-start.12 = (bf16[96,128]{1,0:T(8,128)(2,1)}, bf16[96,128]{1,0:T(8,128)(2,1)S(1)}, u32[]{:S(2)}, u32[]{:S(2)}) collective-permute-start(bf16[96,128]{1,0:T(8,128)(2,1)} %get-tuple-element.200), channel_id=1, source_target_pairs={{0,8},{8,0},{16,24},{24,16},{1,9},{9,1},{17,25},{25,17},{2,10},{10... | collective-permute-start | bytes 73736 | tf_op jit(solution)/shard_map/ppermute | solution.py:1176
  232.2 5.5 %collective-permute-start.13 = (bf16[96,128]{1,0:T(8,128)(2,1)}, bf16[96,128]{1,0:T(8,128)(2,1)S(1)}, u32[]{:S(2)}, u32[]{:S(2)}) collective-permute-start(bf16[96,128]{1,0:T(8,128)(2,1)} %get-tuple-element.201), channel_id=1, source_target_pairs={{0,16},{8,24},{16,0},{24,8},{1,17},{9,25},{17,1},{25,9},{2,18},{10... | collective-permute-start | bytes 73736 | tf_op jit(solution)/shard_map/ppermute | solution.py:1176
  247.1 16.7 %all-to-all-start.12 = ((bf16[32,48,128]{2,1,0:T(8,128)(2,1)}), bf16[32,48,128]{2,1,0:T(8,128)(2,1)S(1)}, u32[]{:S(2)}, u32[]{:S(2)}) async-start(bf16[32,48,128]{2,1,0:T(8,128)(2,1)} %get-tuple-element.203), calls=%async_computation.12 | async-start | bytes 786432 | tf_op jit(solution)/shard_map/all_to_all | solution.py:1166
  250.3 56.4 %reduce-scatter.7.cloned.1.call-start = ((), (), s32[]{:S(2)}) async-start(), calls=%async_computation.21 | async-start | bytes 1769472 | tf_op jit(solution)/shard_map/reduce_scatter | solution.py:1279
  269.0 10.5 %all-to-all-start.13 = ((bf16[32,12,128]{2,1,0:T(8,128)(2,1)}), bf16[32,12,128]{2,1,0:T(8,128)(2,1)S(1)}, u32[]{:S(2)}, u32[]{:S(2)}) async-start(bf16[32,12,128]{2,1,0:T(8,128)(2,1)} %get-tuple-element.214), calls=%async_computation.13 | async-start | bytes 262144 | tf_op jit(solution)/shard_map/all_to_all | solution.py:1166
  283.7 11.5 %collective-permute-start.15 = (bf16[4,2,2,96,256]{4,3,2,1,0:T(8,128)(2,1)}, bf16[4,2,2,96,256]{4,3,2,1,0:T(8,128)(2,1)S(1)}, u32[]{:S(2)}, u32[]{:S(2)}) collective-permute-start(bf16[4,2,2,96,256]{4,3,2,1,0:T(8,128)(2,1)} %get-tuple-element.227), channel_id=1, source_target_pairs={{0,8},{8,0},{1,9},{9,1},{2,10},{10,2},{3,11},{11,3},{4,12},{12,4},... | collective-permute-start | bytes 2359304 | tf_op jit(solution)/shard_map/ppermute | solution.py:1172
  283.9 11.3 %all-to-all-start.14 = ((bf16[32,12,128]{2,1,0:T(8,128)(2,1)}), bf16[32,12,128]{2,1,0:T(8,128)(2,1)S(1)}, u32[]{:S(2)}, u32[]{:S(2)}) async-start(bf16[32,12,128]{2,1,0:T(8,128)(2,1)} %get-tuple-element.222), calls=%async_computation.14 | async-start | bytes 262144 | tf_op jit(solution)/shard_map/all_to_all | solution.py:1166
  287.5 80.1 %reduce-scatter.9.cloned.1.call-start = ((), (), s32[]{:S(2)}) async-start(), calls=%async_computation.22 | async-start | bytes 983040 | tf_op jit(solution)/shard_map/reduce_scatter | solution.py:1317
  298.3 69.3 %reduce-scatter.11.cloned.1.call-start = ((), (), s32[]{:S(2)}) async-start(), calls=%async_computation.23 | async-start | bytes 737280 | tf_op jit(solution)/shard_map/reduce_scatter | solution.py:1317
  312.1 67.7 %all-to-all-start.15 = ((bf16[8,3,16,1024]{3,2,1,0:T(8,128)(2,1)}), bf16[8,3,16,1024]{3,2,1,0:T(8,128)(2,1)S(1)}, u32[]{:S(2)}, u32[]{:S(2)}) async-start(bf16[8,3,16,1024]{3,2,1,0:T(8,128)(2,1)} %get-tuple-element.237), calls=%async_computation.17 | async-start | bytes 1572864 | tf_op jit(solution)/shard_map/all_to_all | solution.py:1169
  315.8 16.7 %collective-permute-start.18 = (bf16[4,168,256]{2,1,0:T(8,128)(2,1)S(1)}, bf16[4,168,256]{2,1,0:T(8,128)(2,1)S(1)}, u32[]{:S(2)}, u32[]{:S(2)}) collective-permute-start(bf16[4,168,256]{2,1,0:T(8,128)(2,1)S(1)} %copy-done.59), channel_id=1, source_target_pairs={{0,1},{1,0},{16,17},{17,16},{2,3},{3,2},{18,19},{19,18},{4,5},{5,4... | collective-permute-start | bytes 1032200 | tf_op jit(solution)/shard_map/ppermute | solution.py:1305
  317.7 14.8 %collective-permute-start.19 = (bf16[4,168,256]{2,1,0:T(8,128)(2,1)S(1)}, bf16[4,168,256]{2,1,0:T(8,128)(2,1)S(1)}, u32[]{:S(2)}, u32[]{:S(2)}) collective-permute-start(bf16[4,168,256]{2,1,0:T(8,128)(2,1)S(1)} %copy-done.58), channel_id=1, source_target_pairs={{0,16},{1,17},{16,0},{17,1},{2,18},{3,19},{18,2},{19,3},{4,20},{5,... | collective-permute-start | bytes 1032200 | tf_op jit(solution)/shard_map/ppermute | solution.py:1305
  318.7 23.7 %collective-permute-start.20 = (bf16[4,168,256]{2,1,0:T(8,128)(2,1)S(1)}, bf16[4,168,256]{2,1,0:T(8,128)(2,1)S(1)}, u32[]{:S(2)}, u32[]{:S(2)}) collective-permute-start(bf16[4,168,256]{2,1,0:T(8,128)(2,1)S(1)} %copy-done.57), channel_id=1, source_target_pairs={{0,17},{1,16},{16,1},{17,0},{2,19},{3,18},{18,3},{19,2},{4,21},{5,... | collective-permute-start | bytes 1032200 | tf_op jit(solution)/shard_map/ppermute | solution.py:1305
  345.6 5.1 %collective-permute-start.21 = (bf16[4,32,256]{2,1,0:T(8,128)(2,1)}, bf16[4,32,256]{2,1,0:T(8,128)(2,1)S(1)}, u32[]{:S(2)}, u32[]{:S(2)}) collective-permute-start(bf16[4,32,256]{2,1,0:T(8,128)(2,1)} %get-tuple-element.249), channel_id=1, source_target_pairs={{0,1},{1,0},{16,17},{17,16},{2,3},{3,2},{18,19},{19,18},{4,5},{5,4... | collective-permute-start | bytes 196616 | tf_op jit(solution)/shard_map/ppermute | solution.py:1305
  345.7 5.0 %collective-permute-start.22 = (bf16[4,32,256]{2,1,0:T(8,128)(2,1)}, bf16[4,32,256]{2,1,0:T(8,128)(2,1)S(1)}, u32[]{:S(2)}, u32[]{:S(2)}) collective-permute-start(bf16[4,32,256]{2,1,0:T(8,128)(2,1)} %get-tuple-element.250), channel_id=1, source_target_pairs={{0,16},{1,17},{16,0},{17,1},{2,18},{3,19},{18,2},{19,3},{4,20},{5,... | collective-permute-start | bytes 196616 | tf_op jit(solution)/shard_map/ppermute | solution.py:1305
  347.1 5.4 %collective-permute-start.23 = (bf16[4,32,256]{2,1,0:T(8,128)(2,1)}, bf16[4,32,256]{2,1,0:T(8,128)(2,1)S(1)}, u32[]{:S(2)}, u32[]{:S(2)}) collective-permute-start(bf16[4,32,256]{2,1,0:T(8,128)(2,1)} %get-tuple-element.251), channel_id=1, source_target_pairs={{0,17},{1,16},{16,1},{17,0},{2,19},{3,18},{18,3},{19,2},{4,21},{5,... | collective-permute-start | bytes 196616 | tf_op jit(solution)/shard_map/ppermute | solution.py:1305
  356.2 5.7 %collective-permute-start.24 = (bf16[200,256]{1,0:T(8,128)(2,1)}, bf16[200,256]{1,0:T(8,128)(2,1)S(1)}, u32[]{:S(2)}, u32[]{:S(2)}) collective-permute-start(bf16[200,256]{1,0:T(8,128)(2,1)} %get-tuple-element.253), channel_id=1, source_target_pairs={{0,2},{2,0},{4,6},{6,4},{1,3},{3,1},{5,7},{7,5},{8,10},{10,8},{12,... | collective-permute-start | bytes 307208 | tf_op jit(solution)/shard_map/ppermute | solution.py:1172
  357.9 9.6 %collective-permute-start.25 = (bf16[200,256]{1,0:T(8,128)(2,1)}, bf16[200,256]{1,0:T(8,128)(2,1)S(1)}, u32[]{:S(2)}, u32[]{:S(2)}) collective-permute-start(bf16[200,256]{1,0:T(8,128)(2,1)} %get-tuple-element.254), channel_id=1, source_target_pairs={{0,4},{2,6},{4,0},{6,2},{1,5},{3,7},{5,1},{7,3},{8,12},{10,14},{12... | collective-permute-start | bytes 307208 | tf_op jit(solution)/shard_map/ppermute | solution.py:1172
  360.2 7.3 %collective-permute-start.26 = (bf16[200,256]{1,0:T(8,128)(2,1)}, bf16[200,256]{1,0:T(8,128)(2,1)S(1)}, u32[]{:S(2)}, u32[]{:S(2)}) collective-permute-start(bf16[200,256]{1,0:T(8,128)(2,1)} %get-tuple-element.255), channel_id=1, source_target_pairs={{0,6},{2,4},{4,2},{6,0},{1,7},{3,5},{5,3},{7,1},{8,14},{10,12},{12... | collective-permute-start | bytes 307208 | tf_op jit(solution)/shard_map/ppermute | solution.py:1172
  370.0 6.6 %collective-permute-start.31 = (bf16[192,512]{1,0:T(8,128)(2,1)}, bf16[192,512]{1,0:T(8,128)(2,1)S(1)}, u32[]{:S(2)}, u32[]{:S(2)}) collective-permute-start(bf16[192,512]{1,0:T(8,128)(2,1)} %bitcast.66), channel_id=1, source_target_pairs={{0,16},{16,0},{1,17},{17,1},{2,18},{18,2},{3,19},{19,3},{4,20},{20... | collective-permute-start | bytes 589832 | tf_op jit(solution)/shard_map/ppermute | solution.py:1172
  371.1 7.6 %collective-permute-start.34 = (bf16[576,128]{1,0:T(8,128)(2,1)}, bf16[576,128]{1,0:T(8,128)(2,1)S(1)}, u32[]{:S(2)}, u32[]{:S(2)}) collective-permute-start(bf16[576,128]{1,0:T(8,128)(2,1)} %bitcast.70), channel_id=1, source_target_pairs={{0,16},{16,0},{1,17},{17,1},{2,18},{18,2},{3,19},{19,3},{4,20},{20... | collective-permute-start | bytes 442376 | tf_op jit(solution)/shard_map/ppermute | solution.py:1172
  372.1 4.5 %collective-permute-start.27 = (bf16[200,256]{1,0:T(8,128)(2,1)}, bf16[200,256]{1,0:T(8,128)(2,1)S(1)}, u32[]{:S(2)}, u32[]{:S(2)}) collective-permute-start(bf16[200,256]{1,0:T(8,128)(2,1)} %get-tuple-element.258.refs_1_), channel_id=1, source_target_pairs={{0,8},{8,0},{1,9},{9,1},{2,10},{10,2},{3,11},{11,3},{4,12},{12,4},... | collective-permute-start | bytes 307208 | tf_op jit(solution)/shard_map/ppermute | solution.py:1172
  372.1 7.7 %collective-permute-start.28 = (bf16[200,256]{1,0:T(8,128)(2,1)}, bf16[200,256]{1,0:T(8,128)(2,1)S(1)}, u32[]{:S(2)}, u32[]{:S(2)}) collective-permute-start(bf16[200,256]{1,0:T(8,128)(2,1)} %get-tuple-element.258.refs_1_), channel_id=1, source_target_pairs={{0,16},{16,0},{1,17},{17,1},{2,18},{18,2},{3,19},{19,3},{4,20},{20... | collective-permute-start | bytes 307208 | tf_op jit(solution)/shard_map/ppermute | solution.py:1172
  373.1 10.7 %collective-permute-start.30 = (bf16[192,512]{1,0:T(8,128)(2,1)}, bf16[192,512]{1,0:T(8,128)(2,1)S(1)}, u32[]{:S(2)}, u32[]{:S(2)}) collective-permute-start(bf16[192,512]{1,0:T(8,128)(2,1)} %bitcast.67), channel_id=1, source_target_pairs={{0,8},{8,0},{1,9},{9,1},{2,10},{10,2},{3,11},{11,3},{4,12},{12,4},... | collective-permute-start | bytes 589832 | tf_op jit(solution)/shard_map/ppermute | solution.py:1172
  376.6 7.3 %collective-permute-start.32 = (bf16[192,512]{1,0:T(8,128)(2,1)S(1)}, bf16[192,512]{1,0:T(8,128)(2,1)S(1)}, u32[]{:S(2)}, u32[]{:S(2)}) collective-permute-start(bf16[192,512]{1,0:T(8,128)(2,1)S(1)} %collective-permute-done.31.refs_3_), channel_id=1, source_target_pairs={{0,8},{8,0},{1,9},{9,1},{2,10},{10,2},{3,11},{11,3},{4,12},{12,4},... | collective-permute-start | bytes 589832 | tf_op jit(solution)/shard_map/ppermute | solution.py:1172
  376.6 7.3 %collective-permute-start.33 = (bf16[576,128]{1,0:T(8,128)(2,1)}, bf16[576,128]{1,0:T(8,128)(2,1)S(1)}, u32[]{:S(2)}, u32[]{:S(2)}) collective-permute-start(bf16[576,128]{1,0:T(8,128)(2,1)} %bitcast.71), channel_id=1, source_target_pairs={{0,8},{8,0},{1,9},{9,1},{2,10},{10,2},{3,11},{11,3},{4,12},{12,4},... | collective-permute-start | bytes 442376 | tf_op jit(solution)/shard_map/ppermute | solution.py:1172
  378.7 5.2 %collective-permute-start.35 = (bf16[576,128]{1,0:T(8,128)(2,1)S(1)}, bf16[576,128]{1,0:T(8,128)(2,1)S(1)}, u32[]{:S(2)}, u32[]{:S(2)}) collective-permute-start(bf16[576,128]{1,0:T(8,128)(2,1)S(1)} %collective-permute-done.34.refs_7_), channel_id=1, source_target_pairs={{0,8},{8,0},{1,9},{9,1},{2,10},{10,2},{3,11},{11,3},{4,12},{12,4},... | collective-permute-start | bytes 442376 | tf_op jit(solution)/shard_map/ppermute | solution.py:1172
  (65 other events, 229.2 us)
Sparse Core Ops, SparseCore 0:
  247.3 28.2 reduce-scatter.4
  278.4 23.0 reduce-scatter.6
  303.9 28.1 reduce-scatter.8
  334.2 25.5 reduce-scatter.10
where the time goes:
time: 398 us; the launch traced here: 396 us
  waiting for transfers between devices  141 us (35%)
  Pallas kernels  103 us (26%)
  starting transfers between devices  72.7 us (18%)
  blocking collectives  39.5 us (10%)
  local copies, waits for them, and re-layouts  22.8 us (6%)
  between operations  14.7 us (4%)
    pallas_call x29, Pallas kernels, kernel_call(): pl.pallas_call(run, out_shape=tuple((jax.ShapeDtypeStruct(o.shape, o.dtyp...  103 us
    all_to_all x11, waiting for transfers between devices, share(): return lax.all_to_all(pay, ALL, 0, 0, tiled=True)  65.2 us
    all_to_all x3, blocking collectives, share(): return lax.all_to_all(pay, ALL, 0, 0, tiled=True)  39.5 us
    all_to_all x11, starting transfers between devices, share(): return lax.all_to_all(pay, ALL, 0, 0, tiled=True)  35.4 us
    ppermute x24, waiting for transfers between devices, swap(): lax.ppermute(block, axis, [(i, i ^ distance) for i in range(lax.axis_size...  26.5 us
    ppermute x6, waiting for transfers between devices, over_plane(): came.append(lax.ppermute(part, ('bhi', 'slo'), pairs) if i or j else part)  26.4 us
    all_to_all x2, waiting for transfers between devices, exchange(): return lax.all_to_all(block, SPACE, 0, 0, tiled=True)  19.5 us
    unnamed x123, local copies, waits for them, and re-layouts  18.1 us
  transfers between devices with their start and end apart: 53, of which 25 were waited for; matrix products, arithmetic and copies ran while one was open for 2% of the time, Pallas kernels for 15%

commit v1 on v0

--- a/solution.py
+++ b/solution.py
@@ -73,7 +73,7 @@
         self.flying.append(copy)
 
 
-def kernel_call(body, outs, args, weights=(), scratch=(), flops=0, raw=(), n_raw=0, scalars=(), passes=(), stacks=()):
+def kernel_call(body, outs, args, weights=(), scratch=(), flops=0, raw=(), n_raw=0, scalars=(), passes=(), stacks=(), limit=60):
     n_s, n_in, n_w, n_p = len(scalars), len(args), len(weights), len(passes)
     n_k = sum(map(len, stacks))
     n_out, n_r = len(outs), len(raw)
@@ -130,7 +130,7 @@
         + list(scratch),
         input_output_aliases={first + j: n_out + n_r + j for j in range(n_p)},
         cost_estimate=pl.CostEstimate(flops=flops, bytes_accessed=held, transcendentals=0),
-        compiler_params=pltpu.CompilerParams(vmem_limit_bytes=max(60 * 2**20, total)),
+        compiler_params=pltpu.CompilerParams(vmem_limit_bytes=max(limit * 2**20, total)),
     )(*scalars, *args, *weights, *(a for g in stacks for a in g), *passes)
     return tuple(results)
 
@@ -157,7 +157,7 @@
 
 
 def stats_shape(q):
-    return (6 * q, F32) if q < 4 else (9 * q, BF)
+    return 9 * q, BF
 
 
 def stats_arr(n, q):
@@ -172,7 +172,7 @@
         high = mean.astype(BF).astype(F32)
         rows_ref[:k] = high
         rows_ref[k : 2 * k] = mean - high
-        rows_ref[2 * k :] = square
+        rows_ref[2 * k : 3 * k] = square
     fill(pay_ref, rows_ref)
 
 
@@ -296,18 +296,19 @@
             for c in range(q):
                 stats_rows(map_ref[pl.ds(m * z.rows, z.rows), cols(c)], rows_ref, m * q + c, z.rows, MICRO * q)
         for m in range(MICRO):
-            rows_ref[pl.ds(6 * q + m, 1), :] = jnp.full((1, LANES), k.s[0][m], F32)
-        fill(pay_ref, rows_ref)
-
-    rows, pad = MICRO * z.rows, 16
-    return kernel_call(
-        body,
-        [arr(rows, z.c_mid), arr(z.n, pad, LANES)],
+            rows_ref[pl.ds(9 * q + m, 1), :] = jnp.full((1, LANES), k.s[0][m], F32)
+        fill_stats(pay_ref, rows_ref, q)
+
+    rows, pad = MICRO * z.rows, -(-(9 * q + MICRO) // 8) * 8
+    return kernel_call(
+        body,
+        [arr(rows, z.c_mid), arr(z.n, pad, LANES, dtype=BF)],
         [x],
         [w],
         [pltpu.VMEM((q, rows, LANES), F32), pltpu.VMEM((pad, LANES), F32)],
         flops=2 * rows * z.c_in * z.c_mid,
         scalars=[ids],
+        limit=24,
     )
 
 
@@ -318,9 +319,9 @@
         got_ref, pre_ref, g_ref, o_ref = k.i
         patch_ref, next_ref, pay_ref, st_ref, mates_ref = k.o
         (rows_ref,) = k.x
-        same = []
-        for m in range(MICRO):
-            view = got_ref[:, pl.ds(6 * q + m, 1), :]
+        same, views = [], got_ref[...].astype(F32)
+        for m in range(MICRO):
+            view = views[:, 9 * q + m : 9 * q + m + 1]
             same += [(view == k.s[0][m]).astype(F32)] * q
         mates_ref[...] = jnp.concatenate(same, axis=1)
         merge_stats(got_ref, mates_ref, st_ref, q, z.rows)
@@ -939,6 +940,8 @@
 def k_stride_grads(maps, pieces, z):
     few = z.c_wide // z.g
     c = 9 * z.c_wide // z.ns
+    wide = z.c_out // z.c_wide
+    d = c // wide
     rows = z.g * pieces[0].shape[0]
 
     def body(k):
@@ -954,7 +957,11 @@
             at = pl.ds(t * z.c_wide, z.c_wide)
             held[at] = dot_tn(lhs[:, at], rhs[...]).astype(BF)
         for s in range(z.ns):
-            k.copy(held.at[pl.ds(s * c, c)], k.raw[0].at[s % z.slo, s // z.slo])
+            for part in range(wide):
+                k.copy(
+                    held.at[pl.ds(s * c + part * d, d)],
+                    k.raw[0].at[s % z.slo, s // z.slo, :, pl.ds(part * few, few)],
+                )
 
     return kernel_call(
         body,
@@ -962,13 +969,13 @@
         [],
         scratch=[pltpu.VMEM((9 * z.c_wide, few), BF), pltpu.VMEM((rows, 9 * z.c_wide), BF)],
         stacks=[maps, pieces],
-        raw=[arr(z.slo, z.ns // z.slo, c, few, dtype=BF)],
-        n_raw=z.ns,
+        raw=[arr(z.slo, z.ns // z.slo, d, wide * few, dtype=BF)],
+        n_raw=wide * z.ns,
         flops=2 * rows * 9 * z.c_wide * few,
     )[0]
 
 
-def k_products(pairs, place, z):
+def k_products(pairs, place, z, passes=()):
     hi = z.ns // z.slo
     widths = [(o.shape[1], g.shape[1]) for o, g in pairs]
     rows = [r // z.n * c // 256 for r, c in widths]
@@ -995,16 +1002,23 @@
         raw=[arr(hi, z.slo, z.nb // 2, total, 256, dtype=BF)] * 2,
         n_raw=2,
         scalars=[place],
+        passes=passes,
         flops=sum(2 * pairs[j][0].shape[0] * r * c for j, (r, c) in enumerate(widths)),
     )
 
 
-def k_sum_plane(groups, where, z, passes=()):
+def k_sum_plane(groups, where, z, early=()):
     hi, high = z.ns // z.slo, z.nb // 2
     rows = [g[0].shape[3] for g in groups]
 
+    tall = [e.shape[1] for e in early]
+
     def body(k):
         (held,) = k.x
+        top = 0
+        for e, r in zip(k.i[2 * len(groups) :], tall):
+            k.copy(e, k.raw[-1].at[:, pl.ds(top, r)])
+            top += r
         at = 0
         for j, r in enumerate(rows):
             both = k.i[2 * j][...].astype(F32) + k.i[2 * j + 1][...].astype(F32)
@@ -1018,12 +1032,12 @@
     return kernel_call(
         body,
         [],
-        [a for g in groups for a in g],
+        [a for g in groups for a in g] + list(early),
         scratch=[pltpu.VMEM((hi, z.slo, high, total, 256), BF)],
-        raw=[arr(hi, total, 256, dtype=BF)] * (z.slo * high),
-        n_raw=z.slo * high,
+        raw=[arr(hi, total, 256, dtype=BF)] * (z.slo * high)
+        + ([arr(hi, sum(tall), early[0].shape[2], dtype=BF)] if early else []),
+        n_raw=z.slo * high + len(early),
         scalars=[where],
-        passes=passes,
     )
 
 
@@ -1067,7 +1081,7 @@
     return kernel_call(body, [arr(*parts[0].shape, dtype=BF)], parts, passes=passes)
 
 
-def k_late_shares(pieces, place, shapes, z):
+def k_late_shares(pieces, place, shapes, z, passes=()):
     n = z.nb
     total = pieces[0].shape[0]
 
@@ -1090,30 +1104,32 @@
         list(pieces),
         scratch=[pltpu.VMEM((n, total, 256), BF)],
         scalars=[place],
-    )
-
-
-def k_early_shares(first, second, place, z):
+        passes=passes,
+    )
+
+
+def k_early_shares(pieces, place, z):
     n = z.g
     some, few = z.c_out // n, z.c_wide // n
     a, b, c = z.c_wide // z.ns, z.c_in // z.ns, 9 * z.c_wide // z.ns
-
-    def body(k):
-        one, two = k.x
+    d = c * few // some
+
+    def body(k):
+        (held,) = k.x
         for j in range(n):
-            one[(k.s[0][0] & (n - 1)) ^ j] = k.i[j][...]
-            two[(k.s[0][0] & (n - 1)) ^ j] = k.i[n + j][...]
+            held[(k.s[0][0] & (n - 1)) ^ j] = k.i[j][...]
         for j in range(n):
-            value = one[j].astype(F32)
+            value = held[j].astype(F32)
             k.o[0][:, pl.ds(j * some, some)] = value[:a]
-            k.o[1][:, pl.ds(j * some, some)] = value[a:]
-            k.o[2][:, pl.ds(j * few, few)] = two[j].astype(F32)
+            k.o[1][:, pl.ds(j * some, some)] = value[a : a + b]
+            for part in range(some // few):
+                k.o[2][pl.ds(part * d, d), pl.ds(j * few, few)] = value[a + b :, part * few : (part + 1) * few]
 
     return kernel_call(
         body,
         [arr(a, z.c_out), arr(b, z.c_out), arr(c, z.c_wide)],
-        [*first, *second],
-        scratch=[pltpu.VMEM((n, a + b, some), BF), pltpu.VMEM((n, c, few), BF)],
+        list(pieces),
+        scratch=[pltpu.VMEM((n, a + b + d, some), BF)],
         scalars=[place],
     )
 
@@ -1206,7 +1222,7 @@
     arrived = exchange(features.reshape(MICRO, z.maps, z.cols, z.c_in).transpose(1, 0, 2, 3))
     pre_reduce, pay = k_reduce(arrived, my_ids.reshape(MICRO), w_reduce, z)
     got = share(pay)
-    ids = got[:, 6 * z.q1 : 6 * z.q1 + MICRO]
+    ids = got[:, 9 * z.q1 : 9 * z.q1 + MICRO].astype(F32)
     same = (ids == my_ids[None]).astype(F32)
     mates = {q: jnp.repeat(same, q, axis=1) for q in (z.q3, z.q4)}
     id_rows = jnp.concatenate([ids, ids, jnp.zeros((n, 2, LANES), F32)], axis=1)
@@ -1231,8 +1247,8 @@
     )
     got = share(pay)
     outs_narrow = everywhere(out_narrow, z.g)
-    out_stride, pre_widen, pay, st_stride, *evens = k_widen(
-        got, mates[z.q4], pre_stride, *vectors["stride"], short_st, w_widen, z, evens
+    out_stride, pre_widen, pay, st_stride = k_widen(
+        got, mates[z.q4], pre_stride, *vectors["stride"], short_st, w_widen, z
     )
     outs_stride = everywhere(out_stride, z.g)
     whole = share(k_views(share(pay), id_rows, z))
@@ -1248,17 +1264,17 @@
     sums = share(k_view_sums(share(pay), id_rows, z))
     delta_shortcut, go_widen, gg_widen, gg_shortcut, d_stride, pay, *more = k_back_widen(
         whole, sums, d_two, pre_widen, pre_shortcut, vectors["widen"][0], vectors["shortcut"][0],
-        pre_stride, st_stride, *vectors["stride"], place, w_widen, z, outs_narrow,
+        pre_stride, st_stride, *vectors["stride"], place, w_widen, z, (*outs_narrow, *evens, *outs_stride),
     )
     got = share(pay)
-    pieces, outs_narrow = more[: z.g], more[z.g :]
+    pieces, outs_narrow, evens, outs_stride = (more[j * z.g : (j + 1) * z.g] for j in range(4))
     d_even = k_even(delta_shortcut, w_shortcut, z)
     first_pieces = trade(pieces)
     go_stride, gg_stride, d_narrow, pay, *more = k_back_stride(
         got, mates[z.q4], d_stride, pre_stride, st_stride, vectors["stride"][0],
-        pre_narrow, st_narrow, *vectors["narrow"], place, w_stride, z, (*first_pieces, *outs_stride, d_even),
-    )
-    pieces, first_pieces, outs_stride, d_even = more[: z.g], more[z.g : 2 * z.g], more[2 * z.g : 3 * z.g], more[3 * z.g]
+        pre_narrow, st_narrow, *vectors["narrow"], place, w_stride, z, (*first_pieces, d_even),
+    )
+    pieces, first_pieces, d_even = more[: z.g], more[z.g : 2 * z.g], more[2 * z.g]
     got = share(pay)
     first = k_first_grads(outs_stride, evens, first_pieces, z)
     first = over_groups(first)
@@ -1281,22 +1297,19 @@
     pairs_some = [(joined, delta_narrow), (out_spatial, delta_expand)]
     kept_some, sent_some = k_products(pairs_some, place, z) if blocks else (None, delta_expand)
     flipped = w_spatial.reshape(9, z.c_mid, z.c_mid).transpose(0, 2, 1).reshape(9 * z.c_mid, z.c_mid)
-    delta_spatial, go_spatial, gg_spatial, d_reduce, pay, sent_some = k_back_spatial(
+    delta_spatial, go_spatial, gg_spatial, d_reduce, pay, sent_some, first = k_back_spatial(
         got, mates[z.q1], d_spatial, pre_spatial, st_spatial, vectors["spatial"][0],
-        pre_reduce, st_reduce, *vectors["reduce"], flipped, z, (sent_some,),
+        pre_reduce, st_reduce, *vectors["reduce"], flipped, z, (sent_some, first),
     )
     got = share(pay)
     pairs_more = [(patch_reduce, delta_spatial)]
     kept_more, sent_more = k_products(pairs_more, place, z) if blocks else (None, delta_spatial)
     came_some = swap(sent_some, "core", 1) if blocks else sent_some
-    delta_reduce, go_reduce, gg_reduce, sent_more, came_some, first = k_back_reduce(
-        got, mates[z.q1], d_reduce, pre_reduce, st_reduce, vectors["reduce"][0], z, (sent_more, came_some, first)
-    )
     where = jnp.stack([lax.axis_index("slo"), lax.axis_index("bhi"), lax.axis_index("shi")]).astype(jnp.int32)
 
-    def over_plane(groups, passes=()):
+    def over_plane(groups, early):
         high = nb // 2
-        parts = k_sum_plane(groups, where, z, passes)
+        parts = k_sum_plane(groups, where, z, early)
         came = []
         for i in range(high):
             for j in range(z.slo):
@@ -1305,34 +1318,36 @@
                 came.append(lax.ppermute(part, ("bhi", "slo"), pairs) if i or j else part)
         return came, parts[high * z.slo :]
 
-    pairs_last = [(maps_in, delta_reduce)]
+    delta_reduce, go_reduce, gg_reduce, sent_more, came_some = k_back_reduce(
+        got, mates[z.q1], d_reduce, pre_reduce, st_reduce, vectors["reduce"][0], z, (sent_more, came_some)
+    )
+    pairs_last, passed = [(maps_in, delta_reduce)], ()
     if blocks:
         kept_last, sent_last = k_products(pairs_last, place, z)
-        late, (sent_last,) = over_plane([(kept_some, came_some), (kept_more, swap(sent_more, "core", 1))], (sent_last,))
-        came_last = swap(sent_last, "core", 1)
-        left, second, came_last = k_input(delta_reduce, d_one, w_reduce, z, (second, came_last))
+        groups = [(kept_some, came_some), (kept_more, swap(sent_more, "core", 1)), (kept_last, swap(sent_last, "core", 1))]
+        passed, (early,) = over_plane(groups, (first[0], second[0]))
     else:
-        (left,) = k_input(delta_reduce, d_one, w_reduce, z)
-    grad_features = exchange(left).transpose(1, 0, 2, 3).reshape(features.shape)
-    first, second = lax.psum_scatter(
-        (first.reshape(first.shape[1:]), second.reshape(second.shape[1:])), "shi", scatter_dimension=0, tiled=True
-    )
+        early = jnp.concatenate([first[0], second[0]], axis=1)
+    left, *passed = k_input(delta_reduce, d_one, w_reduce, z, passed)
+    left = exchange(left)
+    early = lax.psum_scatter(early, "shi", scatter_dimension=0, tiled=True)
     if blocks:
-        last, late = over_plane([(kept_last, came_last)], late)
-        parts = k_sum_line([late, last], where, z)
+        *parts, early = k_sum_line([passed], where, z, (early,))
+        early = k_early_shares(everywhere(early[0], z.g), place, z)
         parts = [p if j == 0 else swap(p, "shi", j) for j, p in enumerate(parts)]
-        late, first, second = k_sum_last(parts, (first, second))
+        late, *early = k_sum_last(parts, early)
         late = everywhere(late, nb)
         shapes = [w.shape for w in (w_narrow, w_expand, w_spatial, w_reduce)]
-        grad_w_narrow, grad_w_expand, grad_w_spatial, grad_w_reduce = k_late_shares(late, place, shapes, z)
+        late = k_late_shares(late, place, shapes, z)
+        grad_w_narrow, grad_w_expand, grad_w_spatial, grad_w_reduce = late
     else:
         late = [dot_tn(o, g).astype(BF) for o, g in pairs_some + pairs_more + pairs_last]
         late = [lax.psum_scatter(w, SPACE, scatter_dimension=0, tiled=True) for w in late]
         late = [w.astype(F32) for w in lax.psum(late, BATCH)]
         grad_w_narrow, grad_w_expand, grad_w_spatial, grad_w_reduce = late
-    first = everywhere(first.reshape(first.shape[1:]), z.g)
-    second = everywhere(second.reshape(second.shape[1:]), z.g)
-    grad_w_widen, grad_w_shortcut, grad_w_stride = k_early_shares(first, second, place, z)
+        early = k_early_shares(everywhere(early[0], z.g), place, z)
+    grad_w_widen, grad_w_shortcut, grad_w_stride = early
+    grad_features = left.transpose(1, 0, 2, 3).reshape(features.shape)
 
     flat = lambda block: block.reshape(-1)
     return (

time: 398 us -> 375 us (0.942)
  waiting for transfers between devices: 141 us -> 132 us
  starting transfers between devices: 72.7 us -> 67.4 us
  blocking collectives: 39.5 us -> 34.9 us
    ppermute x6 -> x3, waiting for transfers between devices: 26.4 us -> 18.2 us  [over_plane(): came.append(lax.ppermute(part, ('bhi', 'slo'), pairs) if i or j else part)]
    all_to_all x3, blocking collectives: 39.5 us -> 34.9 us  [share(): return lax.all_to_all(pay, ALL, 0, 0, tiled=True)]
    ppermute x24 -> x21, waiting for transfers between devices: 26.5 us -> 22.3 us  [swap(): lax.ppermute(block, axis, [(i, i ^ distance) for i in range(lax.axis_size...]
    pallas_call x29 -> x28, Pallas kernels: 103 us -> 99.6 us  [kernel_call(): pl.pallas_call(run, out_shape=tuple((jax.ShapeDtypeStruct(o.shape, o.dtyp...]
    ppermute x24 -> x21, starting transfers between devices: 15.3 us -> 13.3 us  [swap(): lax.ppermute(block, axis, [(i, i ^ distance) for i in range(lax.axis_size...]
    unnamed x123 -> x105, local copies, waits for them, and re-layouts: 18.1 us -> 17.5 us
  transfers between devices with their start and end apart: 53 -> 46, of which waited for: 25 -> 22; matrix products, arithmetic and copies ran while one was open for 2% -> 2% of each run, Pallas kernels for 15% -> 15%
where the time goes in v1:
time: 375 us; the launch traced here: 373 us
  waiting for transfers between devices  132 us (35%)
  Pallas kernels  99.6 us (27%)
  starting transfers between devices  67.4 us (18%)
  blocking collectives  34.9 us (9%)
  local copies, waits for them, and re-layouts  22.1 us (6%)
  between operations  14.5 us (4%)
    pallas_call x28, Pallas kernels, kernel_call(): pl.pallas_call(run, out_shape=tuple((jax.ShapeDtypeStruct(o.shape, o.dtyp...  99.6 us
    all_to_all x11, waiting for transfers between devices, share(): return lax.all_to_all(pay, ALL, 0, 0, tiled=True)  62.3 us
    all_to_all x11, starting transfers between devices, share(): return lax.all_to_all(pay, ALL, 0, 0, tiled=True)  35.5 us
    all_to_all x3, blocking collectives, share(): return lax.all_to_all(pay, ALL, 0, 0, tiled=True)  34.9 us
    ppermute x21, waiting for transfers between devices, swap(): lax.ppermute(block, axis, [(i, i ^ distance) for i in range(lax.axis_size...  22.3 us
    all_to_all x2, waiting for transfers between devices, exchange(): return lax.all_to_all(block, SPACE, 0, 0, tiled=True)  20 us
    ppermute x3, waiting for transfers between devices, over_plane(): came.append(lax.ppermute(part, ('bhi', 'slo'), pairs) if i or j else part)  18.2 us
    unnamed x105, local copies, waits for them, and re-layouts  17.5 us
  transfers between devices with their start and end apart: 46, of which 22 were waited for; matrix products, arithmetic and copies ran while one was open for 2% of the time, Pallas kernels for 15%

profile of v1, /device:TPU:0, one launch (start us, length us, event | category | flops | bytes accessed | tf_op | source)
XLA Modules:
  0.0 373.4 jit_solution(7352283041693535973)
XLA Ops:
  9.4 7.3 %all-to-all-start = ((bf16[8,3,16,1024]{3,2,1,0:T(8,128)(2,1)}), bf16[8,3,16,1024]{3,2,1,0:T(8,128)(2,1)S(1)}, u32[]{:S(2)}, u32[]{:S(2)}) async-start(bf16[8,3,16,1024]{3,2,1,0:T(8,128)(2,1)} %bitcast.57), calls=%async_computation | async-start | bytes 1572864 | tf_op jit(solution)/shard_map/all_to_all | solution.py:1185
  16.8 20.0 %all-to-all-done.refs_1_ = bf16[8,3,16,1024]{3,2,1,0:T(8,128)(2,1)S(1)} async-done(((bf16[8,3,16,1024]{3,2,1,0:T(8,128)(2,1)}), bf16[8,3,16,1024]{3,2,1,0:T(8,128)(2,1)S(1)}, u32[]{:S(2)}, u32[]{:S(2)}) %all-to-all-start) | async-done | bytes 786464 | tf_op jit(solution)/shard_map/all_to_all | solution.py:1185
  39.6 12.1 %all_to_all.80.refs_1_ = bf16[32,24,128]{2,1,0:T(8,128)(2,1)} all-to-all(bf16[32,24,128]{2,1,0:T(8,128)(2,1)S(1)} %get-tuple-element.148), channel_id=1, replica_groups=mesh['bhi'=2,'core'=2,'shi'=4,'slo'=2] {'bhi','core','shi','slo'}, dimensions={0} | all-to-all | bytes 393216 | tf_op jit(solution)/shard_map/all_to_all | solution.py:1182
  51.7 3.8 %shard_map.408 = (bf16[384,2304]{1,0:T(8,128)(2,1)}, f32[384,256]{1,0:T(8,128)}, bf16[32,18,128]{2,1,0:T(8,128)(2,1)}, f32[12,128]{1,0:T(8,128)}, f32[32,6,128]{2,1,0:T(8,128)}) custom-call(f32[3]{0:T(128)} %copy-done.2, bf16[32,24,128]{2,1,0:T(8,128)(2,1)} %all_to_all.80.refs_1_, f32[384,256]{1,0:T(8,128)} %copy-done, f32[1,256]{1,0:T(1,128)} %bitcast.85, ...), custom_call_target="tpu_custom_call" | custom-call | flops 452984832 | bytes 4186112 | tf_op jit(solution)/shard_map/pallas_call | solution.py:123
  55.5 11.8 %all_to_all.81.refs_0_ = bf16[32,18,128]{2,1,0:T(8,128)(2,1)} all-to-all(bf16[32,18,128]{2,1,0:T(8,128)(2,1)} %get-tuple-element.150), channel_id=1, replica_groups=mesh['bhi'=2,'core'=2,'shi'=4,'slo'=2] {'bhi','core','shi','slo'}, dimensions={0} | all-to-all | bytes 294912 | tf_op jit(solution)/shard_map/all_to_all | solution.py:1182
  67.4 3.3 shard_map.409
  70.6 3.0 all-to-all-start.3
  76.7 14.6 %all-to-all-done.3.refs_0_ = bf16[32,72,128]{2,1,0:T(8,128)(2,1)S(1)} async-done(((bf16[32,72,128]{2,1,0:T(8,128)(2,1)}), bf16[32,72,128]{2,1,0:T(8,128)(2,1)S(1)}, u32[]{:S(2)}, u32[]{:S(2)}) %all-to-all-start.3) | async-done | bytes 589856 | tf_op jit(solution)/shard_map/all_to_all | solution.py:1182
  92.2 4.9 %shard_map.410 = (f32[384,1024]{1,0:T(8,128)}, bf16[384,1024]{1,0:T(8,128)(2,1)}, bf16[96,1024]{1,0:T(8,128)(2,1)}, f32[384,512]{1,0:T(8,128)}, bf16[32,36,128]{2,1,0:T(8,128)(2,1)}, /*index=5*/f32[48,128]{1,0:T(8,128)}) custom-call(bf16[32,72,128]{2,1,0:T(8,128)(2,1)} %copy-done.6, f32[32,24,128]{2,1,0:T(8,128)} %broadcast_bitcast_fusion.refs_1_, ...), custom_call_target="tpu_custom_call" | custom-call | flops 402653184 | bytes 8060928 | tf_op jit(solution)/shard_map/pallas_call | solution.py:123
  100.7 11.3 %all-to-all-done.4.refs_0_ = bf16[32,36,128]{2,1,0:T(8,128)(2,1)S(1)} async-done(((bf16[32,36,128]{2,1,0:T(8,128)(2,1)}), bf16[32,36,128]{2,1,0:T(8,128)(2,1)S(1)}, u32[]{:S(2)}, u32[]{:S(2)}) %all-to-all-start.4) | async-done | bytes 294944 | tf_op jit(solution)/shard_map/all_to_all | solution.py:1182
  112.7 4.6 %shard_map.411 = (bf16[384,512]{1,0:T(8,128)(2,1)}, f32[96,512]{1,0:T(8,128)}, bf16[32,36,128]{2,1,0:T(8,128)(2,1)}, f32[24,128]{1,0:T(8,128)}) custom-call(bf16[32,36,128]{2,1,0:T(8,128)(2,1)} %copy-done.17, f32[32,12,128]{2,1,0:T(8,128)} %copy.90.refs_1_.refs_2_, f32[384,512]{1,0:T(8,128)} %get-tuple-element.156.refs_2_.refs_7_.refs_3_, ...), custom_call_target="tpu_custom_call" | custom-call | flops 452984832 | bytes 6897664 | tf_op jit(solution)/shard_map/pallas_call | solution.py:123
  120.0 4.1 %shard_map.412 = (f32[96,2048]{1,0:T(8,128)}, f32[16,8,128]{2,1,0:T(8,128)}) custom-call(bf16[96,1024]{1,0:T(8,128)(2,1)} %get-tuple-element.159.refs_0_.refs_17_, bf16[1024,2048]{1,0:T(8,128)(2,1)} %refs_1_.3), custom_call_target="tpu_custom_call" | custom-call | flops 402653184 | bytes 5242880 | tf_op jit(solution)/shard_map/pallas_call | solution.py:123
  124.1 8.0 %all-to-all-done.5.refs_0_ = bf16[32,36,128]{2,1,0:T(8,128)(2,1)S(1)} async-done(((bf16[32,36,128]{2,1,0:T(8,128)(2,1)}), bf16[32,36,128]{2,1,0:T(8,128)(2,1)S(1)}, u32[]{:S(2)}, u32[]{:S(2)}) %all-to-all-start.5) | async-done | bytes 294944 | tf_op jit(solution)/shard_map/all_to_all | solution.py:1182
  132.8 3.5 shard_map.413
  142.2 4.4 %all-to-all-done.6.refs_0_ = f32[32,8,128]{2,1,0:T(8,128)S(1)} async-done(((f32[32,8,128]{2,1,0:T(8,128)}), f32[32,8,128]{2,1,0:T(8,128)S(1)}, u32[]{:S(2)}, u32[]{:S(2)}) %all-to-all-start.6) | async-done | bytes 131104 | tf_op jit(solution)/shard_map/all_to_all | solution.py:1182
  149.1 11.0 %all_to_all.82.refs_0_.refs_1_ = f32[32,8,128]{2,1,0:T(8,128)} all-to-all(f32[32,8,128]{2,1,0:T(8,128)} %shard_map.414), channel_id=1, replica_groups=mesh['bhi'=2,'core'=2,'shi'=4,'slo'=2] {'bhi','core','shi','slo'}, dimensions={0} | all-to-all | bytes 262144 | tf_op jit(solution)/shard_map/all_to_all | solution.py:1182
  160.1 3.5 shard_map.415
  168.5 5.4 %all-to-all-done.8.refs_0_ = f32[32,8,128]{2,1,0:T(8,128)S(1)} async-done(((f32[32,8,128]{2,1,0:T(8,128)}), f32[32,8,128]{2,1,0:T(8,128)S(1)}, u32[]{:S(2)}, u32[]{:S(2)}) %all-to-all-start.8) | async-done | bytes 131104 | tf_op jit(solution)/shard_map/all_to_all | solution.py:1182
  180.9 4.4 %collective-permute-done.7.refs_23_ = bf16[96,512]{1,0:T(8,128)(2,1)S(1)} collective-permute-done((bf16[96,512]{1,0:T(8,128)(2,1)S(1)}, bf16[96,512]{1,0:T(8,128)(2,1)S(1)}, u32[]{:S(2)}, u32[]{:S(2)}) %collective-permute-start.7) | collective-permute-done | bytes 98336 | tf_op jit(solution)/shard_map/ppermute | solution.py:1188
  187.5 4.4 %shard_map.417 = (bf16[96,2048]{1,0:T(8,128)(2,1)}, f32[16,128]{1,0:T(8,128)}, f32[16,128]{1,0:T(8,128)}, f32[16,128]{1,0:T(8,128)}, f32[96,512]{1,0:T(8,128)}, ...) custom-call(s32[1]{0:T(128)} %bitcast.23.refs_0_, ...), custom_call_target="tpu_custom_call", output_to_operand_aliasing={{10}: (13, {}), {11}: (14, {}), {12}: (15, {}), {13}: (16, ... | custom-call | flops 201326592 | bytes 5758976 | tf_op jit(solution)/shard_map/pallas_call | solution.py:123
  191.9 5.0 %all-to-all-start.10 = ((bf16[32,24,128]{2,1,0:T(8,128)(2,1)}), bf16[32,24,128]{2,1,0:T(8,128)(2,1)S(1)}, u32[]{:S(2)}, u32[]{:S(2)}) async-start(bf16[32,24,128]{2,1,0:T(8,128)(2,1)} %get-tuple-element.170), calls=%async_computation.10 | async-start | bytes 393216 | tf_op jit(solution)/shard_map/all_to_all | solution.py:1182
  198.9 4.5 %shard_map.418.refs_16_ = f32[96,1024]{1,0:T(8,128)} custom-call(bf16[96,2048]{1,0:T(8,128)(2,1)} %get-tuple-element.177.refs_0_, bf16[1024,2048]{1,0:T(8,128)(2,1)} %refs_1_.3), custom_call_target="tpu_custom_call" | custom-call | flops 402653184 | bytes 4980736 | tf_op jit(solution)/shard_map/pallas_call | solution.py:123
  203.4 3.4 collective-permute-done.10.refs_14_
  206.8 3.5 collective-permute-done.11.refs_15_
  211.1 6.0 %shard_map.419 = (f32[4,128]{1,0:T(4,128)}, f32[4,128]{1,0:T(4,128)}, f32[384,512]{1,0:T(8,128)}, bf16[32,24,128]{2,1,0:T(8,128)(2,1)}, bf16[96,128]{1,0:T(8,128...) custom-call(s32[1]{0:T(128)} %bitcast.23.refs_0_, ...), custom_call_target="tpu_custom_call", output_to_operand_aliasing={{8}: (12, {}), {9}: (13, {}), {10}: (14, {}), {11}: (15, {}... | custom-call | flops 452984832 | bytes 7309312 | tf_op jit(solution)/shard_map/pallas_call | solution.py:123
  217.1 4.7 %all-to-all-start.11 = ((bf16[32,24,128]{2,1,0:T(8,128)(2,1)}), bf16[32,24,128]{2,1,0:T(8,128)(2,1)S(1)}, u32[]{:S(2)}, u32[]{:S(2)}) async-start(bf16[32,24,128]{2,1,0:T(8,128)(2,1)} %get-tuple-element.178), calls=%async_computation.11 | async-start | bytes 393216 | tf_op jit(solution)/shard_map/all_to_all | solution.py:1182
  223.9 3.8 %shard_map.420.refs_11_ = bf16[2,4,192,512]{3,2,1,0:T(8,128)(2,1)} custom-call(bf16[96,512]{1,0:T(8,128)(2,1)} %get-tuple-element.183.refs_0_, bf16[96,512]{1,0:T(8,128)(2,1)} %get-tuple-element.184.refs_1_, bf16[96,512]{1,0:T(8,128)(2,1)} %get-tuple-element.185.refs_2_, bf16[96,512]{1,0:T(8,128)(2,1)} %get-tuple-element.186.refs_3_, ...), custom_call_target="tpu_custom_call" | custom-call | flops 603979776 | bytes 1966080 | tf_op jit(solution)/shard_map/pallas_call | solution.py:123
  231.0 6.0 %shard_map.421 = (bf16[384,512]{1,0:T(8,128)(2,1)}, f32[4,128]{1,0:T(4,128)}, f32[4,128]{1,0:T(4,128)}, f32[384,1024]{1,0:T(8,128)}, bf16[32,48,128]{2,1,0:T(8,1...) custom-call(bf16[32,24,128]{2,1,0:T(8,128)(2,1)} %copy-done.24, ...), custom_call_target="tpu_custom_call", output_to_operand_aliasing={{5}: (11, {}), {6}: (12, {}), {7}: (13, {}), {8}: (14, {}),... | custom-call | flops 402653184 | bytes 8955904 | tf_op jit(solution)/shard_map/pallas_call | solution.py:123
  237.1 3.2 all-to-all-start.12
  240.3 4.1 %shard_map.422.refs_11_ = bf16[2,4,144,512]{3,2,1,0:T(8,128)(2,1)} custom-call(bf16[384,512]{1,0:T(8,128)(2,1)} %get-tuple-element.202.refs_0_, bf16[384,512]{1,0:T(8,128)(2,1)} %get-tuple-element.203.refs_1_, bf16[384,512]{1,0:T(8,128)(2,1)} %get-tuple-element.204.refs_2_, bf16[384,512]{1,0:T(8,128)(2,1)} %get-tuple-element.205.refs_3_, ...), custom_call_target="tpu_custom_call" | custom-call | flops 452984832 | bytes 1671168 | tf_op jit(solution)/shard_map/pallas_call | solution.py:123
  244.4 9.4 %all-to-all-done.12.refs_0_ = bf16[32,48,128]{2,1,0:T(8,128)(2,1)S(1)} async-done(((bf16[32,48,128]{2,1,0:T(8,128)(2,1)}), bf16[32,48,128]{2,1,0:T(8,128)(2,1)S(1)}, u32[]{:S(2)}, u32[]{:S(2)}) %all-to-all-start.12) | async-done | bytes 393248 | tf_op jit(solution)/shard_map/all_to_all | solution.py:1182
  254.6 4.3 %shard_map.423 = (bf16[384,1024]{1,0:T(8,128)(2,1)}, f32[8,128]{1,0:T(8,128)}, f32[8,128]{1,0:T(8,128)}, f32[384,256]{1,0:T(8,128)}, bf16[32,12,128]{2,1,0:T(8,128)(2,1)}, /*index=5*/bf16[2,4,144,512]{3,2,1,0:T(8,128)(2,1)}) custom-call(bf16[32,48,128]{2,1,0:T(8,128)(2,1)} %copy-done.15, ...), custom_call_target="tpu_custom_call", output_to_operand_aliasing={{5}: (11, {})} | custom-call | flops 201326592 | bytes 6172672 | tf_op jit(solution)/shard_map/pallas_call | solution.py:123
  259.0 2.9 all-to-all-start.13
  263.5 3.8 %shard_map.424 = (bf16[4,2,2,96,256]{4,3,2,1,0:T(8,128)(2,1)}, bf16[4,2,2,96,256]{4,3,2,1,0:T(8,128)(2,1)}) custom-call(s32[1]{0:T(128)} %bitcast.23.refs_0_, bf16[384,1024]{1,0:T(8,128)(2,1)} %get-tuple-element.213.refs_1_, bf16[384,512]{1,0:T(8,128)(2,1)} %get-tuple-element.214.refs_2_, bf16[384,256]{1,0:T(8,128)(2,1)} %get-tuple-element.215.refs_3_, ...), custom_call_target="tpu_custom_call" | custom-call | flops 603979776 | bytes 2162688 | tf_op jit(solution)/shard_map/pallas_call | solution.py:123
  270.1 3.6 shard_map.425
  273.8 3.6 all-to-all-start.14
  277.5 3.3 shard_map.426
  280.8 4.3 %all-to-all-done.14.refs_0_ = bf16[32,12,128]{2,1,0:T(8,128)(2,1)S(1)} async-done(((bf16[32,12,128]{2,1,0:T(8,128)(2,1)}), bf16[32,12,128]{2,1,0:T(8,128)(2,1)S(1)}, u32[]{:S(2)}, u32[]{:S(2)}) %all-to-all-start.14) | async-done | bytes 98336 | tf_op jit(solution)/shard_map/all_to_all | solution.py:1182
  293.6 4.7 %shard_map.429 = (bf16[4,200,256]{2,1,0:T(8,128)(2,1)}, bf16[4,200,256]{2,1,0:T(8,128)(2,1)}, bf16[4,200,256]{2,1,0:T(8,128)(2,1)}, bf16[4,200,256]{2,1,0:T(8,128)(2,1)}, bf16[4,336,512]{2,1,0:T(8,128)(2,1)}) custom-call(s32[3]{0:T(128)} %pad_add_fusion.refs_0_, bf16[4,2,2,96,256]{4,3,2,1,0:T(8,128)(2,1)} %get-tuple-element.226.refs_1_, ...), custom_call_target="tpu_custom_call" | custom-call | bytes 4653056 | tf_op jit(solution)/shard_map/pallas_call | solution.py:123
  301.9 9.0 %collective-permute-done.18.refs_4_ = bf16[4,200,256]{2,1,0:T(8,128)(2,1)S(1)} collective-permute-done((bf16[4,200,256]{2,1,0:T(8,128)(2,1)}, bf16[4,200,256]{2,1,0:T(8,128)(2,1)S(1)}, u32[]{:S(2)}, u32[]{:S(2)}) %collective-permute-start.18) | collective-permute-done | bytes 409632 | tf_op jit(solution)/shard_map/ppermute | solution.py:1318
  310.9 9.2 %collective-permute-done.19.refs_5_ = bf16[4,200,256]{2,1,0:T(8,128)(2,1)S(1)} collective-permute-done((bf16[4,200,256]{2,1,0:T(8,128)(2,1)}, bf16[4,200,256]{2,1,0:T(8,128)(2,1)S(1)}, u32[]{:S(2)}, u32[]{:S(2)}) %collective-permute-start.19) | collective-permute-done | bytes 409632 | tf_op jit(solution)/shard_map/ppermute | solution.py:1318
  321.0 3.0 shard_map.430
  324.0 3.6 all-to-all-start.15
  329.5 3.0 shard_map.431
  334.1 8.3 %collective-permute-done.25.refs_3_ = bf16[336,512]{1,0:T(8,128)(2,1)S(1)} collective-permute-done((bf16[336,512]{1,0:T(8,128)(2,1)}, bf16[336,512]{1,0:T(8,128)(2,1)S(1)}, u32[]{:S(2)}, u32[]{:S(2)}) %collective-permute-start.25) | collective-permute-done | bytes 344096 | tf_op jit(solution)/shard_map/ppermute | solution.py:1188
  348.4 3.2 shard_map.432
  351.6 3.0 collective-permute-done.22.refs_2_
  357.8 4.1 %collective-permute-done.28.refs_3_ = bf16[200,256]{1,0:T(8,128)(2,1)S(1)} collective-permute-done((bf16[200,256]{1,0:T(8,128)(2,1)}, bf16[200,256]{1,0:T(8,128)(2,1)S(1)}, u32[]{:S(2)}, u32[]{:S(2)}) %collective-permute-start.28) | collective-permute-done | bytes 102432 | tf_op jit(solution)/shard_map/ppermute | solution.py:1188
  (197 shorter events, 82.9 us)
Async XLA Ops:
  7.2 29.6 %copy-start.1 = (bf16[1024,256]{1,0:T(8,128)(2,1)S(1)}, bf16[1024,256]{1,0:T(8,128)(2,1)}, u32[]{:S(2)}) copy-start(bf16[1024,256]{1,0:T(8,128)(2,1)} %refs_2_.3) | copy-start | bytes 1572868
  9.4 27.4 %all-to-all-start = ((bf16[8,3,16,1024]{3,2,1,0:T(8,128)(2,1)}), bf16[8,3,16,1024]{3,2,1,0:T(8,128)(2,1)S(1)}, u32[]{:S(2)}, u32[]{:S(2)}) async-start(bf16[8,3,16,1024]{3,2,1,0:T(8,128)(2,1)} %bitcast.57), calls=%async_computation | async-start | bytes 1572864 | tf_op jit(solution)/shard_map/all_to_all | solution.py:1185
  16.8 34.9 %copy-start.2 = (f32[3]{0:T(128)}, f32[3]{0:T(128)S(1)}, u32[]{:S(2)}) copy-start(f32[3]{0:T(128)S(1)} %convert_reduce_fusion.refs_0_) | copy-start | bytes 40
  70.6 20.7 %all-to-all-start.3 = ((bf16[32,72,128]{2,1,0:T(8,128)(2,1)}), bf16[32,72,128]{2,1,0:T(8,128)(2,1)S(1)}, u32[]{:S(2)}, u32[]{:S(2)}) async-start(bf16[32,72,128]{2,1,0:T(8,128)(2,1)} %get-tuple-element.153), calls=%async_computation.3 | async-start | bytes 1179648 | tf_op jit(solution)/shard_map/all_to_all | solution.py:1182
  97.2 14.8 %all-to-all-start.4 = ((bf16[32,36,128]{2,1,0:T(8,128)(2,1)}), bf16[32,36,128]{2,1,0:T(8,128)(2,1)S(1)}, u32[]{:S(2)}, u32[]{:S(2)}) async-start(bf16[32,36,128]{2,1,0:T(8,128)(2,1)} %get-tuple-element.155), calls=%async_computation.4 | async-start | bytes 655360 | tf_op jit(solution)/shard_map/all_to_all | solution.py:1182
  117.3 14.8 %all-to-all-start.5 = ((bf16[32,36,128]{2,1,0:T(8,128)(2,1)}), bf16[32,36,128]{2,1,0:T(8,128)(2,1)S(1)}, u32[]{:S(2)}, u32[]{:S(2)}) async-start(bf16[32,36,128]{2,1,0:T(8,128)(2,1)} %get-tuple-element.157), calls=%async_computation.5 | async-start | bytes 655360 | tf_op jit(solution)/shard_map/all_to_all | solution.py:1182
  136.3 10.3 %all-to-all-start.6 = ((f32[32,8,128]{2,1,0:T(8,128)}), f32[32,8,128]{2,1,0:T(8,128)S(1)}, u32[]{:S(2)}, u32[]{:S(2)}) async-start(f32[32,8,128]{2,1,0:T(8,128)} %get-tuple-element.161), calls=%async_computation.6 | async-start | bytes 262144 | tf_op jit(solution)/shard_map/all_to_all | solution.py:1182
  139.7 28.2 %collective-permute-start.1 = (bf16[384,512]{1,0:T(8,128)(2,1)S(1)}, bf16[384,512]{1,0:T(8,128)(2,1)S(1)}, u32[]{:S(2)}, u32[]{:S(2)}) collective-permute-start(bf16[384,512]{1,0:T(8,128)(2,1)S(1)} %copy-done.11), channel_id=1, source_target_pairs={{0,16},{16,0},{1,17},{17,1},{2,18},{18,2},{3,19},{19,3},{4,20},{20... | collective-permute-start | bytes 1179656 | tf_op jit(solution)/shard_map/ppermute | solution.py:1188
  163.6 10.3 %all-to-all-start.8 = ((f32[32,8,128]{2,1,0:T(8,128)}), f32[32,8,128]{2,1,0:T(8,128)S(1)}, u32[]{:S(2)}, u32[]{:S(2)}) async-start(f32[32,8,128]{2,1,0:T(8,128)} %get-tuple-element.165), calls=%async_computation.8 | async-start | bytes 262144 | tf_op jit(solution)/shard_map/all_to_all | solution.py:1182
  166.2 12.9 %collective-permute-start.4 = (bf16[96,1024]{1,0:T(8,128)(2,1)S(1)}, bf16[96,1024]{1,0:T(8,128)(2,1)S(1)}, u32[]{:S(2)}, u32[]{:S(2)}) collective-permute-start(bf16[96,1024]{1,0:T(8,128)(2,1)S(1)} %copy-done.7), channel_id=1, source_target_pairs={{0,16},{16,0},{1,17},{17,1},{2,18},{18,2},{3,19},{19,3},{4,20},{20... | collective-permute-start | bytes 589832 | tf_op jit(solution)/shard_map/ppermute | solution.py:1188
  167.9 17.4 %collective-permute-start = (bf16[384,512]{1,0:T(8,128)(2,1)S(1)}, bf16[384,512]{1,0:T(8,128)(2,1)S(1)}, u32[]{:S(2)}, u32[]{:S(2)}) collective-permute-start(bf16[384,512]{1,0:T(8,128)(2,1)S(1)} %copy-done.11), channel_id=1, source_target_pairs={{0,8},{8,0},{1,9},{9,1},{2,10},{10,2},{3,11},{11,3},{4,12},{12,4},... | collective-permute-start | bytes 1179656 | tf_op jit(solution)/shard_map/ppermute | solution.py:1188
  167.9 18.7 %collective-permute-start.2 = (bf16[384,512]{1,0:T(8,128)(2,1)S(1)}, bf16[384,512]{1,0:T(8,128)(2,1)S(1)}, u32[]{:S(2)}, u32[]{:S(2)}) collective-permute-start(bf16[384,512]{1,0:T(8,128)(2,1)S(1)} %collective-permute-done.1.refs_15_), channel_id=1, source_target_pairs={{0,8},{8,0},{1,9},{9,1},{2,10},{10,2},{3,11},{11,3},{4,12},{12,4},... | collective-permute-start | bytes 1179656 | tf_op jit(solution)/shard_map/ppermute | solution.py:1188
  168.4 12.4 %collective-permute-start.3 = (bf16[96,1024]{1,0:T(8,128)(2,1)S(1)}, bf16[96,1024]{1,0:T(8,128)(2,1)S(1)}, u32[]{:S(2)}, u32[]{:S(2)}) collective-permute-start(bf16[96,1024]{1,0:T(8,128)(2,1)S(1)} %copy-done.7), channel_id=1, source_target_pairs={{0,8},{8,0},{1,9},{9,1},{2,10},{10,2},{3,11},{11,3},{4,12},{12,4},... | collective-permute-start | bytes 589832 | tf_op jit(solution)/shard_map/ppermute | solution.py:1188
  176.3 10.3 %all-to-all-start.9 = ((f32[32,8,128]{2,1,0:T(8,128)}), f32[32,8,128]{2,1,0:T(8,128)S(1)}, u32[]{:S(2)}, u32[]{:S(2)}) async-start(f32[32,8,128]{2,1,0:T(8,128)} %shard_map.416), calls=%async_computation.9 | async-start | bytes 262144 | tf_op jit(solution)/shard_map/all_to_all | solution.py:1182
  179.1 6.2 %collective-permute-start.5 = (bf16[96,1024]{1,0:T(8,128)(2,1)S(1)}, bf16[96,1024]{1,0:T(8,128)(2,1)S(1)}, u32[]{:S(2)}, u32[]{:S(2)}) collective-permute-start(bf16[96,1024]{1,0:T(8,128)(2,1)S(1)} %collective-permute-done.4.refs_19_), channel_id=1, source_target_pairs={{0,8},{8,0},{1,9},{9,1},{2,10},{10,2},{3,11},{11,3},{4,12},{12,4},... | collective-permute-start | bytes 589832 | tf_op jit(solution)/shard_map/ppermute | solution.py:1188
  179.2 6.1 %collective-permute-start.7 = (bf16[96,512]{1,0:T(8,128)(2,1)S(1)}, bf16[96,512]{1,0:T(8,128)(2,1)S(1)}, u32[]{:S(2)}, u32[]{:S(2)}) collective-permute-start(bf16[96,512]{1,0:T(8,128)(2,1)S(1)} %copy-done.32), channel_id=1, source_target_pairs={{0,16},{16,0},{1,17},{17,1},{2,18},{18,2},{3,19},{19,3},{4,20},{20... | collective-permute-start | bytes 294920 | tf_op jit(solution)/shard_map/ppermute | solution.py:1188
  180.8 4.5 %collective-permute-start.6 = (bf16[96,512]{1,0:T(8,128)(2,1)S(1)}, bf16[96,512]{1,0:T(8,128)(2,1)S(1)}, u32[]{:S(2)}, u32[]{:S(2)}) collective-permute-start(bf16[96,512]{1,0:T(8,128)(2,1)S(1)} %copy-done.32), channel_id=1, source_target_pairs={{0,8},{8,0},{1,9},{9,1},{2,10},{10,2},{3,11},{11,3},{4,12},{12,4},... | collective-permute-start | bytes 294920 | tf_op jit(solution)/shard_map/ppermute | solution.py:1188
  185.3 1.3 collective-permute-start.8
  191.9 18.5 %all-to-all-start.10 = ((bf16[32,24,128]{2,1,0:T(8,128)(2,1)}), bf16[32,24,128]{2,1,0:T(8,128)(2,1)S(1)}, u32[]{:S(2)}, u32[]{:S(2)}) async-start(bf16[32,24,128]{2,1,0:T(8,128)(2,1)} %get-tuple-element.170), calls=%async_computation.10 | async-start | bytes 393216 | tf_op jit(solution)/shard_map/all_to_all | solution.py:1182
  196.9 6.5 %collective-permute-start.9 = (bf16[96,1024]{1,0:T(8,128)(2,1)}, bf16[96,1024]{1,0:T(8,128)(2,1)S(1)}, u32[]{:S(2)}, u32[]{:S(2)}) collective-permute-start(bf16[96,1024]{1,0:T(8,128)(2,1)} %get-tuple-element.174), channel_id=1, source_target_pairs={{0,8},{8,0},{16,24},{24,16},{1,9},{9,1},{17,25},{25,17},{2,10},{10... | collective-permute-start | bytes 589832 | tf_op jit(solution)/shard_map/ppermute | solution.py:1192
  197.2 9.6 %collective-permute-start.10 = (bf16[96,1024]{1,0:T(8,128)(2,1)}, bf16[96,1024]{1,0:T(8,128)(2,1)S(1)}, u32[]{:S(2)}, u32[]{:S(2)}) collective-permute-start(bf16[96,1024]{1,0:T(8,128)(2,1)} %get-tuple-element.175), channel_id=1, source_target_pairs={{0,16},{8,24},{16,0},{24,8},{1,17},{9,25},{17,1},{25,9},{2,18},{10... | collective-permute-start | bytes 589832 | tf_op jit(solution)/shard_map/ppermute | solution.py:1192
  198.9 11.5 %collective-permute-start.11 = (bf16[96,1024]{1,0:T(8,128)(2,1)}, bf16[96,1024]{1,0:T(8,128)(2,1)S(1)}, u32[]{:S(2)}, u32[]{:S(2)}) collective-permute-start(bf16[96,1024]{1,0:T(8,128)(2,1)} %get-tuple-element.176), channel_id=1, source_target_pairs={{0,24},{8,16},{16,8},{24,0},{1,25},{9,17},{17,9},{25,1},{2,26},{10... | collective-permute-start | bytes 589832 | tf_op jit(solution)/shard_map/ppermute | solution.py:1192
  217.1 13.2 %all-to-all-start.11 = ((bf16[32,24,128]{2,1,0:T(8,128)(2,1)}), bf16[32,24,128]{2,1,0:T(8,128)(2,1)S(1)}, u32[]{:S(2)}, u32[]{:S(2)}) async-start(bf16[32,24,128]{2,1,0:T(8,128)(2,1)} %get-tuple-element.178), calls=%async_computation.11 | async-start | bytes 393216 | tf_op jit(solution)/shard_map/all_to_all | solution.py:1182
  221.8 47.6 %reduce-scatter.4.cloned.1.call-start = ((), (), s32[]{:S(2)}) async-start(), calls=%async_computation.19 | async-start | bytes 2359296 | tf_op jit(solution)/shard_map/reduce_scatter | solution.py:1287
  221.8 5.8 %collective-permute-start.12 = (bf16[96,128]{1,0:T(8,128)(2,1)}, bf16[96,128]{1,0:T(8,128)(2,1)S(1)}, u32[]{:S(2)}, u32[]{:S(2)}) collective-permute-start(bf16[96,128]{1,0:T(8,128)(2,1)} %get-tuple-element.196), channel_id=1, source_target_pairs={{0,8},{8,0},{16,24},{24,16},{1,9},{9,1},{17,25},{25,17},{2,10},{10... | collective-permute-start | bytes 73736 | tf_op jit(solution)/shard_map/ppermute | solution.py:1192
  222.2 5.5 %collective-permute-start.13 = (bf16[96,128]{1,0:T(8,128)(2,1)}, bf16[96,128]{1,0:T(8,128)(2,1)S(1)}, u32[]{:S(2)}, u32[]{:S(2)}) collective-permute-start(bf16[96,128]{1,0:T(8,128)(2,1)} %get-tuple-element.197), channel_id=1, source_target_pairs={{0,16},{8,24},{16,0},{24,8},{1,17},{9,25},{17,1},{25,9},{2,18},{10... | collective-permute-start | bytes 73736 | tf_op jit(solution)/shard_map/ppermute | solution.py:1192
  223.8 3.9 %collective-permute-start.14 = (bf16[96,128]{1,0:T(8,128)(2,1)}, bf16[96,128]{1,0:T(8,128)(2,1)S(1)}, u32[]{:S(2)}, u32[]{:S(2)}) collective-permute-start(bf16[96,128]{1,0:T(8,128)(2,1)} %get-tuple-element.198), channel_id=1, source_target_pairs={{0,24},{8,16},{16,8},{24,0},{1,25},{9,17},{17,9},{25,1},{2,26},{10... | collective-permute-start | bytes 73736 | tf_op jit(solution)/shard_map/ppermute | solution.py:1192
  237.1 16.8 %all-to-all-start.12 = ((bf16[32,48,128]{2,1,0:T(8,128)(2,1)}), bf16[32,48,128]{2,1,0:T(8,128)(2,1)S(1)}, u32[]{:S(2)}, u32[]{:S(2)}) async-start(bf16[32,48,128]{2,1,0:T(8,128)(2,1)} %get-tuple-element.199), calls=%async_computation.12 | async-start | bytes 786432 | tf_op jit(solution)/shard_map/all_to_all | solution.py:1182
  240.3 51.7 %reduce-scatter.6.cloned.1.call-start = ((), (), s32[]{:S(2)}) async-start(), calls=%async_computation.20 | async-start | bytes 1769472 | tf_op jit(solution)/shard_map/reduce_scatter | solution.py:1295
  259.0 10.5 %all-to-all-start.13 = ((bf16[32,12,128]{2,1,0:T(8,128)(2,1)}), bf16[32,12,128]{2,1,0:T(8,128)(2,1)S(1)}, u32[]{:S(2)}, u32[]{:S(2)}) async-start(bf16[32,12,128]{2,1,0:T(8,128)(2,1)} %get-tuple-element.210), calls=%async_computation.13 | async-start | bytes 262144 | tf_op jit(solution)/shard_map/all_to_all | solution.py:1182
  273.7 11.5 %collective-permute-start.15 = (bf16[4,2,2,96,256]{4,3,2,1,0:T(8,128)(2,1)}, bf16[4,2,2,96,256]{4,3,2,1,0:T(8,128)(2,1)S(1)}, u32[]{:S(2)}, u32[]{:S(2)}) collective-permute-start(bf16[4,2,2,96,256]{4,3,2,1,0:T(8,128)(2,1)} %get-tuple-element.224), channel_id=1, source_target_pairs={{0,8},{8,0},{1,9},{9,1},{2,10},{10,2},{3,11},{11,3},{4,12},{12,4},... | collective-permute-start | bytes 2359304 | tf_op jit(solution)/shard_map/ppermute | solution.py:1188
  273.8 11.3 %all-to-all-start.14 = ((bf16[32,12,128]{2,1,0:T(8,128)(2,1)}), bf16[32,12,128]{2,1,0:T(8,128)(2,1)S(1)}, u32[]{:S(2)}, u32[]{:S(2)}) async-start(bf16[32,12,128]{2,1,0:T(8,128)(2,1)} %get-tuple-element.219), calls=%async_computation.15 | async-start | bytes 262144 | tf_op jit(solution)/shard_map/all_to_all | solution.py:1182
  277.4 52.1 %reduce-scatter.8.cloned.1.call-start = ((), (), s32[]{:S(2)}) async-start(), calls=%async_computation.21 | async-start | bytes 1720320 | tf_op jit(solution)/shard_map/reduce_scatter | solution.py:1333
  288.3 4.5 %collective-permute-start.16 = (bf16[4,2,2,72,256]{4,3,2,1,0:T(8,128)(2,1)}, bf16[4,2,2,72,256]{4,3,2,1,0:T(8,128)(2,1)S(1)}, u32[]{:S(2)}, u32[]{:S(2)}) collective-permute-start(bf16[4,2,2,72,256]{4,3,2,1,0:T(8,128)(2,1)} %get-tuple-element.229), channel_id=1, source_target_pairs={{0,8},{8,0},{1,9},{9,1},{2,10},{10,2},{3,11},{11,3},{4,12},{12,4},... | collective-permute-start | bytes 1769480 | tf_op jit(solution)/shard_map/ppermute | solution.py:1188
  290.9 1.8 collective-permute-start.17
  298.4 12.6 %collective-permute-start.18 = (bf16[4,200,256]{2,1,0:T(8,128)(2,1)}, bf16[4,200,256]{2,1,0:T(8,128)(2,1)S(1)}, u32[]{:S(2)}, u32[]{:S(2)}) collective-permute-start(bf16[4,200,256]{2,1,0:T(8,128)(2,1)} %get-tuple-element.235), channel_id=1, source_target_pairs={{0,1},{1,0},{16,17},{17,16},{2,3},{3,2},{18,19},{19,18},{4,5},{5,4... | collective-permute-start | bytes 1228808 | tf_op jit(solution)/shard_map/ppermute | solution.py:1318
  299.7 20.4 %collective-permute-start.19 = (bf16[4,200,256]{2,1,0:T(8,128)(2,1)}, bf16[4,200,256]{2,1,0:T(8,128)(2,1)S(1)}, u32[]{:S(2)}, u32[]{:S(2)}) collective-permute-start(bf16[4,200,256]{2,1,0:T(8,128)(2,1)} %get-tuple-element.236), channel_id=1, source_target_pairs={{0,16},{1,17},{16,0},{17,1},{2,18},{3,19},{18,2},{19,3},{4,20},{5,... | collective-permute-start | bytes 1228808 | tf_op jit(solution)/shard_map/ppermute | solution.py:1318
  300.4 19.7 %collective-permute-start.20 = (bf16[4,200,256]{2,1,0:T(8,128)(2,1)}, bf16[4,200,256]{2,1,0:T(8,128)(2,1)S(1)}, u32[]{:S(2)}, u32[]{:S(2)}) collective-permute-start(bf16[4,200,256]{2,1,0:T(8,128)(2,1)} %get-tuple-element.237), channel_id=1, source_target_pairs={{0,17},{1,16},{16,1},{17,0},{2,19},{3,18},{18,3},{19,2},{4,21},{5,... | collective-permute-start | bytes 1228808 | tf_op jit(solution)/shard_map/ppermute | solution.py:1318
  324.0 37.9 %all-to-all-start.15 = ((bf16[8,3,16,1024]{3,2,1,0:T(8,128)(2,1)}), bf16[8,3,16,1024]{3,2,1,0:T(8,128)(2,1)S(1)}, u32[]{:S(2)}, u32[]{:S(2)}) async-start(bf16[8,3,16,1024]{3,2,1,0:T(8,128)(2,1)} %get-tuple-element.238), calls=%async_computation.17 | async-start | bytes 1572864 | tf_op jit(solution)/shard_map/all_to_all | solution.py:1185
  332.6 9.9 %collective-permute-start.25 = (bf16[336,512]{1,0:T(8,128)(2,1)}, bf16[336,512]{1,0:T(8,128)(2,1)S(1)}, u32[]{:S(2)}, u32[]{:S(2)}) collective-permute-start(bf16[336,512]{1,0:T(8,128)(2,1)} %bitcast.64), channel_id=1, source_target_pairs={{0,16},{16,0},{1,17},{17,1},{2,18},{18,2},{3,19},{19,3},{4,20},{20... | collective-permute-start | bytes 1032200 | tf_op jit(solution)/shard_map/ppermute | solution.py:1188
  334.1 12.7 %collective-permute-start.24 = (bf16[336,512]{1,0:T(8,128)(2,1)}, bf16[336,512]{1,0:T(8,128)(2,1)S(1)}, u32[]{:S(2)}, u32[]{:S(2)}) collective-permute-start(bf16[336,512]{1,0:T(8,128)(2,1)} %bitcast.65), channel_id=1, source_target_pairs={{0,8},{8,0},{1,9},{9,1},{2,10},{10,2},{3,11},{11,3},{4,12},{12,4},... | collective-permute-start | bytes 1032200 | tf_op jit(solution)/shard_map/ppermute | solution.py:1188
  342.5 4.4 %collective-permute-start.26 = (bf16[336,512]{1,0:T(8,128)(2,1)S(1)}, bf16[336,512]{1,0:T(8,128)(2,1)S(1)}, u32[]{:S(2)}, u32[]{:S(2)}) collective-permute-start(bf16[336,512]{1,0:T(8,128)(2,1)S(1)} %collective-permute-done.25.refs_3_), channel_id=1, source_target_pairs={{0,8},{8,0},{1,9},{9,1},{2,10},{10,2},{3,11},{11,3},{4,12},{12,4},... | collective-permute-start | bytes 1032200 | tf_op jit(solution)/shard_map/ppermute | solution.py:1188
  342.5 9.1 %collective-permute-start.21 = (bf16[200,256]{1,0:T(8,128)(2,1)}, bf16[200,256]{1,0:T(8,128)(2,1)S(1)}, u32[]{:S(2)}, u32[]{:S(2)}) collective-permute-start(bf16[200,256]{1,0:T(8,128)(2,1)} %get-tuple-element.245), channel_id=1, source_target_pairs={{0,2},{2,0},{4,6},{6,4},{1,3},{3,1},{5,7},{7,5},{8,10},{10,8},{12,... | collective-permute-start | bytes 307208 | tf_op jit(solution)/shard_map/ppermute | solution.py:1188
  342.5 12.0 %collective-permute-start.22 = (bf16[200,256]{1,0:T(8,128)(2,1)}, bf16[200,256]{1,0:T(8,128)(2,1)S(1)}, u32[]{:S(2)}, u32[]{:S(2)}) collective-permute-start(bf16[200,256]{1,0:T(8,128)(2,1)} %get-tuple-element.246), channel_id=1, source_target_pairs={{0,4},{2,6},{4,0},{6,2},{1,5},{3,7},{5,1},{7,3},{8,12},{10,14},{12... | collective-permute-start | bytes 307208 | tf_op jit(solution)/shard_map/ppermute | solution.py:1188
  344.4 10.1 %collective-permute-start.23 = (bf16[200,256]{1,0:T(8,128)(2,1)}, bf16[200,256]{1,0:T(8,128)(2,1)S(1)}, u32[]{:S(2)}, u32[]{:S(2)}) collective-permute-start(bf16[200,256]{1,0:T(8,128)(2,1)} %get-tuple-element.247), channel_id=1, source_target_pairs={{0,6},{2,4},{4,2},{6,0},{1,7},{3,5},{5,3},{7,1},{8,14},{10,12},{12... | collective-permute-start | bytes 307208 | tf_op jit(solution)/shard_map/ppermute | solution.py:1188
  357.0 4.9 %collective-permute-start.28 = (bf16[200,256]{1,0:T(8,128)(2,1)}, bf16[200,256]{1,0:T(8,128)(2,1)S(1)}, u32[]{:S(2)}, u32[]{:S(2)}) collective-permute-start(bf16[200,256]{1,0:T(8,128)(2,1)} %get-tuple-element.252.refs_1_), channel_id=1, source_target_pairs={{0,16},{16,0},{1,17},{17,1},{2,18},{18,2},{3,19},{19,3},{4,20},{20... | collective-permute-start | bytes 307208 | tf_op jit(solution)/shard_map/ppermute | solution.py:1188
  357.8 5.1 %collective-permute-start.27 = (bf16[200,256]{1,0:T(8,128)(2,1)}, bf16[200,256]{1,0:T(8,128)(2,1)S(1)}, u32[]{:S(2)}, u32[]{:S(2)}) collective-permute-start(bf16[200,256]{1,0:T(8,128)(2,1)} %get-tuple-element.252.refs_1_), channel_id=1, source_target_pairs={{0,8},{8,0},{1,9},{9,1},{2,10},{10,2},{3,11},{11,3},{4,12},{12,4},... | collective-permute-start | bytes 307208 | tf_op jit(solution)/shard_map/ppermute | solution.py:1188
  361.9 1.3 collective-permute-start.29
  (49 other events, 166.0 us)
Sparse Core Ops, SparseCore 0:
  237.2 28.2 reduce-scatter.3
  268.4 23.0 reduce-scatter.5
  298.5 30.9 reduce-scatter.7

commit v2 on v1

--- a/solution.py
+++ b/solution.py
@@ -43,6 +43,13 @@
     return 0.5 * (1.0 + t) + (0.5 * ROOT) * v * (1.0 - t * t) * (1.0 + (3.0 * CUBE) * square)
 
 
+def gelu_both(v):
+    square = v * v
+    t = jnp.tanh(ROOT * (v + CUBE * (square * v)))
+    half = 0.5 * (1.0 + t)
+    return v * half, half + (0.5 * ROOT) * v * (1.0 - t * t) * (1.0 + (3.0 * CUBE) * square)
+
+
 def cols(c):
     return pl.ds(c * LANES, LANES)
 
@@ -57,8 +64,9 @@
         self.w_copies, self.out_pairs, self.sems = starts, {}, sems
         self.flying, self.sent = [], set()
 
-    def wait_w(self, n=0):
-        self.w_copies[n].wait()
+    def wait_w(self, n=0, chunk=None):
+        for copy in self.w_copies[n] if chunk is None else [self.w_copies[n][chunk]]:
+            copy.wait()
 
     def send(self, n):
         src, dst, sem = self.out_pairs[n]
@@ -73,7 +81,7 @@
         self.flying.append(copy)
 
 
-def kernel_call(body, outs, args, weights=(), scratch=(), flops=0, raw=(), n_raw=0, scalars=(), passes=(), stacks=(), limit=60):
+def kernel_call(body, outs, args, weights=(), scratch=(), flops=0, raw=(), n_raw=0, scalars=(), passes=(), stacks=(), limit=63, chunks=1):
     n_s, n_in, n_w, n_p = len(scalars), len(args), len(weights), len(passes)
     n_k = sum(map(len, stacks))
     n_out, n_r = len(outs), len(raw)
@@ -92,14 +100,18 @@
         out, raw_refs, _ = take(n_out), take(n_r), take(n_p)
         v_in, v_w, v_out, v_k = take(n_in), take(n_w), take(n_out), take(len(stacks))
         (sems,) = take(1)
-        sem = [sems.at[j] for j in range(n_in + n_w + n_k + n_out + n_raw)]
+        sem = [sems.at[j] for j in range(n_in + n_w * chunks + n_k + n_out + n_raw)]
         in_copies = [pltpu.make_async_copy(a, v, sem.pop(0)) for a, v in zip(ins, v_in)]
         for pile, v in zip(piles, v_k):
             for j, a in enumerate(pile):
                 rows = a.shape[0]
                 in_copies.append(pltpu.make_async_copy(a, v.at[pl.ds(j * rows, rows)], sem.pop(0)))
-        w_copies = [pltpu.make_async_copy(a, v, sem.pop(0)) for a, v in zip(w_any, v_w)]
-        for copy in in_copies + w_copies:
+        w_copies = []
+        for a, v in zip(w_any, v_w):
+            some = a.shape[0] // chunks
+            parts = [pl.ds(j * some, some) for j in range(chunks)]
+            w_copies.append([pltpu.make_async_copy(a.at[at], v.at[at], sem.pop(0)) for at in parts])
+        for copy in in_copies + [c for copies in w_copies for c in copies]:
             copy.start()
         k = Kernel(v_in, v_w, v_out, raw_refs, s, v_k, refs, w_copies, sem[n_out:])
         k.out_pairs = {j: (v_out[j], out[j], sem[j]) for j in range(n_out)}
@@ -126,7 +138,7 @@
         in_specs=[pl.BlockSpec(memory_space=pltpu.SMEM)] * n_s + [outside] * (n_in + n_w + n_k + n_p),
         out_specs=tuple([outside] * (n_out + n_r + n_p)),
         scratch_shapes=[pltpu.VMEM(a.shape, a.dtype) for a in (*args, *weights, *outs, *piled)]
-        + [pltpu.SemaphoreType.DMA((n_in + n_w + n_k + n_out + n_raw,))]
+        + [pltpu.SemaphoreType.DMA((n_in + n_w * chunks + n_k + n_out + n_raw,))]
         + list(scratch),
         input_output_aliases={first + j: n_out + n_r + j for j in range(n_p)},
         cost_estimate=pl.CostEstimate(flops=flops, bytes_accessed=held, transcendentals=0),
@@ -362,48 +374,88 @@
         act_ref, next_ref, pay_ref, st_ref = k.o
         (rows_ref,) = k.x
         merge_stats(got_ref, mates_ref, st_ref, q, z.rows)
+        k_o, k_q = MICRO * qo, MICRO * q
+        rows_ref[...] = jnp.zeros(rows_ref.shape, F32)
         for m in range(MICRO):
             for c in range(q):
                 mean, inverse = row(st_ref, m * q + c), row(st_ref, (MICRO + m) * q + c)
                 at = pl.ds(m * z.rows, z.rows)
                 x = pre_ref[at, cols(c)]
-                act_ref[at, cols(c)] = gelu(g_ref[:, cols(c)] * ((x - mean) * inverse) + o_ref[:, cols(c)]).astype(BF)
+                act = gelu(g_ref[:, cols(c)] * ((x - mean) * inverse) + o_ref[:, cols(c)]).astype(BF)
+                act_ref[at, cols(c)] = act
+                mean = jnp.sum(act.astype(F32), axis=0, keepdims=True) * (1.0 / z.rows)
+                high = mean.astype(BF).astype(F32)
+                rows_ref[pl.ds(k_o + m * q + c, 1), :] = high
+                rows_ref[pl.ds(k_o + k_q + m * q + c, 1), :] = mean - high
         k.send(0)
         k.wait_w()
         next_ref[...] = dot(act_ref[...], k.w[0][...])
         k.send(1)
         for m in range(MICRO):
             for c in range(qo):
-                stats_rows(next_ref[pl.ds(m * z.rows, z.rows), cols(c)], rows_ref, m * qo + c, z.rows, MICRO * qo)
-        fill_stats(pay_ref, rows_ref, qo)
+                x = next_ref[pl.ds(m * z.rows, z.rows), cols(c)]
+                away = x - jnp.sum(x, axis=0, keepdims=True) * (1.0 / z.rows)
+                rows_ref[pl.ds(m * qo + c, 1), :] = jnp.sum(away * away, axis=0, keepdims=True)
+        fill(pay_ref, rows_ref)
 
     rows = MICRO * z.rows
     return kernel_call(
         body,
-        [arr(rows, z.c_mid, dtype=BF), arr(rows, z.c_in), stats_arr(z.n, qo), arr(6 * q, LANES)],
+        [arr(rows, z.c_mid, dtype=BF), arr(rows, z.c_in), arr(z.n, z.q_product, LANES, dtype=BF), arr(6 * q, LANES)],
         [got, mates, pre, gain, offset],
         [w],
-        [pltpu.VMEM((stats_shape(qo)[0], LANES), F32)],
+        [pltpu.VMEM((z.q_product, LANES), F32)],
         flops=2 * rows * z.c_in * z.c_mid,
     )
 
 
-def k_narrow(got, mates, pre, gain, offset, maps_in, w, z):
+def merge_product(got_ref, mates_ref, same_ref, w_ref, line_ref, st_ref, between_ref, q, qo, size):
+    n, tall = got_ref.shape[0], got_ref.shape[1]
+    ko, kq = MICRO * qo, MICRO * q
+    mates = n // NVIEW
+    got = got_ref[...].astype(F32)
+    line_ref[...] = got.reshape(n * tall, LANES)
+    squares = jnp.sum(mates_ref[...] * got[:, :ko], axis=0)
+
+    def part(r):
+        return line_ref[pl.ds(r, n, stride=tall), :].astype(BF)
+
+    lines = [
+        jnp.concatenate([part(first + m * q + c) for c in range(q)], axis=1)
+        for first in (ko, ko + kq)
+        for m in range(MICRO)
+    ]
+    both = dot(jnp.concatenate(lines, axis=0), w_ref[...])
+    means = both[: MICRO * n] + both[MICRO * n :]
+    for m in range(MICRO):
+        same = same_ref[m]
+        for c in range(qo):
+            x = means[m * n : (m + 1) * n, c * LANES : (c + 1) * LANES]
+            mean = jnp.sum(same * x, axis=0, keepdims=True) * (1.0 / mates)
+            away = x - mean
+            st_ref[pl.ds(m * qo + c, 1), :] = mean
+            between_ref[pl.ds(m * qo + c, 1), :] = jnp.sum(same * (away * away), axis=0, keepdims=True)
+    total = squares + size * between_ref[...]
+    st_ref[ko:] = lax.rsqrt(total * (1.0 / (mates * size)) + EPSILON)
+
+
+def k_narrow(got, mates, same, pre, gain, offset, maps_in, w_before, w, z):
     q, qo = z.q3, z.q4
 
     def body(k):
-        got_ref, mates_ref, pre_ref, g_ref, o_ref, in_ref = k.i
-        res_ref, join_ref, even_ref, next_ref, pay_ref, st_ref = k.o
-        (rows_ref,) = k.x
-        merge_stats(got_ref, mates_ref, st_ref, q, z.rows)
+        got_ref, mates_ref, same_ref, wb_ref, pre_ref, g_ref, o_ref, in_ref = k.i
+        slope_ref, join_ref, even_ref, next_ref, pay_ref, st_ref = k.o
+        rows_ref, line_ref, between_ref = k.x
+        merge_product(got_ref, mates_ref, same_ref, wb_ref, line_ref, st_ref, between_ref, z.q1, q, z.rows)
         for m in range(MICRO):
             for c in range(q):
                 mean, inverse = row(st_ref, m * q + c), row(st_ref, (MICRO + m) * q + c)
                 at = pl.ds(m * z.rows, z.rows)
                 x = pre_ref[at, cols(c)]
                 res = g_ref[:, cols(c)] * ((x - mean) * inverse) + o_ref[:, cols(c)] + in_ref[at, cols(c)].astype(F32)
-                res_ref[at, cols(c)] = res
-                joined = gelu(res).astype(BF)
+                joined, slope = gelu_both(res)
+                slope_ref[at, cols(c)] = slope.astype(BF)
+                joined = joined.astype(BF)
                 join_ref[at, cols(c)] = joined
                 even_ref[pl.ds(m * z.half, z.half), cols(c)] = joined[: z.half]
         for j in range(3):
@@ -420,16 +472,20 @@
     return kernel_call(
         body,
         [
-            arr(rows, z.c_in),
+            arr(rows, z.c_in, dtype=BF),
             arr(rows, z.c_in, dtype=BF),
             arr(MICRO * z.half, z.c_in, dtype=BF),
             arr(rows, z.c_wide),
             stats_arr(z.n, qo),
             arr(6 * q, LANES),
         ],
-        [got, mates, pre, gain, offset, maps_in],
+        [got, mates, same, w_before, pre, gain, offset, maps_in],
         [w],
-        [pltpu.VMEM((stats_shape(qo)[0], LANES), F32)],
+        [
+            pltpu.VMEM((stats_shape(qo)[0], LANES), F32),
+            pltpu.VMEM((z.n * z.q_product, LANES), F32),
+            pltpu.VMEM((MICRO * q, LANES), F32),
+        ],
         flops=2 * rows * z.c_in * z.c_wide,
     )
 
@@ -452,8 +508,12 @@
                     act_ref[pl.ds(m * z.rows + i * z.half, z.half), cols(c)] = phase[p].astype(BF)
                 write_patches(phase, patch_ref, m, z.half, c, z.c_wide, 1, ((0, 0),))
         k.send(0)
-        k.wait_w()
-        next_ref[...] = dot(patch_ref[...], k.w[0][...])
+        value = 0.0
+        for tap in range(9):
+            k.wait_w(chunk=tap)
+            at = pl.ds(tap * z.c_wide, z.c_wide)
+            value = value + dot(patch_ref[:, at], k.w[0][at])
+        next_ref[...] = value
         k.send(1)
         for m in range(MICRO):
             for c in range(q):
@@ -469,21 +529,26 @@
         [pltpu.VMEM((rows, 9 * z.c_wide), BF), pltpu.VMEM((stats_shape(q)[0], LANES), F32)],
         flops=2 * rows * 9 * z.c_wide * z.c_wide,
         passes=passes,
+        chunks=9,
     )
 
 
 def k_shortcut(even, w, z):
     def body(k):
         (e_ref,), (next_ref, st_ref) = k.i, k.o
-        k.wait_w()
-        next_ref[...] = dot(e_ref[...], k.w[0][...])
+        value = 0.0
+        for j in range(4):
+            k.wait_w(chunk=j)
+            at = pl.ds(j * z.c_in // 4, z.c_in // 4)
+            value = value + dot(e_ref[:, at], k.w[0][at])
+        next_ref[...] = value
         for c in range(z.q6):
             for m in range(MICRO):
                 stats_rows(next_ref[pl.ds(m * z.half, z.half), cols(c)], st_ref.at[c], m, z.half, MICRO)
 
     rows = MICRO * z.half
     return kernel_call(
-        body, [arr(rows, z.c_out), arr(z.q6, 8, LANES)], [even], [w], flops=2 * rows * z.c_in * z.c_out
+        body, [arr(rows, z.c_out), arr(z.q6, 8, LANES)], [even], [w], flops=2 * rows * z.c_in * z.c_out, chunks=4
     )
 
 
@@ -539,7 +604,7 @@
         pay_ref[...] = jnp.where(ids > 0.5, hi[...][None], lo[...][None])
 
     return kernel_call(
-        body, [arr(z.n, 8, LANES)], [got, ids], scratch=[pltpu.VMEM((8, LANES), F32)] * 2
+        body, [arr(z.n, 8, LANES)], [got, ids], scratch=[pltpu.VMEM((8, LANES), F32)] * 2, limit=16
     )[0]
 
 
@@ -592,7 +657,7 @@
                 both[v, pl.ds(2 * MICRO + k, 1), :] = totals[k]
         pay_ref[...] = jnp.where(ids > 0.5, both[1][None], both[0][None])
 
-    return kernel_call(body, [arr(z.n, 8, LANES)], [got, ids], scratch=[pltpu.VMEM((2, 8, LANES), F32)])[0]
+    return kernel_call(body, [arr(z.n, 8, LANES)], [got, ids], scratch=[pltpu.VMEM((2, 8, LANES), F32)], limit=16)[0]
 
 
 def back_rows(x, d, st_ref, sum_ref, m, q, c, gain):
@@ -679,7 +744,7 @@
         at = pl.ds(m * n_rows, n_rows)
         for c in range(q):
             out_ref[at, cols(c)] = back_rows(
-                pre_ref[at, cols(c)], d_ref[at, cols(c)], st_ref, sum_ref, m, q, c, g_ref[:, cols(c)]
+                pre_ref[at, cols(c)], d_ref[at, cols(c)].astype(F32), st_ref, sum_ref, m, q, c, g_ref[:, cols(c)]
             ).astype(BF)
 
 
@@ -695,8 +760,10 @@
         for j in range(z.g):
             at = pl.ds(pl.multiple_of(((k.s[0][0] & (z.g - 1)) ^ j) * some, some), some)
             k.copy(delta_ref.at[:, at], k.raw[j])
-        k.wait_w()
-        contrib[...] = dot_nt(delta_ref[...], k.w[0][...])
+        for tap in range(9):
+            k.wait_w(chunk=tap)
+            at = pl.ds(tap * z.c_wide, z.c_wide)
+            contrib[:, at] = dot_nt(delta_ref[...], k.w[0][at])
         for m in range(MICRO):
             for c in range(q):
                 phase = {}
@@ -734,17 +801,18 @@
         ],
         flops=2 * rows * 9 * z.c_wide * z.c_wide,
         passes=passes,
+        chunks=9,
         raw=[arr(rows, z.c_wide // z.g, dtype=BF)] * z.g,
         n_raw=z.g,
         scalars=[place],
     )
 
 
-def k_back_narrow(got, mates, d, pre_n, st_n, gain_n, even, res, pre, st, w, z, passes=()):
+def k_back_narrow(got, mates, d, pre_n, st_n, gain_n, even, slope, pre, st, w, z, passes=()):
     q, qo = z.q4, z.q3
 
     def body(k):
-        got_ref, mates_ref, d_ref, pn_ref, sn_ref, gn_ref, even_ref, res_ref, pre_ref, st_ref = k.i
+        got_ref, mates_ref, d_ref, pn_ref, sn_ref, gn_ref, even_ref, slope_ref, pre_ref, st_ref = k.i
         delta_ref, t_off, t_gain, d_next, pay_ref = k.o
         rows_ref, sum_ref, tmp = k.x
         back_start((got_ref, d_ref, pn_ref, sn_ref, gn_ref), mates_ref, sum_ref, delta_ref, q, z.rows, (t_off, t_gain))
@@ -757,17 +825,17 @@
             for c in range(qo):
                 tmp[some, cols(c)] = tmp[some, cols(c)] + even_ref[pl.ds(m * z.half, z.half), cols(c)]
                 d_join = tmp[at, cols(c)].astype(BF).astype(F32)
-                one = gelu_slope(res_ref[at, cols(c)]) * d_join
+                one = slope_ref[at, cols(c)].astype(F32) * d_join
                 hat = (pre_ref[at, cols(c)] - row(st_ref, m * qo + c)) * row(st_ref, (MICRO + m) * qo + c)
-                d_next[at, cols(c)] = one
+                d_next[at, cols(c)] = one.astype(BF)
                 sum_rows(one, hat, rows_ref, m * qo + c, MICRO * qo)
         fill(pay_ref, rows_ref)
 
     rows = MICRO * z.rows
     return kernel_call(
         body,
-        [arr(rows, z.c_wide, dtype=BF)] + [arr(q, LANES)] * 2 + [arr(rows, z.c_in), arr(z.n, 6 * qo, LANES, dtype=BF)],
-        [got, mates, d, pre_n, st_n, gain_n, even, res, pre, st],
+        [arr(rows, z.c_wide, dtype=BF)] + [arr(q, LANES)] * 2 + [arr(rows, z.c_in, dtype=BF), arr(z.n, 6 * qo, LANES, dtype=BF)],
+        [got, mates, d, pre_n, st_n, gain_n, even, slope, pre, st],
         [w],
         [
             pltpu.VMEM((6 * qo, LANES), F32),
@@ -856,22 +924,36 @@
     )
 
 
-def k_back_reduce(got, mates, d, pre_r, st_r, gain_r, z, passes=()):
-    q = z.q1
-
-    def body(k):
-        got_ref, mates_ref, d_ref, pr_ref, sr_ref, gr_ref = k.i
+def k_back_reduce(got, mates, d, pre_r, st_r, gain_r, maps_in, place, z, passes=()):
+    q, hi, r = z.q1, z.ns // z.slo, z.c_in // z.n
+
+    def body(k):
+        got_ref, mates_ref, d_ref, pr_ref, sr_ref, gr_ref, *maps = k.i
         delta_ref, t_off, t_gain = k.o
-        (sum_ref,) = k.x
+        sum_ref, *held = k.x
         back_start((got_ref, d_ref, pr_ref, sr_ref, gr_ref), mates_ref, sum_ref, delta_ref, q, z.rows, (t_off, t_gain))
+        k.send(0)
+        if maps:
+            (held,) = held
+            product = dot_tn(maps[0][...], delta_ref[...])
+            held[...] = product.reshape(hi, z.slo, z.nb // 2, 2, r, z.c_mid).astype(BF)
+            core = k.s[0][0] & 1
+            k.copy(held.at[:, :, :, core], k.raw[0])
+            k.copy(held.at[:, :, :, 1 - core], k.raw[1])
 
     rows = MICRO * z.rows
+    maps = [] if maps_in is None else [maps_in]
     return kernel_call(
         body,
         [arr(rows, z.c_mid, dtype=BF)] + [arr(q, LANES)] * 2,
-        [got, mates, d, pre_r, st_r, gain_r],
-        scratch=[pltpu.VMEM((6 * q, LANES), F32)],
+        [got, mates, d, pre_r, st_r, gain_r, *maps],
+        scratch=[pltpu.VMEM((6 * q, LANES), F32)]
+        + [pltpu.VMEM((hi, z.slo, z.nb // 2, 2, r, z.c_mid), BF) for _ in maps],
         passes=passes,
+        scalars=[place],
+        raw=[arr(hi, z.slo, z.nb // 2, r, z.c_mid, dtype=BF)] * (2 * len(maps)),
+        n_raw=2 * len(maps),
+        flops=2 * rows * z.c_in * z.c_mid,
     )
 
 
@@ -886,7 +968,7 @@
                     for px in range(2):
                         at = pl.ds(m * z.rows + (2 * (y % 2) + px) * z.half + (y // 2) * 8, 8)
                         line[c, pl.ds((y * MICRO + m) * z.cols + px, 8, stride=2), :] = (
-                            one_ref[at, cols(c)] + tmp[at, cols(c)]
+                            one_ref[at, cols(c)].astype(F32) + tmp[at, cols(c)]
                         )
                     out_ref[y, m, :, cols(c)] = line[c, pl.ds((y * MICRO + m) * z.cols, z.cols), :].astype(BF)
 
@@ -1172,6 +1254,7 @@
     z.c_in, z.c_mid = w_reduce.shape
     z.c_wide, z.c_out = w_widen.shape
     z.q1, z.q3, z.q4, z.q6 = (c // LANES for c in (z.c_mid, z.c_in, z.c_wide, z.c_out))
+    z.q_product = -(-MICRO * (z.q3 + 2 * z.q1) // 8) * 8
     assert features.shape[2] == 1 and cotangent.shape[1] == 1 and z.maps == z.ns and z.cols == 16
     yh, xh = z.height // 2, z.cols // 2
     n, ns, nb = z.n, z.ns, z.nb
@@ -1236,8 +1319,8 @@
     got = share(pay)
     out_spatial, pre_expand, pay, st_spatial = k_expand(got, mates[z.q1], pre_spatial, *vectors["spatial"], w_expand, z)
     got = share(pay)
-    residual_one, joined, even, pre_narrow, pay, st_expand = k_narrow(
-        got, mates[z.q3], pre_expand, *vectors["expand"], maps_in, w_narrow, z
+    slope_one, joined, even, pre_narrow, pay, st_expand = k_narrow(
+        got, mates[z.q3], same.transpose(1, 0, 2), pre_expand, *vectors["expand"], maps_in, w_expand, w_narrow, z
     )
     evens = everywhere(even, z.g)
     got = share(pay)
@@ -1281,7 +1364,7 @@
     pieces = trade(pieces)
     delta_narrow, go_narrow, gg_narrow, d_one, pay, first, *pieces = k_back_narrow(
         got, mates[z.q4], d_narrow, pre_narrow, st_narrow, vectors["narrow"][0],
-        d_even, residual_one, pre_expand, st_expand, w_narrow, z, (first, *pieces),
+        d_even, slope_one, pre_expand, st_expand, w_narrow, z, (first, *pieces),
     )
     got = share(pay)
     first = lax.psum_scatter(first, "slo", scatter_dimension=0, tiled=True)
@@ -1318,12 +1401,13 @@
                 came.append(lax.ppermute(part, ("bhi", "slo"), pairs) if i or j else part)
         return came, parts[high * z.slo :]
 
-    delta_reduce, go_reduce, gg_reduce, sent_more, came_some = k_back_reduce(
-        got, mates[z.q1], d_reduce, pre_reduce, st_reduce, vectors["reduce"][0], z, (sent_more, came_some)
+    delta_reduce, go_reduce, gg_reduce, *more = k_back_reduce(
+        got, mates[z.q1], d_reduce, pre_reduce, st_reduce, vectors["reduce"][0], maps_in if blocks else None, place, z,
+        (sent_more, came_some, where),
     )
     pairs_last, passed = [(maps_in, delta_reduce)], ()
     if blocks:
-        kept_last, sent_last = k_products(pairs_last, place, z)
+        kept_last, sent_last, sent_more, came_some, where = more
         groups = [(kept_some, came_some), (kept_more, swap(sent_more, "core", 1)), (kept_last, swap(sent_last, "core", 1))]
         passed, (early,) = over_plane(groups, (first[0], second[0]))
     else:

time: 375 us -> 363 us (0.968)
  Pallas kernels: 99.6 us -> 94.5 us
  waiting for transfers between devices: 132 us -> 127 us
    all_to_all x11, waiting for transfers between devices: 62.3 us -> 56.5 us  [share(): return lax.all_to_all(pay, ALL, 0, 0, tiled=True)]
    pallas_call x28 -> x27, Pallas kernels: 99.6 us -> 94.5 us  [kernel_call(): pl.pallas_call(run, out_shape=tuple((jax.ShapeDtypeStruct(o.shape, o.dtyp...]
    unnamed x105 -> x79, local copies, waits for them, and re-layouts: 17.5 us -> 13.5 us
  transfers between devices with their start and end apart: 46 -> 46, of which waited for: 22 -> 23; matrix products, arithmetic and copies ran while one was open for 2% -> 2% of each run, Pallas kernels for 15% -> 14%
where the time goes in v2:
time: 363 us; the launch traced here: 361 us
  waiting for transfers between devices  127 us (35%)
  Pallas kernels  94.5 us (26%)
  starting transfers between devices  69.8 us (19%)
  blocking collectives  34 us (9%)
  local copies, waits for them, and re-layouts  18.8 us (5%)
  between operations  14.4 us (4%)
    pallas_call x27, Pallas kernels, kernel_call(): pl.pallas_call(run, out_shape=tuple((jax.ShapeDtypeStruct(o.shape, o.dtyp...  94.5 us
    all_to_all x11, waiting for transfers between devices, share(): return lax.all_to_all(pay, ALL, 0, 0, tiled=True)  56.5 us
    all_to_all x11, starting transfers between devices, share(): return lax.all_to_all(pay, ALL, 0, 0, tiled=True)  36.1 us
    all_to_all x3, blocking collectives, share(): return lax.all_to_all(pay, ALL, 0, 0, tiled=True)  34 us
    ppermute x21, waiting for transfers between devices, swap(): lax.ppermute(block, axis, [(i, i ^ distance) for i in range(lax.axis_size...  20.9 us
    all_to_all x2, waiting for transfers between devices, exchange(): return lax.all_to_all(block, SPACE, 0, 0, tiled=True)  20 us
    ppermute x3, waiting for transfers between devices, over_plane(): came.append(lax.ppermute(part, ('bhi', 'slo'), pairs) if i or j else part)  18 us
    ppermute x21, starting transfers between devices, swap(): lax.ppermute(block, axis, [(i, i ^ distance) for i in range(lax.axis_size...  14.2 us
  transfers between devices with their start and end apart: 46, of which 23 were waited for; matrix products, arithmetic and copies ran while one was open for 2% of the time, Pallas kernels for 14%

profile of v2, /device:TPU:0, one launch (start us, length us, event | category | flops | bytes accessed | tf_op | source)
XLA Modules:
  0.0 361.2 jit_solution(8043539327947950103)
XLA Ops:
  9.4 7.3 %all-to-all-start = ((bf16[8,3,16,1024]{3,2,1,0:T(8,128)(2,1)}), bf16[8,3,16,1024]{3,2,1,0:T(8,128)(2,1)S(1)}, u32[]{:S(2)}, u32[]{:S(2)}) async-start(bf16[8,3,16,1024]{3,2,1,0:T(8,128)(2,1)} %bitcast.59), calls=%async_computation | async-start | bytes 1572864 | tf_op jit(solution)/shard_map/all_to_all | solution.py:1268
  16.8 20.0 %all-to-all-done.refs_1_ = bf16[8,3,16,1024]{3,2,1,0:T(8,128)(2,1)S(1)} async-done(((bf16[8,3,16,1024]{3,2,1,0:T(8,128)(2,1)}), bf16[8,3,16,1024]{3,2,1,0:T(8,128)(2,1)S(1)}, u32[]{:S(2)}, u32[]{:S(2)}) %all-to-all-start) | async-done | bytes 786464 | tf_op jit(solution)/shard_map/all_to_all | solution.py:1268
  39.6 12.1 %all_to_all.80.refs_1_ = bf16[32,24,128]{2,1,0:T(8,128)(2,1)} all-to-all(bf16[32,24,128]{2,1,0:T(8,128)(2,1)S(1)} %get-tuple-element.149), channel_id=1, replica_groups=mesh['bhi'=2,'core'=2,'shi'=4,'slo'=2] {'bhi','core','shi','slo'}, dimensions={0} | all-to-all | bytes 393216 | tf_op jit(solution)/shard_map/all_to_all | solution.py:1265
  51.7 3.8 %shard_map.408 = (bf16[384,2304]{1,0:T(8,128)(2,1)}, f32[384,256]{1,0:T(8,128)}, bf16[32,18,128]{2,1,0:T(8,128)(2,1)}, f32[12,128]{1,0:T(8,128)}, f32[32,6,128]{2,1,0:T(8,128)}) custom-call(f32[3]{0:T(128)} %copy-done.2, bf16[32,24,128]{2,1,0:T(8,128)(2,1)} %all_to_all.80.refs_1_, f32[384,256]{1,0:T(8,128)} %copy-done, f32[1,256]{1,0:T(1,128)} %bitcast.84, ...), custom_call_target="tpu_custom_call" | custom-call | flops 452984832 | bytes 4186112 | tf_op jit(solution)/shard_map/pallas_call | solution.py:135
  55.5 11.8 %all_to_all.81.refs_0_ = bf16[32,18,128]{2,1,0:T(8,128)(2,1)} all-to-all(bf16[32,18,128]{2,1,0:T(8,128)(2,1)} %get-tuple-element.151), channel_id=1, replica_groups=mesh['bhi'=2,'core'=2,'shi'=4,'slo'=2] {'bhi','core','shi','slo'}, dimensions={0} | all-to-all | bytes 294912 | tf_op jit(solution)/shard_map/all_to_all | solution.py:1265
  67.3 3.2 shard_map.409
  70.6 3.3 all-to-all-start.3
  77.7 8.4 %all-to-all-done.3.refs_0_ = bf16[32,40,128]{2,1,0:T(8,128)(2,1)} async-done(((bf16[32,40,128]{2,1,0:T(8,128)(2,1)}), bf16[32,40,128]{2,1,0:T(8,128)(2,1)}, u32[]{:S(2)}, u32[]{:S(2)}) %all-to-all-start.3) | async-done | bytes 327712 | tf_op jit(solution)/shard_map/all_to_all | solution.py:1265
  86.0 5.7 %shard_map.410 = (bf16[384,1024]{1,0:T(8,128)(2,1)}, bf16[384,1024]{1,0:T(8,128)(2,1)}, bf16[96,1024]{1,0:T(8,128)(2,1)}, f32[384,512]{1,0:T(8,128)}, bf16[32,36,128]{2,1,0:T(8,128)(2,1)}, /*index=5*/f32[48,128]{1,0:T(8,128)}) custom-call(bf16[32,40,128]{2,1,0:T(8,128)(2,1)} %all-to-all-done.3.refs_0_, f32[32,24,128]{2,1,0:T(8,128)} %broadcast_bitcast_fusion.refs_1_, ...), custom_call_target="tpu_custom_call" | custom-call | flops 402653184 | bytes 7585792 | tf_op jit(solution)/shard_map/pallas_call | solution.py:135
  95.2 11.3 %all-to-all-done.4.refs_0_ = bf16[32,36,128]{2,1,0:T(8,128)(2,1)S(1)} async-done(((bf16[32,36,128]{2,1,0:T(8,128)(2,1)}), bf16[32,36,128]{2,1,0:T(8,128)(2,1)S(1)}, u32[]{:S(2)}, u32[]{:S(2)}) %all-to-all-start.4) | async-done | bytes 294944 | tf_op jit(solution)/shard_map/all_to_all | solution.py:1265
  107.2 4.0 %shard_map.411 = (bf16[384,512]{1,0:T(8,128)(2,1)}, f32[96,512]{1,0:T(8,128)}, bf16[32,36,128]{2,1,0:T(8,128)(2,1)}, f32[24,128]{1,0:T(8,128)}) custom-call(bf16[32,36,128]{2,1,0:T(8,128)(2,1)} %copy-done.13, f32[32,12,128]{2,1,0:T(8,128)} %copy.93.refs_1_.refs_2_, f32[384,512]{1,0:T(8,128)} %get-tuple-element.157.refs_2_.refs_7_.refs_3_, ...), custom_call_target="tpu_custom_call" | custom-call | flops 452984832 | bytes 6897664 | tf_op jit(solution)/shard_map/pallas_call | solution.py:135
  114.0 3.6 shard_map.412
  117.6 8.5 %all-to-all-done.5.refs_0_ = bf16[32,36,128]{2,1,0:T(8,128)(2,1)S(1)} async-done(((bf16[32,36,128]{2,1,0:T(8,128)(2,1)}), bf16[32,36,128]{2,1,0:T(8,128)(2,1)S(1)}, u32[]{:S(2)}, u32[]{:S(2)}) %all-to-all-start.5) | async-done | bytes 294944 | tf_op jit(solution)/shard_map/all_to_all | solution.py:1265
  126.7 3.4 shard_map.413
  135.5 5.1 %all-to-all-done.6.refs_0_ = f32[32,8,128]{2,1,0:T(8,128)S(1)} async-done(((f32[32,8,128]{2,1,0:T(8,128)}), f32[32,8,128]{2,1,0:T(8,128)S(1)}, u32[]{:S(2)}, u32[]{:S(2)}) %all-to-all-start.6) | async-done | bytes 131104 | tf_op jit(solution)/shard_map/all_to_all | solution.py:1265
  141.2 10.1 %all_to_all.82.refs_0_.refs_1_ = f32[32,8,128]{2,1,0:T(8,128)} all-to-all(f32[32,8,128]{2,1,0:T(8,128)S(1)} %shard_map.414), channel_id=1, replica_groups=mesh['bhi'=2,'core'=2,'shi'=4,'slo'=2] {'bhi','core','shi','slo'}, dimensions={0} | all-to-all | bytes 262144 | tf_op jit(solution)/shard_map/all_to_all | solution.py:1265
  151.3 3.5 shard_map.415
  159.8 5.5 %all-to-all-done.8.refs_0_ = f32[32,8,128]{2,1,0:T(8,128)S(1)} async-done(((f32[32,8,128]{2,1,0:T(8,128)}), f32[32,8,128]{2,1,0:T(8,128)S(1)}, u32[]{:S(2)}, u32[]{:S(2)}) %all-to-all-start.8) | async-done | bytes 131104 | tf_op jit(solution)/shard_map/all_to_all | solution.py:1265
  171.0 4.4 %collective-permute-done.7.refs_23_ = bf16[96,512]{1,0:T(8,128)(2,1)S(1)} collective-permute-done((bf16[96,512]{1,0:T(8,128)(2,1)}, bf16[96,512]{1,0:T(8,128)(2,1)S(1)}, u32[]{:S(2)}, u32[]{:S(2)}) %collective-permute-start.7) | collective-permute-done | bytes 98336 | tf_op jit(solution)/shard_map/ppermute | solution.py:1271
  177.4 4.4 %shard_map.417 = (bf16[96,2048]{1,0:T(8,128)(2,1)}, f32[16,128]{1,0:T(8,128)}, f32[16,128]{1,0:T(8,128)}, f32[16,128]{1,0:T(8,128)}, f32[96,512]{1,0:T(8,128)}, ...) custom-call(s32[1]{0:T(128)} %bitcast.24.refs_0_, ...), custom_call_target="tpu_custom_call", output_to_operand_aliasing={{10}: (13, {}), {11}: (14, {}), {12}: (15, {}), {13}: (16, ... | custom-call | flops 201326592 | bytes 5758976 | tf_op jit(solution)/shard_map/pallas_call | solution.py:135
  181.8 5.2 %all-to-all-start.10 = ((bf16[32,24,128]{2,1,0:T(8,128)(2,1)}), bf16[32,24,128]{2,1,0:T(8,128)(2,1)S(1)}, u32[]{:S(2)}, u32[]{:S(2)}) async-start(bf16[32,24,128]{2,1,0:T(8,128)(2,1)} %get-tuple-element.171), calls=%async_computation.10 | async-start | bytes 393216 | tf_op jit(solution)/shard_map/all_to_all | solution.py:1265
  189.0 4.5 %shard_map.418.refs_16_ = f32[96,1024]{1,0:T(8,128)} custom-call(bf16[96,2048]{1,0:T(8,128)(2,1)} %get-tuple-element.178.refs_0_, bf16[1024,2048]{1,0:T(8,128)(2,1)} %refs_1_.3), custom_call_target="tpu_custom_call" | custom-call | flops 402653184 | bytes 4980736 | tf_op jit(solution)/shard_map/pallas_call | solution.py:135
  193.6 3.4 collective-permute-done.10.refs_14_
  196.9 3.5 collective-permute-done.11.refs_15_
  201.2 6.3 %shard_map.419 = (f32[4,128]{1,0:T(4,128)}, f32[4,128]{1,0:T(4,128)}, f32[384,512]{1,0:T(8,128)}, bf16[32,24,128]{2,1,0:T(8,128)(2,1)}, bf16[96,128]{1,0:T(8,128...) custom-call(s32[1]{0:T(128)} %bitcast.24.refs_0_, ...), custom_call_target="tpu_custom_call", output_to_operand_aliasing={{8}: (12, {}), {9}: (13, {}), {10}: (14, {}), {11}: (15, {}... | custom-call | flops 452984832 | bytes 7309312 | tf_op jit(solution)/shard_map/pallas_call | solution.py:135
  207.5 4.7 %all-to-all-start.11 = ((bf16[32,24,128]{2,1,0:T(8,128)(2,1)}), bf16[32,24,128]{2,1,0:T(8,128)(2,1)S(1)}, u32[]{:S(2)}, u32[]{:S(2)}) async-start(bf16[32,24,128]{2,1,0:T(8,128)(2,1)} %get-tuple-element.179), calls=%async_computation.11 | async-start | bytes 393216 | tf_op jit(solution)/shard_map/all_to_all | solution.py:1265
  214.2 3.9 %shard_map.420.refs_11_ = bf16[2,4,192,512]{3,2,1,0:T(8,128)(2,1)} custom-call(bf16[96,512]{1,0:T(8,128)(2,1)} %get-tuple-element.184.refs_0_, bf16[96,512]{1,0:T(8,128)(2,1)} %get-tuple-element.185.refs_1_, bf16[96,512]{1,0:T(8,128)(2,1)} %get-tuple-element.186.refs_2_, bf16[96,512]{1,0:T(8,128)(2,1)} %get-tuple-element.187.refs_3_, ...), custom_call_target="tpu_custom_call" | custom-call | flops 603979776 | bytes 1966080 | tf_op jit(solution)/shard_map/pallas_call | solution.py:135
  221.4 4.9 %shard_map.421 = (bf16[384,512]{1,0:T(8,128)(2,1)}, f32[4,128]{1,0:T(4,128)}, f32[4,128]{1,0:T(4,128)}, bf16[384,1024]{1,0:T(8,128)(2,1)}, bf16[32,48,128]{2,1,0...) custom-call(bf16[32,24,128]{2,1,0:T(8,128)(2,1)} %copy-done.20, ...), custom_call_target="tpu_custom_call", output_to_operand_aliasing={{5}: (11, {}), {6}: (12, {}), {7}: (13, {}), {8}: (14, {}),... | custom-call | flops 402653184 | bytes 7383040 | tf_op jit(solution)/shard_map/pallas_call | solution.py:135
  226.3 3.2 all-to-all-start.12
  229.6 4.1 %shard_map.422.refs_11_ = bf16[2,4,144,512]{3,2,1,0:T(8,128)(2,1)} custom-call(bf16[384,512]{1,0:T(8,128)(2,1)} %get-tuple-element.203.refs_0_, bf16[384,512]{1,0:T(8,128)(2,1)} %get-tuple-element.204.refs_1_, bf16[384,512]{1,0:T(8,128)(2,1)} %get-tuple-element.205.refs_2_, bf16[384,512]{1,0:T(8,128)(2,1)} %get-tuple-element.206.refs_3_, ...), custom_call_target="tpu_custom_call" | custom-call | flops 452984832 | bytes 1671168 | tf_op jit(solution)/shard_map/pallas_call | solution.py:135
  233.7 9.4 %all-to-all-done.12.refs_0_ = bf16[32,48,128]{2,1,0:T(8,128)(2,1)S(1)} async-done(((bf16[32,48,128]{2,1,0:T(8,128)(2,1)}), bf16[32,48,128]{2,1,0:T(8,128)(2,1)S(1)}, u32[]{:S(2)}, u32[]{:S(2)}) %all-to-all-start.12) | async-done | bytes 393248 | tf_op jit(solution)/shard_map/all_to_all | solution.py:1265
  243.9 4.1 %shard_map.423 = (bf16[384,1024]{1,0:T(8,128)(2,1)}, f32[8,128]{1,0:T(8,128)}, f32[8,128]{1,0:T(8,128)}, f32[384,256]{1,0:T(8,128)}, bf16[32,12,128]{2,1,0:T(8,128)(2,1)}, /*index=5*/bf16[2,4,144,512]{3,2,1,0:T(8,128)(2,1)}) custom-call(bf16[32,48,128]{2,1,0:T(8,128)(2,1)} %copy-done.11, ...), custom_call_target="tpu_custom_call", output_to_operand_aliasing={{5}: (11, {})} | custom-call | flops 201326592 | bytes 5386240 | tf_op jit(solution)/shard_map/pallas_call | solution.py:135
  248.0 2.9 all-to-all-start.13
  252.6 3.8 %shard_map.424 = (bf16[4,2,2,96,256]{4,3,2,1,0:T(8,128)(2,1)}, bf16[4,2,2,96,256]{4,3,2,1,0:T(8,128)(2,1)}) custom-call(s32[1]{0:T(128)} %bitcast.24.refs_0_, bf16[384,1024]{1,0:T(8,128)(2,1)} %get-tuple-element.214.refs_1_, bf16[384,512]{1,0:T(8,128)(2,1)} %get-tuple-element.215.refs_2_, bf16[384,256]{1,0:T(8,128)(2,1)} %get-tuple-element.216.refs_3_, ...), custom_call_target="tpu_custom_call" | custom-call | flops 603979776 | bytes 2162688 | tf_op jit(solution)/shard_map/pallas_call | solution.py:135
  259.1 3.6 shard_map.425
  262.9 3.6 all-to-all-start.14
  267.2 3.3 shard_map.426
  270.5 3.7 %all-to-all-done.14.refs_1_ = bf16[32,12,128]{2,1,0:T(8,128)(2,1)S(1)} async-done(((bf16[32,12,128]{2,1,0:T(8,128)(2,1)}), bf16[32,12,128]{2,1,0:T(8,128)(2,1)S(1)}, u32[]{:S(2)}, u32[]{:S(2)}) %all-to-all-start.14) | async-done | bytes 98336 | tf_op jit(solution)/shard_map/all_to_all | solution.py:1265
  275.2 3.0 shard_map.427
  281.7 4.7 %shard_map.428 = (bf16[4,200,256]{2,1,0:T(8,128)(2,1)}, bf16[4,200,256]{2,1,0:T(8,128)(2,1)}, bf16[4,200,256]{2,1,0:T(8,128)(2,1)}, bf16[4,200,256]{2,1,0:T(8,128)(2,1)}, bf16[4,336,512]{2,1,0:T(8,128)(2,1)}) custom-call(s32[3]{0:T(128)} %get-tuple-element.227.refs_0_, bf16[4,2,2,96,256]{4,3,2,1,0:T(8,128)(2,1)} %get-tuple-element.228.refs_1_, ...), custom_call_target="tpu_custom_call" | custom-call | bytes 4653056 | tf_op jit(solution)/shard_map/pallas_call | solution.py:135
  290.0 9.0 %collective-permute-done.18.refs_4_ = bf16[4,200,256]{2,1,0:T(8,128)(2,1)S(1)} collective-permute-done((bf16[4,200,256]{2,1,0:T(8,128)(2,1)}, bf16[4,200,256]{2,1,0:T(8,128)(2,1)S(1)}, u32[]{:S(2)}, u32[]{:S(2)}) %collective-permute-start.18) | collective-permute-done | bytes 409632 | tf_op jit(solution)/shard_map/ppermute | solution.py:1401
  299.1 8.9 %collective-permute-done.19.refs_5_ = bf16[4,200,256]{2,1,0:T(8,128)(2,1)S(1)} collective-permute-done((bf16[4,200,256]{2,1,0:T(8,128)(2,1)}, bf16[4,200,256]{2,1,0:T(8,128)(2,1)S(1)}, u32[]{:S(2)}, u32[]{:S(2)}) %collective-permute-start.19) | collective-permute-done | bytes 409632 | tf_op jit(solution)/shard_map/ppermute | solution.py:1401
  311.5 4.5 %all-to-all-start.15 = ((bf16[8,3,16,1024]{3,2,1,0:T(8,128)(2,1)}), bf16[8,3,16,1024]{3,2,1,0:T(8,128)(2,1)S(1)}, u32[]{:S(2)}, u32[]{:S(2)}) async-start(bf16[8,3,16,1024]{3,2,1,0:T(8,128)(2,1)} %get-tuple-element.240), calls=%async_computation.17 | async-start | bytes 1572864 | tf_op jit(solution)/shard_map/all_to_all | solution.py:1268
  318.8 3.0 shard_map.430
  323.5 8.3 %collective-permute-done.25.refs_3_ = bf16[336,512]{1,0:T(8,128)(2,1)S(1)} collective-permute-done((bf16[336,512]{1,0:T(8,128)(2,1)}, bf16[336,512]{1,0:T(8,128)(2,1)S(1)}, u32[]{:S(2)}, u32[]{:S(2)}) %collective-permute-start.25) | collective-permute-done | bytes 344096 | tf_op jit(solution)/shard_map/ppermute | solution.py:1271
  336.9 3.2 shard_map.431
  340.1 3.7 %collective-permute-done.22.refs_2_ = bf16[200,256]{1,0:T(8,128)(2,1)} collective-permute-done((bf16[200,256]{1,0:T(8,128)(2,1)}, bf16[200,256]{1,0:T(8,128)(2,1)}, u32[]{:S(2)}, u32[]{:S(2)}) %collective-permute-start.22) | collective-permute-done | bytes 102432 | tf_op jit(solution)/shard_map/ppermute | solution.py:1271
  347.2 3.4 collective-permute-done.28.refs_3_
  (171 shorter events, 77.5 us)
Async XLA Ops:
  7.2 29.6 %copy-start.1 = (bf16[1024,256]{1,0:T(8,128)(2,1)S(1)}, bf16[1024,256]{1,0:T(8,128)(2,1)}, u32[]{:S(2)}) copy-start(bf16[1024,256]{1,0:T(8,128)(2,1)} %refs_2_.3) | copy-start | bytes 1572868
  9.4 27.4 %all-to-all-start = ((bf16[8,3,16,1024]{3,2,1,0:T(8,128)(2,1)}), bf16[8,3,16,1024]{3,2,1,0:T(8,128)(2,1)S(1)}, u32[]{:S(2)}, u32[]{:S(2)}) async-start(bf16[8,3,16,1024]{3,2,1,0:T(8,128)(2,1)} %bitcast.59), calls=%async_computation | async-start | bytes 1572864 | tf_op jit(solution)/shard_map/all_to_all | solution.py:1268
  16.8 34.9 %copy-start.2 = (f32[3]{0:T(128)}, f32[3]{0:T(128)S(1)}, u32[]{:S(2)}) copy-start(f32[3]{0:T(128)S(1)} %convert_reduce_fusion.refs_0_) | copy-start | bytes 40
  70.6 15.5 %all-to-all-start.3 = ((bf16[32,40,128]{2,1,0:T(8,128)(2,1)}), bf16[32,40,128]{2,1,0:T(8,128)(2,1)}, u32[]{:S(2)}, u32[]{:S(2)}) async-start(bf16[32,40,128]{2,1,0:T(8,128)(2,1)} %get-tuple-element.154), calls=%async_computation.3 | async-start | bytes 655360 | tf_op jit(solution)/shard_map/all_to_all | solution.py:1265
  91.8 14.8 %all-to-all-start.4 = ((bf16[32,36,128]{2,1,0:T(8,128)(2,1)}), bf16[32,36,128]{2,1,0:T(8,128)(2,1)S(1)}, u32[]{:S(2)}, u32[]{:S(2)}) async-start(bf16[32,36,128]{2,1,0:T(8,128)(2,1)} %get-tuple-element.156), calls=%async_computation.4 | async-start | bytes 655360 | tf_op jit(solution)/shard_map/all_to_all | solution.py:1265
  111.3 14.8 %all-to-all-start.5 = ((bf16[32,36,128]{2,1,0:T(8,128)(2,1)}), bf16[32,36,128]{2,1,0:T(8,128)(2,1)S(1)}, u32[]{:S(2)}, u32[]{:S(2)}) async-start(bf16[32,36,128]{2,1,0:T(8,128)(2,1)} %get-tuple-element.158), calls=%async_computation.5 | async-start | bytes 655360 | tf_op jit(solution)/shard_map/all_to_all | solution.py:1265
  130.2 10.3 %all-to-all-start.6 = ((f32[32,8,128]{2,1,0:T(8,128)}), f32[32,8,128]{2,1,0:T(8,128)S(1)}, u32[]{:S(2)}, u32[]{:S(2)}) async-start(f32[32,8,128]{2,1,0:T(8,128)} %get-tuple-element.162), calls=%async_computation.6 | async-start | bytes 262144 | tf_op jit(solution)/shard_map/all_to_all | solution.py:1265
  133.7 25.7 %collective-permute-start.1 = (bf16[384,512]{1,0:T(8,128)(2,1)S(1)}, bf16[384,512]{1,0:T(8,128)(2,1)}, u32[]{:S(2)}, u32[]{:S(2)}) collective-permute-start(bf16[384,512]{1,0:T(8,128)(2,1)S(1)} %copy-done.9), channel_id=1, source_target_pairs={{0,16},{16,0},{1,17},{17,1},{2,18},{18,2},{3,19},{19,3},{4,20},{20... | collective-permute-start | bytes 1179656 | tf_op jit(solution)/shard_map/ppermute | solution.py:1271
  154.8 10.5 %all-to-all-start.8 = ((f32[32,8,128]{2,1,0:T(8,128)}), f32[32,8,128]{2,1,0:T(8,128)S(1)}, u32[]{:S(2)}, u32[]{:S(2)}) async-start(f32[32,8,128]{2,1,0:T(8,128)} %get-tuple-element.166), calls=%async_computation.8 | async-start | bytes 262144 | tf_op jit(solution)/shard_map/all_to_all | solution.py:1265
  157.6 11.4 %collective-permute-start.4 = (bf16[96,1024]{1,0:T(8,128)(2,1)S(1)}, bf16[96,1024]{1,0:T(8,128)(2,1)S(1)}, u32[]{:S(2)}, u32[]{:S(2)}) collective-permute-start(bf16[96,1024]{1,0:T(8,128)(2,1)S(1)} %copy-done.6), channel_id=1, source_target_pairs={{0,16},{16,0},{1,17},{17,1},{2,18},{18,2},{3,19},{19,3},{4,20},{20... | collective-permute-start | bytes 589832 | tf_op jit(solution)/shard_map/ppermute | solution.py:1271
  159.3 16.1 %collective-permute-start = (bf16[384,512]{1,0:T(8,128)(2,1)S(1)}, bf16[384,512]{1,0:T(8,128)(2,1)S(1)}, u32[]{:S(2)}, u32[]{:S(2)}) collective-permute-start(bf16[384,512]{1,0:T(8,128)(2,1)S(1)} %copy-done.9), channel_id=1, source_target_pairs={{0,8},{8,0},{1,9},{9,1},{2,10},{10,2},{3,11},{11,3},{4,12},{12,4},... | collective-permute-start | bytes 1179656 | tf_op jit(solution)/shard_map/ppermute | solution.py:1271
  159.3 17.4 %collective-permute-start.2 = (bf16[384,512]{1,0:T(8,128)(2,1)}, bf16[384,512]{1,0:T(8,128)(2,1)}, u32[]{:S(2)}, u32[]{:S(2)}) collective-permute-start(bf16[384,512]{1,0:T(8,128)(2,1)} %collective-permute-done.1.refs_15_), channel_id=1, source_target_pairs={{0,8},{8,0},{1,9},{9,1},{2,10},{10,2},{3,11},{11,3},{4,12},{12,4},... | collective-permute-start | bytes 1179656 | tf_op jit(solution)/shard_map/ppermute | solution.py:1271
  159.8 11.1 %collective-permute-start.3 = (bf16[96,1024]{1,0:T(8,128)(2,1)S(1)}, bf16[96,1024]{1,0:T(8,128)(2,1)S(1)}, u32[]{:S(2)}, u32[]{:S(2)}) collective-permute-start(bf16[96,1024]{1,0:T(8,128)(2,1)S(1)} %copy-done.6), channel_id=1, source_target_pairs={{0,8},{8,0},{1,9},{9,1},{2,10},{10,2},{3,11},{11,3},{4,12},{12,4},... | collective-permute-start | bytes 589832 | tf_op jit(solution)/shard_map/ppermute | solution.py:1271
  166.4 10.3 %all-to-all-start.9 = ((f32[32,8,128]{2,1,0:T(8,128)}), f32[32,8,128]{2,1,0:T(8,128)S(1)}, u32[]{:S(2)}, u32[]{:S(2)}) async-start(f32[32,8,128]{2,1,0:T(8,128)} %shard_map.416), calls=%async_computation.9 | async-start | bytes 262144 | tf_op jit(solution)/shard_map/all_to_all | solution.py:1265
  169.0 6.4 %collective-permute-start.5 = (bf16[96,1024]{1,0:T(8,128)(2,1)S(1)}, bf16[96,1024]{1,0:T(8,128)(2,1)S(1)}, u32[]{:S(2)}, u32[]{:S(2)}) collective-permute-start(bf16[96,1024]{1,0:T(8,128)(2,1)S(1)} %collective-permute-done.4.refs_19_), channel_id=1, source_target_pairs={{0,8},{8,0},{1,9},{9,1},{2,10},{10,2},{3,11},{11,3},{4,12},{12,4},... | collective-permute-start | bytes 589832 | tf_op jit(solution)/shard_map/ppermute | solution.py:1271
  169.2 6.2 %collective-permute-start.7 = (bf16[96,512]{1,0:T(8,128)(2,1)}, bf16[96,512]{1,0:T(8,128)(2,1)S(1)}, u32[]{:S(2)}, u32[]{:S(2)}) collective-permute-start(bf16[96,512]{1,0:T(8,128)(2,1)} %get-tuple-element.170.refs_21_), channel_id=1, source_target_pairs={{0,16},{16,0},{1,17},{17,1},{2,18},{18,2},{3,19},{19,3},{4,20},{20... | collective-permute-start | bytes 294920 | tf_op jit(solution)/shard_map/ppermute | solution.py:1271
  170.9 5.4 %collective-permute-start.6 = (bf16[96,512]{1,0:T(8,128)(2,1)}, bf16[96,512]{1,0:T(8,128)(2,1)S(1)}, u32[]{:S(2)}, u32[]{:S(2)}) collective-permute-start(bf16[96,512]{1,0:T(8,128)(2,1)} %get-tuple-element.170.refs_21_), channel_id=1, source_target_pairs={{0,8},{8,0},{1,9},{9,1},{2,10},{10,2},{3,11},{11,3},{4,12},{12,4},... | collective-permute-start | bytes 294920 | tf_op jit(solution)/shard_map/ppermute | solution.py:1271
  175.4 1.3 collective-permute-start.8
  181.8 18.7 %all-to-all-start.10 = ((bf16[32,24,128]{2,1,0:T(8,128)(2,1)}), bf16[32,24,128]{2,1,0:T(8,128)(2,1)S(1)}, u32[]{:S(2)}, u32[]{:S(2)}) async-start(bf16[32,24,128]{2,1,0:T(8,128)(2,1)} %get-tuple-element.171), calls=%async_computation.10 | async-start | bytes 393216 | tf_op jit(solution)/shard_map/all_to_all | solution.py:1265
  187.0 6.5 %collective-permute-start.9 = (bf16[96,1024]{1,0:T(8,128)(2,1)}, bf16[96,1024]{1,0:T(8,128)(2,1)S(1)}, u32[]{:S(2)}, u32[]{:S(2)}) collective-permute-start(bf16[96,1024]{1,0:T(8,128)(2,1)} %get-tuple-element.175), channel_id=1, source_target_pairs={{0,8},{8,0},{16,24},{24,16},{1,9},{9,1},{17,25},{25,17},{2,10},{10... | collective-permute-start | bytes 589832 | tf_op jit(solution)/shard_map/ppermute | solution.py:1275
  187.3 9.6 %collective-permute-start.10 = (bf16[96,1024]{1,0:T(8,128)(2,1)}, bf16[96,1024]{1,0:T(8,128)(2,1)S(1)}, u32[]{:S(2)}, u32[]{:S(2)}) collective-permute-start(bf16[96,1024]{1,0:T(8,128)(2,1)} %get-tuple-element.176), channel_id=1, source_target_pairs={{0,16},{8,24},{16,0},{24,8},{1,17},{9,25},{17,1},{25,9},{2,18},{10... | collective-permute-start | bytes 589832 | tf_op jit(solution)/shard_map/ppermute | solution.py:1275
  189.0 11.5 %collective-permute-start.11 = (bf16[96,1024]{1,0:T(8,128)(2,1)}, bf16[96,1024]{1,0:T(8,128)(2,1)S(1)}, u32[]{:S(2)}, u32[]{:S(2)}) collective-permute-start(bf16[96,1024]{1,0:T(8,128)(2,1)} %get-tuple-element.177), channel_id=1, source_target_pairs={{0,24},{8,16},{16,8},{24,0},{1,25},{9,17},{17,9},{25,1},{2,26},{10... | collective-permute-start | bytes 589832 | tf_op jit(solution)/shard_map/ppermute | solution.py:1275
  207.5 13.2 %all-to-all-start.11 = ((bf16[32,24,128]{2,1,0:T(8,128)(2,1)}), bf16[32,24,128]{2,1,0:T(8,128)(2,1)S(1)}, u32[]{:S(2)}, u32[]{:S(2)}) async-start(bf16[32,24,128]{2,1,0:T(8,128)(2,1)} %get-tuple-element.179), calls=%async_computation.11 | async-start | bytes 393216 | tf_op jit(solution)/shard_map/all_to_all | solution.py:1265
  212.2 46.3 %reduce-scatter.4.cloned.1.call-start = ((), (), s32[]{:S(2)}) async-start(), calls=%async_computation.19 | async-start | bytes 2359296 | tf_op jit(solution)/shard_map/reduce_scatter | solution.py:1370
  212.2 5.9 %collective-permute-start.12 = (bf16[96,128]{1,0:T(8,128)(2,1)}, bf16[96,128]{1,0:T(8,128)(2,1)S(1)}, u32[]{:S(2)}, u32[]{:S(2)}) collective-permute-start(bf16[96,128]{1,0:T(8,128)(2,1)} %get-tuple-element.197), channel_id=1, source_target_pairs={{0,8},{8,0},{16,24},{24,16},{1,9},{9,1},{17,25},{25,17},{2,10},{10... | collective-permute-start | bytes 73736 | tf_op jit(solution)/shard_map/ppermute | solution.py:1275
  212.5 5.6 %collective-permute-start.13 = (bf16[96,128]{1,0:T(8,128)(2,1)}, bf16[96,128]{1,0:T(8,128)(2,1)S(1)}, u32[]{:S(2)}, u32[]{:S(2)}) collective-permute-start(bf16[96,128]{1,0:T(8,128)(2,1)} %get-tuple-element.198), channel_id=1, source_target_pairs={{0,16},{8,24},{16,0},{24,8},{1,17},{9,25},{17,1},{25,9},{2,18},{10... | collective-permute-start | bytes 73736 | tf_op jit(solution)/shard_map/ppermute | solution.py:1275
  214.2 3.9 %collective-permute-start.14 = (bf16[96,128]{1,0:T(8,128)(2,1)}, bf16[96,128]{1,0:T(8,128)(2,1)S(1)}, u32[]{:S(2)}, u32[]{:S(2)}) collective-permute-start(bf16[96,128]{1,0:T(8,128)(2,1)} %get-tuple-element.199), channel_id=1, source_target_pairs={{0,24},{8,16},{16,8},{24,0},{1,25},{9,17},{17,9},{25,1},{2,26},{10... | collective-permute-start | bytes 73736 | tf_op jit(solution)/shard_map/ppermute | solution.py:1275
  226.3 16.8 %all-to-all-start.12 = ((bf16[32,48,128]{2,1,0:T(8,128)(2,1)}), bf16[32,48,128]{2,1,0:T(8,128)(2,1)S(1)}, u32[]{:S(2)}, u32[]{:S(2)}) async-start(bf16[32,48,128]{2,1,0:T(8,128)(2,1)} %get-tuple-element.200), calls=%async_computation.12 | async-start | bytes 786432 | tf_op jit(solution)/shard_map/all_to_all | solution.py:1265
  229.6 51.2 %reduce-scatter.6.cloned.1.call-start = ((), (), s32[]{:S(2)}) async-start(), calls=%async_computation.20 | async-start | bytes 1769472 | tf_op jit(solution)/shard_map/reduce_scatter | solution.py:1378
  248.0 10.5 %all-to-all-start.13 = ((bf16[32,12,128]{2,1,0:T(8,128)(2,1)}), bf16[32,12,128]{2,1,0:T(8,128)(2,1)S(1)}, u32[]{:S(2)}, u32[]{:S(2)}) async-start(bf16[32,12,128]{2,1,0:T(8,128)(2,1)} %get-tuple-element.211), calls=%async_computation.13 | async-start | bytes 262144 | tf_op jit(solution)/shard_map/all_to_all | solution.py:1265
  262.7 11.5 %collective-permute-start.15 = (bf16[4,2,2,96,256]{4,3,2,1,0:T(8,128)(2,1)}, bf16[4,2,2,96,256]{4,3,2,1,0:T(8,128)(2,1)S(1)}, u32[]{:S(2)}, u32[]{:S(2)}) collective-permute-start(bf16[4,2,2,96,256]{4,3,2,1,0:T(8,128)(2,1)} %get-tuple-element.225), channel_id=1, source_target_pairs={{0,8},{8,0},{1,9},{9,1},{2,10},{10,2},{3,11},{11,3},{4,12},{12,4},... | collective-permute-start | bytes 2359304 | tf_op jit(solution)/shard_map/ppermute | solution.py:1271
  262.9 11.4 %all-to-all-start.14 = ((bf16[32,12,128]{2,1,0:T(8,128)(2,1)}), bf16[32,12,128]{2,1,0:T(8,128)(2,1)S(1)}, u32[]{:S(2)}, u32[]{:S(2)}) async-start(bf16[32,12,128]{2,1,0:T(8,128)(2,1)} %get-tuple-element.220), calls=%async_computation.15 | async-start | bytes 262144 | tf_op jit(solution)/shard_map/all_to_all | solution.py:1265
  266.5 52.3 %reduce-scatter.8.cloned.1.call-start = ((), (), s32[]{:S(2)}) async-start(), calls=%async_computation.21 | async-start | bytes 1720320 | tf_op jit(solution)/shard_map/reduce_scatter | solution.py:1417
  278.2 2.7 collective-permute-start.16
  278.4 2.5 collective-permute-start.17
  286.5 12.6 %collective-permute-start.18 = (bf16[4,200,256]{2,1,0:T(8,128)(2,1)}, bf16[4,200,256]{2,1,0:T(8,128)(2,1)S(1)}, u32[]{:S(2)}, u32[]{:S(2)}) collective-permute-start(bf16[4,200,256]{2,1,0:T(8,128)(2,1)} %get-tuple-element.237), channel_id=1, source_target_pairs={{0,1},{1,0},{16,17},{17,16},{2,3},{3,2},{18,19},{19,18},{4,5},{5,4... | collective-permute-start | bytes 1228808 | tf_op jit(solution)/shard_map/ppermute | solution.py:1401
  287.8 20.2 %collective-permute-start.19 = (bf16[4,200,256]{2,1,0:T(8,128)(2,1)}, bf16[4,200,256]{2,1,0:T(8,128)(2,1)S(1)}, u32[]{:S(2)}, u32[]{:S(2)}) collective-permute-start(bf16[4,200,256]{2,1,0:T(8,128)(2,1)} %get-tuple-element.238), channel_id=1, source_target_pairs={{0,16},{1,17},{16,0},{17,1},{2,18},{3,19},{18,2},{19,3},{4,20},{5,... | collective-permute-start | bytes 1228808 | tf_op jit(solution)/shard_map/ppermute | solution.py:1401
  288.5 19.5 %collective-permute-start.20 = (bf16[4,200,256]{2,1,0:T(8,128)(2,1)}, bf16[4,200,256]{2,1,0:T(8,128)(2,1)}, u32[]{:S(2)}, u32[]{:S(2)}) collective-permute-start(bf16[4,200,256]{2,1,0:T(8,128)(2,1)} %get-tuple-element.239), channel_id=1, source_target_pairs={{0,17},{1,16},{16,1},{17,0},{2,19},{3,18},{18,3},{19,2},{4,21},{5,... | collective-permute-start | bytes 1228808 | tf_op jit(solution)/shard_map/ppermute | solution.py:1401
  311.5 39.1 %all-to-all-start.15 = ((bf16[8,3,16,1024]{3,2,1,0:T(8,128)(2,1)}), bf16[8,3,16,1024]{3,2,1,0:T(8,128)(2,1)S(1)}, u32[]{:S(2)}, u32[]{:S(2)}) async-start(bf16[8,3,16,1024]{3,2,1,0:T(8,128)(2,1)} %get-tuple-element.240), calls=%async_computation.17 | async-start | bytes 1572864 | tf_op jit(solution)/shard_map/all_to_all | solution.py:1268
  321.9 9.9 %collective-permute-start.25 = (bf16[336,512]{1,0:T(8,128)(2,1)}, bf16[336,512]{1,0:T(8,128)(2,1)S(1)}, u32[]{:S(2)}, u32[]{:S(2)}) collective-permute-start(bf16[336,512]{1,0:T(8,128)(2,1)} %bitcast.66), channel_id=1, source_target_pairs={{0,16},{16,0},{1,17},{17,1},{2,18},{18,2},{3,19},{19,3},{4,20},{20... | collective-permute-start | bytes 1032200 | tf_op jit(solution)/shard_map/ppermute | solution.py:1271
  323.5 13.4 %collective-permute-start.24 = (bf16[336,512]{1,0:T(8,128)(2,1)}, bf16[336,512]{1,0:T(8,128)(2,1)}, u32[]{:S(2)}, u32[]{:S(2)}) collective-permute-start(bf16[336,512]{1,0:T(8,128)(2,1)} %bitcast.67), channel_id=1, source_target_pairs={{0,8},{8,0},{1,9},{9,1},{2,10},{10,2},{3,11},{11,3},{4,12},{12,4},... | collective-permute-start | bytes 1032200 | tf_op jit(solution)/shard_map/ppermute | solution.py:1271
  332.5 4.4 %collective-permute-start.26 = (bf16[336,512]{1,0:T(8,128)(2,1)S(1)}, bf16[336,512]{1,0:T(8,128)(2,1)}, u32[]{:S(2)}, u32[]{:S(2)}) collective-permute-start(bf16[336,512]{1,0:T(8,128)(2,1)S(1)} %collective-permute-done.25.refs_3_), channel_id=1, source_target_pairs={{0,8},{8,0},{1,9},{9,1},{2,10},{10,2},{3,11},{11,3},{4,12},{12,4},... | collective-permute-start | bytes 1032200 | tf_op jit(solution)/shard_map/ppermute | solution.py:1271
  332.5 7.6 %collective-permute-start.21 = (bf16[200,256]{1,0:T(8,128)(2,1)}, bf16[200,256]{1,0:T(8,128)(2,1)S(1)}, u32[]{:S(2)}, u32[]{:S(2)}) collective-permute-start(bf16[200,256]{1,0:T(8,128)(2,1)} %get-tuple-element.247), channel_id=1, source_target_pairs={{0,2},{2,0},{4,6},{6,4},{1,3},{3,1},{5,7},{7,5},{8,10},{10,8},{12,... | collective-permute-start | bytes 307208 | tf_op jit(solution)/shard_map/ppermute | solution.py:1271
  332.5 11.3 %collective-permute-start.22 = (bf16[200,256]{1,0:T(8,128)(2,1)}, bf16[200,256]{1,0:T(8,128)(2,1)}, u32[]{:S(2)}, u32[]{:S(2)}) collective-permute-start(bf16[200,256]{1,0:T(8,128)(2,1)} %get-tuple-element.248), channel_id=1, source_target_pairs={{0,4},{2,6},{4,0},{6,2},{1,5},{3,7},{5,1},{7,3},{8,12},{10,14},{12... | collective-permute-start | bytes 307208 | tf_op jit(solution)/shard_map/ppermute | solution.py:1271
  334.6 9.2 %collective-permute-start.23 = (bf16[200,256]{1,0:T(8,128)(2,1)}, bf16[200,256]{1,0:T(8,128)(2,1)}, u32[]{:S(2)}, u32[]{:S(2)}) collective-permute-start(bf16[200,256]{1,0:T(8,128)(2,1)} %get-tuple-element.249), channel_id=1, source_target_pairs={{0,6},{2,4},{4,2},{6,0},{1,7},{3,5},{5,3},{7,1},{8,14},{10,12},{12... | collective-permute-start | bytes 307208 | tf_op jit(solution)/shard_map/ppermute | solution.py:1271
  345.6 4.9 %collective-permute-start.28 = (bf16[200,256]{1,0:T(8,128)(2,1)}, bf16[200,256]{1,0:T(8,128)(2,1)S(1)}, u32[]{:S(2)}, u32[]{:S(2)}) collective-permute-start(bf16[200,256]{1,0:T(8,128)(2,1)} %get-tuple-element.254.refs_1_), channel_id=1, source_target_pairs={{0,16},{16,0},{1,17},{17,1},{2,18},{18,2},{3,19},{19,3},{4,20},{20... | collective-permute-start | bytes 307208 | tf_op jit(solution)/shard_map/ppermute | solution.py:1271
  347.2 4.4 %collective-permute-start.27 = (bf16[200,256]{1,0:T(8,128)(2,1)}, bf16[200,256]{1,0:T(8,128)(2,1)}, u32[]{:S(2)}, u32[]{:S(2)}) collective-permute-start(bf16[200,256]{1,0:T(8,128)(2,1)} %get-tuple-element.254.refs_1_), channel_id=1, source_target_pairs={{0,8},{8,0},{1,9},{9,1},{2,10},{10,2},{3,11},{11,3},{4,12},{12,4},... | collective-permute-start | bytes 307208 | tf_op jit(solution)/shard_map/ppermute | solution.py:1271
  350.6 1.4 collective-permute-start.29
  (36 other events, 112.6 us)
Sparse Core Ops, SparseCore 0:
  226.4 28.3 reduce-scatter.3
  257.7 23.0 reduce-scatter.5
  286.6 32.1 reduce-scatter.7

commit v3 on v2

--- a/solution.py
+++ b/solution.py
@@ -320,7 +320,7 @@
         [pltpu.VMEM((q, rows, LANES), F32), pltpu.VMEM((pad, LANES), F32)],
         flops=2 * rows * z.c_in * z.c_mid,
         scalars=[ids],
-        limit=24,
+        limit=16,
     )
 
 
@@ -683,12 +683,13 @@
 
     def body(k):
         st2, sum_ref, d_ref, w_ref, s_ref, gw, gs, pre_ref, st_ref, g_ref, o_ref = k.i
-        ds_ref, t_off, t_gw, t_gs, d_next, pay_ref = k.o
+        ds_ref, t_off, t_gw, t_gs, t_again, d_next, pay_ref = k.o
         dw_ref, rows_ref, tmp = k.x
         scale = 1.0 / (z.n // NVIEW * z.half)
         for c in range(n_c):
             first, second = sum_ref.at[c], sum_ref.at[n_c + c]
             t_off[pl.ds(c, 1), :] = row(first, 2 * MICRO)
+            t_again[pl.ds(c, 1), :] = row(first, 2 * MICRO)
             t_gw[pl.ds(c, 1), :] = row(first, 2 * MICRO + 1)
             t_gs[pl.ds(c, 1), :] = row(second, 2 * MICRO)
             sw, ss = st2.at[c], st2.at[n_c + c]
@@ -720,7 +721,7 @@
     return kernel_call(
         body,
         [arr(rows, z.c_out, dtype=BF)]
-        + [arr(n_c, LANES)] * 3
+        + [arr(n_c, LANES)] * 4
         + [arr(rows, z.c_wide), arr(z.n, 6 * q, LANES, dtype=BF)],
         [whole, sums, d_two, pre_w, pre_s, gain_w, gain_s, pre, st, gain, offset],
         [w],
@@ -1186,6 +1187,7 @@
         list(pieces),
         scratch=[pltpu.VMEM((n, total, 256), BF)],
         scalars=[place],
+        limit=24,
         passes=passes,
     )
 
@@ -1213,6 +1215,7 @@
         list(pieces),
         scratch=[pltpu.VMEM((n, a + b + d, some), BF)],
         scalars=[place],
+        limit=24,
     )
 
 
@@ -1345,7 +1348,7 @@
     )
 
     sums = share(k_view_sums(share(pay), id_rows, z))
-    delta_shortcut, go_widen, gg_widen, gg_shortcut, d_stride, pay, *more = k_back_widen(
+    delta_shortcut, go_widen, gg_widen, gg_shortcut, go_shortcut, d_stride, pay, *more = k_back_widen(
         whole, sums, d_two, pre_widen, pre_shortcut, vectors["widen"][0], vectors["shortcut"][0],
         pre_stride, st_stride, *vectors["stride"], place, w_widen, z, (*outs_narrow, *evens, *outs_stride),
     )
@@ -1457,7 +1460,7 @@
         flat(gg_widen),
         flat(go_widen),
         flat(gg_shortcut),
-        flat(go_widen),
+        flat(go_shortcut),
     )
 
 

time: 363 us -> 361 us (level)
    unnamed x79 -> x76, local copies, waits for them, and re-layouts: 13.5 us -> 13.1 us
  transfers between devices with their start and end apart: 46 -> 46, of which waited for: 23 -> 22; matrix products, arithmetic and copies ran while one was open for 2% -> 2% of each run, Pallas kernels for 14% -> 14%
where the time goes in v3:
time: 361 us; the launch traced here: 359 us
  waiting for transfers between devices  127 us (35%)
  Pallas kernels  93.1 us (26%)
  starting transfers between devices  69.7 us (19%)
  blocking collectives  34 us (9%)
  local copies, waits for them, and re-layouts  18.4 us (5%)
  between operations  14.4 us (4%)
    pallas_call x27, Pallas kernels, kernel_call(): pl.pallas_call(run, out_shape=tuple((jax.ShapeDtypeStruct(o.shape, o.dtyp...  93.1 us
    all_to_all x11, waiting for transfers between devices, share(): return lax.all_to_all(pay, ALL, 0, 0, tiled=True)  56.6 us
    all_to_all x11, starting transfers between devices, share(): return lax.all_to_all(pay, ALL, 0, 0, tiled=True)  36.1 us
    all_to_all x3, blocking collectives, share(): return lax.all_to_all(pay, ALL, 0, 0, tiled=True)  34 us
    ppermute x21, waiting for transfers between devices, swap(): lax.ppermute(block, axis, [(i, i ^ distance) for i in range(lax.axis_size...  20.6 us
    all_to_all x2, waiting for transfers between devices, exchange(): return lax.all_to_all(block, SPACE, 0, 0, tiled=True)  20 us
    ppermute x3, waiting for transfers between devices, over_plane(): came.append(lax.ppermute(part, ('bhi', 'slo'), pairs) if i or j else part)  18 us
    ppermute x21, starting transfers between devices, swap(): lax.ppermute(block, axis, [(i, i ^ distance) for i in range(lax.axis_size...  14.1 us
  transfers between devices with their start and end apart: 46, of which 22 were waited for; matrix products, arithmetic and copies ran while one was open for 2% of the time, Pallas kernels for 14%

profile of v3, /device:TPU:0, one launch (start us, length us, event | category | flops | bytes accessed | tf_op | source)
XLA Modules:
  0.0 359.3 jit_solution(17733890781131589647)
XLA Ops:
  9.4 7.3 %all-to-all-start = ((bf16[8,3,16,1024]{3,2,1,0:T(8,128)(2,1)}), bf16[8,3,16,1024]{3,2,1,0:T(8,128)(2,1)S(1)}, u32[]{:S(2)}, u32[]{:S(2)}) async-start(bf16[8,3,16,1024]{3,2,1,0:T(8,128)(2,1)} %bitcast.60), calls=%async_computation | async-start | bytes 1572864 | tf_op jit(solution)/shard_map/all_to_all | solution.py:1271
  16.8 20.0 %all-to-all-done.refs_1_ = bf16[8,3,16,1024]{3,2,1,0:T(8,128)(2,1)S(1)} async-done(((bf16[8,3,16,1024]{3,2,1,0:T(8,128)(2,1)}), bf16[8,3,16,1024]{3,2,1,0:T(8,128)(2,1)S(1)}, u32[]{:S(2)}, u32[]{:S(2)}) %all-to-all-start) | async-done | bytes 786464 | tf_op jit(solution)/shard_map/all_to_all | solution.py:1271
  39.6 12.1 %all_to_all.80.refs_1_ = bf16[32,24,128]{2,1,0:T(8,128)(2,1)} all-to-all(bf16[32,24,128]{2,1,0:T(8,128)(2,1)S(1)} %get-tuple-element.150), channel_id=1, replica_groups=mesh['bhi'=2,'core'=2,'shi'=4,'slo'=2] {'bhi','core','shi','slo'}, dimensions={0} | all-to-all | bytes 393216 | tf_op jit(solution)/shard_map/all_to_all | solution.py:1268
  51.7 3.8 %shard_map.408 = (bf16[384,2304]{1,0:T(8,128)(2,1)}, f32[384,256]{1,0:T(8,128)}, bf16[32,18,128]{2,1,0:T(8,128)(2,1)}, f32[12,128]{1,0:T(8,128)}, f32[32,6,128]{2,1,0:T(8,128)}) custom-call(f32[3]{0:T(128)} %copy-done.4, bf16[32,24,128]{2,1,0:T(8,128)(2,1)} %all_to_all.80.refs_1_, f32[384,256]{1,0:T(8,128)} %copy-done, f32[1,256]{1,0:T(1,128)} %bitcast.85, ...), custom_call_target="tpu_custom_call" | custom-call | flops 452984832 | bytes 4186112 | tf_op jit(solution)/shard_map/pallas_call | solution.py:135
  55.5 11.8 %all_to_all.81.refs_0_ = bf16[32,18,128]{2,1,0:T(8,128)(2,1)} all-to-all(bf16[32,18,128]{2,1,0:T(8,128)(2,1)} %get-tuple-element.152), channel_id=1, replica_groups=mesh['bhi'=2,'core'=2,'shi'=4,'slo'=2] {'bhi','core','shi','slo'}, dimensions={0} | all-to-all | bytes 294912 | tf_op jit(solution)/shard_map/all_to_all | solution.py:1268
  67.4 3.2 shard_map.409
  70.6 3.3 all-to-all-start.3
  77.7 8.4 %all-to-all-done.3.refs_0_ = bf16[32,40,128]{2,1,0:T(8,128)(2,1)} async-done(((bf16[32,40,128]{2,1,0:T(8,128)(2,1)}), bf16[32,40,128]{2,1,0:T(8,128)(2,1)}, u32[]{:S(2)}, u32[]{:S(2)}) %all-to-all-start.3) | async-done | bytes 327712 | tf_op jit(solution)/shard_map/all_to_all | solution.py:1268
  86.1 5.7 %shard_map.410 = (bf16[384,1024]{1,0:T(8,128)(2,1)}, bf16[384,1024]{1,0:T(8,128)(2,1)}, bf16[96,1024]{1,0:T(8,128)(2,1)}, f32[384,512]{1,0:T(8,128)}, bf16[32,36,128]{2,1,0:T(8,128)(2,1)}, /*index=5*/f32[48,128]{1,0:T(8,128)}) custom-call(bf16[32,40,128]{2,1,0:T(8,128)(2,1)} %all-to-all-done.3.refs_0_, f32[32,24,128]{2,1,0:T(8,128)} %broadcast_bitcast_fusion.refs_1_, ...), custom_call_target="tpu_custom_call" | custom-call | flops 402653184 | bytes 7585792 | tf_op jit(solution)/shard_map/pallas_call | solution.py:135
  95.3 11.3 %all-to-all-done.4.refs_0_ = bf16[32,36,128]{2,1,0:T(8,128)(2,1)S(1)} async-done(((bf16[32,36,128]{2,1,0:T(8,128)(2,1)}), bf16[32,36,128]{2,1,0:T(8,128)(2,1)S(1)}, u32[]{:S(2)}, u32[]{:S(2)}) %all-to-all-start.4) | async-done | bytes 294944 | tf_op jit(solution)/shard_map/all_to_all | solution.py:1268
  107.3 4.0 %shard_map.411 = (bf16[384,512]{1,0:T(8,128)(2,1)}, f32[96,512]{1,0:T(8,128)}, bf16[32,36,128]{2,1,0:T(8,128)(2,1)}, f32[24,128]{1,0:T(8,128)}) custom-call(bf16[32,36,128]{2,1,0:T(8,128)(2,1)} %copy-done.15, f32[32,12,128]{2,1,0:T(8,128)} %copy.93.refs_1_.refs_2_, f32[384,512]{1,0:T(8,128)} %get-tuple-element.158.refs_2_.refs_7_.refs_3_, ...), custom_call_target="tpu_custom_call" | custom-call | flops 452984832 | bytes 6897664 | tf_op jit(solution)/shard_map/pallas_call | solution.py:135
  114.0 3.6 %shard_map.412 = (f32[96,2048]{1,0:T(8,128)}, f32[16,8,128]{2,1,0:T(8,128)}) custom-call(bf16[96,1024]{1,0:T(8,128)(2,1)} %get-tuple-element.161.refs_0_.refs_17_, bf16[1024,2048]{1,0:T(8,128)(2,1)} %refs_1_.3), custom_call_target="tpu_custom_call" | custom-call | flops 402653184 | bytes 5242880 | tf_op jit(solution)/shard_map/pallas_call | solution.py:135
  117.6 8.5 %all-to-all-done.5.refs_0_ = bf16[32,36,128]{2,1,0:T(8,128)(2,1)S(1)} async-done(((bf16[32,36,128]{2,1,0:T(8,128)(2,1)}), bf16[32,36,128]{2,1,0:T(8,128)(2,1)S(1)}, u32[]{:S(2)}, u32[]{:S(2)}) %all-to-all-start.5) | async-done | bytes 294944 | tf_op jit(solution)/shard_map/all_to_all | solution.py:1268
  126.7 3.4 shard_map.413
  135.5 5.1 %all-to-all-done.6.refs_0_ = f32[32,8,128]{2,1,0:T(8,128)S(1)} async-done(((f32[32,8,128]{2,1,0:T(8,128)}), f32[32,8,128]{2,1,0:T(8,128)S(1)}, u32[]{:S(2)}, u32[]{:S(2)}) %all-to-all-start.6) | async-done | bytes 131104 | tf_op jit(solution)/shard_map/all_to_all | solution.py:1268
  141.2 10.1 %all_to_all.82.refs_0_.refs_1_ = f32[32,8,128]{2,1,0:T(8,128)} all-to-all(f32[32,8,128]{2,1,0:T(8,128)S(1)} %shard_map.414), channel_id=1, replica_groups=mesh['bhi'=2,'core'=2,'shi'=4,'slo'=2] {'bhi','core','shi','slo'}, dimensions={0} | all-to-all | bytes 262144 | tf_op jit(solution)/shard_map/all_to_all | solution.py:1268
  151.3 3.5 shard_map.415
  159.8 5.5 %all-to-all-done.8.refs_0_ = f32[32,8,128]{2,1,0:T(8,128)S(1)} async-done(((f32[32,8,128]{2,1,0:T(8,128)}), f32[32,8,128]{2,1,0:T(8,128)S(1)}, u32[]{:S(2)}, u32[]{:S(2)}) %all-to-all-start.8) | async-done | bytes 131104 | tf_op jit(solution)/shard_map/all_to_all | solution.py:1268
  171.0 4.4 %collective-permute-done.7.refs_23_ = bf16[96,512]{1,0:T(8,128)(2,1)S(1)} collective-permute-done((bf16[96,512]{1,0:T(8,128)(2,1)}, bf16[96,512]{1,0:T(8,128)(2,1)S(1)}, u32[]{:S(2)}, u32[]{:S(2)}) %collective-permute-start.7) | collective-permute-done | bytes 98336 | tf_op jit(solution)/shard_map/ppermute | solution.py:1274
  177.4 4.4 %shard_map.417 = (bf16[96,2048]{1,0:T(8,128)(2,1)}, f32[16,128]{1,0:T(8,128)}, f32[16,128]{1,0:T(8,128)}, f32[16,128]{1,0:T(8,128)}, f32[16,128]{1,0:T(8,128)}, ...) custom-call(s32[1]{0:T(128)} %bitcast.24.refs_0_, ...), custom_call_target="tpu_custom_call", output_to_operand_aliasing={{11}: (13, {}), {12}: (14, {}), {13}: (15, {}), {14}: (16, ... | custom-call | flops 201326592 | bytes 5767168 | tf_op jit(solution)/shard_map/pallas_call | solution.py:135
  181.8 5.2 %all-to-all-start.10 = ((bf16[32,24,128]{2,1,0:T(8,128)(2,1)}), bf16[32,24,128]{2,1,0:T(8,128)(2,1)S(1)}, u32[]{:S(2)}, u32[]{:S(2)}) async-start(bf16[32,24,128]{2,1,0:T(8,128)(2,1)} %get-tuple-element.172), calls=%async_computation.10 | async-start | bytes 393216 | tf_op jit(solution)/shard_map/all_to_all | solution.py:1268
  189.0 4.5 %shard_map.418.refs_16_ = f32[96,1024]{1,0:T(8,128)} custom-call(bf16[96,2048]{1,0:T(8,128)(2,1)} %get-tuple-element.179.refs_0_, bf16[1024,2048]{1,0:T(8,128)(2,1)} %refs_1_.3), custom_call_target="tpu_custom_call" | custom-call | flops 402653184 | bytes 4980736 | tf_op jit(solution)/shard_map/pallas_call | solution.py:135
  193.6 3.4 collective-permute-done.10.refs_14_
  197.0 3.5 collective-permute-done.11.refs_15_
  201.2 6.3 %shard_map.419 = (f32[4,128]{1,0:T(4,128)}, f32[4,128]{1,0:T(4,128)}, f32[384,512]{1,0:T(8,128)}, bf16[32,24,128]{2,1,0:T(8,128)(2,1)}, bf16[96,128]{1,0:T(8,128...) custom-call(s32[1]{0:T(128)} %bitcast.24.refs_0_, ...), custom_call_target="tpu_custom_call", output_to_operand_aliasing={{8}: (12, {}), {9}: (13, {}), {10}: (14, {}), {11}: (15, {}... | custom-call | flops 452984832 | bytes 7309312 | tf_op jit(solution)/shard_map/pallas_call | solution.py:135
  207.5 4.7 %all-to-all-start.11 = ((bf16[32,24,128]{2,1,0:T(8,128)(2,1)}), bf16[32,24,128]{2,1,0:T(8,128)(2,1)S(1)}, u32[]{:S(2)}, u32[]{:S(2)}) async-start(bf16[32,24,128]{2,1,0:T(8,128)(2,1)} %get-tuple-element.180), calls=%async_computation.11 | async-start | bytes 393216 | tf_op jit(solution)/shard_map/all_to_all | solution.py:1268
  214.2 3.8 %shard_map.420.refs_11_ = bf16[2,4,192,512]{3,2,1,0:T(8,128)(2,1)} custom-call(bf16[96,512]{1,0:T(8,128)(2,1)} %get-tuple-element.185.refs_0_, bf16[96,512]{1,0:T(8,128)(2,1)} %get-tuple-element.186.refs_1_, bf16[96,512]{1,0:T(8,128)(2,1)} %get-tuple-element.187.refs_2_, bf16[96,512]{1,0:T(8,128)(2,1)} %get-tuple-element.188.refs_3_, ...), custom_call_target="tpu_custom_call" | custom-call | flops 603979776 | bytes 1966080 | tf_op jit(solution)/shard_map/pallas_call | solution.py:135
  221.4 4.9 %shard_map.421 = (bf16[384,512]{1,0:T(8,128)(2,1)}, f32[4,128]{1,0:T(4,128)}, f32[4,128]{1,0:T(4,128)}, bf16[384,1024]{1,0:T(8,128)(2,1)}, bf16[32,48,128]{2,1,0...) custom-call(bf16[32,24,128]{2,1,0:T(8,128)(2,1)} %copy-done.22, ...), custom_call_target="tpu_custom_call", output_to_operand_aliasing={{5}: (11, {}), {6}: (12, {}), {7}: (13, {}), {8}: (14, {}),... | custom-call | flops 402653184 | bytes 7383040 | tf_op jit(solution)/shard_map/pallas_call | solution.py:135
  226.3 3.2 all-to-all-start.12
  229.6 4.1 %shard_map.422.refs_11_ = bf16[2,4,144,512]{3,2,1,0:T(8,128)(2,1)} custom-call(bf16[384,512]{1,0:T(8,128)(2,1)} %get-tuple-element.204.refs_0_, bf16[384,512]{1,0:T(8,128)(2,1)} %get-tuple-element.205.refs_1_, bf16[384,512]{1,0:T(8,128)(2,1)} %get-tuple-element.206.refs_2_, bf16[384,512]{1,0:T(8,128)(2,1)} %get-tuple-element.207.refs_3_, ...), custom_call_target="tpu_custom_call" | custom-call | flops 452984832 | bytes 1671168 | tf_op jit(solution)/shard_map/pallas_call | solution.py:135
  233.7 9.4 %all-to-all-done.12.refs_0_ = bf16[32,48,128]{2,1,0:T(8,128)(2,1)S(1)} async-done(((bf16[32,48,128]{2,1,0:T(8,128)(2,1)}), bf16[32,48,128]{2,1,0:T(8,128)(2,1)S(1)}, u32[]{:S(2)}, u32[]{:S(2)}) %all-to-all-start.12) | async-done | bytes 393248 | tf_op jit(solution)/shard_map/all_to_all | solution.py:1268
  243.8 4.1 %shard_map.423 = (bf16[384,1024]{1,0:T(8,128)(2,1)}, f32[8,128]{1,0:T(8,128)}, f32[8,128]{1,0:T(8,128)}, f32[384,256]{1,0:T(8,128)}, bf16[32,12,128]{2,1,0:T(8,128)(2,1)}, /*index=5*/bf16[2,4,144,512]{3,2,1,0:T(8,128)(2,1)}) custom-call(bf16[32,48,128]{2,1,0:T(8,128)(2,1)} %copy-done.13, ...), custom_call_target="tpu_custom_call", output_to_operand_aliasing={{5}: (11, {})} | custom-call | flops 201326592 | bytes 5386240 | tf_op jit(solution)/shard_map/pallas_call | solution.py:135
  248.0 2.9 all-to-all-start.13
  252.5 3.8 %shard_map.424 = (bf16[4,2,2,96,256]{4,3,2,1,0:T(8,128)(2,1)}, bf16[4,2,2,96,256]{4,3,2,1,0:T(8,128)(2,1)}) custom-call(s32[1]{0:T(128)} %bitcast.24.refs_0_, bf16[384,1024]{1,0:T(8,128)(2,1)} %get-tuple-element.215.refs_1_, bf16[384,512]{1,0:T(8,128)(2,1)} %get-tuple-element.216.refs_2_, bf16[384,256]{1,0:T(8,128)(2,1)} %get-tuple-element.217.refs_3_, ...), custom_call_target="tpu_custom_call" | custom-call | flops 603979776 | bytes 2162688 | tf_op jit(solution)/shard_map/pallas_call | solution.py:135
  259.1 3.6 shard_map.425
  262.9 3.5 all-to-all-start.14
  267.1 3.4 shard_map.426
  270.4 3.8 %all-to-all-done.14.refs_1_ = bf16[32,12,128]{2,1,0:T(8,128)(2,1)S(1)} async-done(((bf16[32,12,128]{2,1,0:T(8,128)(2,1)}), bf16[32,12,128]{2,1,0:T(8,128)(2,1)S(1)}, u32[]{:S(2)}, u32[]{:S(2)}) %all-to-all-start.14) | async-done | bytes 98336 | tf_op jit(solution)/shard_map/all_to_all | solution.py:1268
  275.1 3.0 shard_map.427
  281.7 4.7 %shard_map.428 = (bf16[4,200,256]{2,1,0:T(8,128)(2,1)}, bf16[4,200,256]{2,1,0:T(8,128)(2,1)}, bf16[4,200,256]{2,1,0:T(8,128)(2,1)}, bf16[4,200,256]{2,1,0:T(8,128)(2,1)}, bf16[4,336,512]{2,1,0:T(8,128)(2,1)}) custom-call(s32[3]{0:T(128)} %get-tuple-element.228.refs_0_, bf16[4,2,2,96,256]{4,3,2,1,0:T(8,128)(2,1)} %get-tuple-element.229.refs_1_, ...), custom_call_target="tpu_custom_call" | custom-call | bytes 4653056 | tf_op jit(solution)/shard_map/pallas_call | solution.py:135
  290.0 9.0 %collective-permute-done.18.refs_4_ = bf16[4,200,256]{2,1,0:T(8,128)(2,1)S(1)} collective-permute-done((bf16[4,200,256]{2,1,0:T(8,128)(2,1)}, bf16[4,200,256]{2,1,0:T(8,128)(2,1)S(1)}, u32[]{:S(2)}, u32[]{:S(2)}) %collective-permute-start.18) | collective-permute-done | bytes 409632 | tf_op jit(solution)/shard_map/ppermute | solution.py:1404
  299.0 8.9 %collective-permute-done.19.refs_5_ = bf16[4,200,256]{2,1,0:T(8,128)(2,1)S(1)} collective-permute-done((bf16[4,200,256]{2,1,0:T(8,128)(2,1)}, bf16[4,200,256]{2,1,0:T(8,128)(2,1)S(1)}, u32[]{:S(2)}, u32[]{:S(2)}) %collective-permute-start.19) | collective-permute-done | bytes 409632 | tf_op jit(solution)/shard_map/ppermute | solution.py:1404
  308.7 2.8 shard_map.429
  311.5 4.6 %all-to-all-start.15 = ((bf16[8,3,16,1024]{3,2,1,0:T(8,128)(2,1)}), bf16[8,3,16,1024]{3,2,1,0:T(8,128)(2,1)S(1)}, u32[]{:S(2)}, u32[]{:S(2)}) async-start(bf16[8,3,16,1024]{3,2,1,0:T(8,128)(2,1)} %get-tuple-element.241), calls=%async_computation.17 | async-start | bytes 1572864 | tf_op jit(solution)/shard_map/all_to_all | solution.py:1271
  318.8 3.0 shard_map.430
  323.5 8.3 %collective-permute-done.25.refs_3_ = bf16[336,512]{1,0:T(8,128)(2,1)S(1)} collective-permute-done((bf16[336,512]{1,0:T(8,128)(2,1)}, bf16[336,512]{1,0:T(8,128)(2,1)S(1)}, u32[]{:S(2)}, u32[]{:S(2)}) %collective-permute-start.25) | collective-permute-done | bytes 344096 | tf_op jit(solution)/shard_map/ppermute | solution.py:1274
  339.6 3.5 collective-permute-done.22.refs_2_
  346.5 3.4 collective-permute-done.28.refs_3_
  (168 shorter events, 76.0 us)
Async XLA Ops:
  7.2 29.6 %copy-start.1 = (bf16[1024,256]{1,0:T(8,128)(2,1)S(1)}, bf16[1024,256]{1,0:T(8,128)(2,1)}, u32[]{:S(2)}) copy-start(bf16[1024,256]{1,0:T(8,128)(2,1)} %refs_2_.3) | copy-start | bytes 1572868
  9.4 27.4 %all-to-all-start = ((bf16[8,3,16,1024]{3,2,1,0:T(8,128)(2,1)}), bf16[8,3,16,1024]{3,2,1,0:T(8,128)(2,1)S(1)}, u32[]{:S(2)}, u32[]{:S(2)}) async-start(bf16[8,3,16,1024]{3,2,1,0:T(8,128)(2,1)} %bitcast.60), calls=%async_computation | async-start | bytes 1572864 | tf_op jit(solution)/shard_map/all_to_all | solution.py:1271
  16.8 34.9 %copy-start.4 = (f32[3]{0:T(128)}, f32[3]{0:T(128)S(1)}, u32[]{:S(2)}) copy-start(f32[3]{0:T(128)S(1)} %convert_reduce_fusion.refs_0_) | copy-start | bytes 40
  70.6 15.5 %all-to-all-start.3 = ((bf16[32,40,128]{2,1,0:T(8,128)(2,1)}), bf16[32,40,128]{2,1,0:T(8,128)(2,1)}, u32[]{:S(2)}, u32[]{:S(2)}) async-start(bf16[32,40,128]{2,1,0:T(8,128)(2,1)} %get-tuple-element.155), calls=%async_computation.3 | async-start | bytes 655360 | tf_op jit(solution)/shard_map/all_to_all | solution.py:1268
  91.8 14.8 %all-to-all-start.4 = ((bf16[32,36,128]{2,1,0:T(8,128)(2,1)}), bf16[32,36,128]{2,1,0:T(8,128)(2,1)S(1)}, u32[]{:S(2)}, u32[]{:S(2)}) async-start(bf16[32,36,128]{2,1,0:T(8,128)(2,1)} %get-tuple-element.157), calls=%async_computation.4 | async-start | bytes 655360 | tf_op jit(solution)/shard_map/all_to_all | solution.py:1268
  111.3 14.8 %all-to-all-start.5 = ((bf16[32,36,128]{2,1,0:T(8,128)(2,1)}), bf16[32,36,128]{2,1,0:T(8,128)(2,1)S(1)}, u32[]{:S(2)}, u32[]{:S(2)}) async-start(bf16[32,36,128]{2,1,0:T(8,128)(2,1)} %get-tuple-element.159), calls=%async_computation.5 | async-start | bytes 655360 | tf_op jit(solution)/shard_map/all_to_all | solution.py:1268
  130.2 10.3 %all-to-all-start.6 = ((f32[32,8,128]{2,1,0:T(8,128)}), f32[32,8,128]{2,1,0:T(8,128)S(1)}, u32[]{:S(2)}, u32[]{:S(2)}) async-start(f32[32,8,128]{2,1,0:T(8,128)} %get-tuple-element.163), calls=%async_computation.6 | async-start | bytes 262144 | tf_op jit(solution)/shard_map/all_to_all | solution.py:1268
  133.7 25.7 %collective-permute-start.1 = (bf16[384,512]{1,0:T(8,128)(2,1)S(1)}, bf16[384,512]{1,0:T(8,128)(2,1)}, u32[]{:S(2)}, u32[]{:S(2)}) collective-permute-start(bf16[384,512]{1,0:T(8,128)(2,1)S(1)} %copy-done.11), channel_id=1, source_target_pairs={{0,16},{16,0},{1,17},{17,1},{2,18},{18,2},{3,19},{19,3},{4,20},{20... | collective-permute-start | bytes 1179656 | tf_op jit(solution)/shard_map/ppermute | solution.py:1274
  154.8 10.5 %all-to-all-start.8 = ((f32[32,8,128]{2,1,0:T(8,128)}), f32[32,8,128]{2,1,0:T(8,128)S(1)}, u32[]{:S(2)}, u32[]{:S(2)}) async-start(f32[32,8,128]{2,1,0:T(8,128)} %get-tuple-element.167), calls=%async_computation.8 | async-start | bytes 262144 | tf_op jit(solution)/shard_map/all_to_all | solution.py:1268
  157.6 11.4 %collective-permute-start.4 = (bf16[96,1024]{1,0:T(8,128)(2,1)S(1)}, bf16[96,1024]{1,0:T(8,128)(2,1)S(1)}, u32[]{:S(2)}, u32[]{:S(2)}) collective-permute-start(bf16[96,1024]{1,0:T(8,128)(2,1)S(1)} %copy-done.8), channel_id=1, source_target_pairs={{0,16},{16,0},{1,17},{17,1},{2,18},{18,2},{3,19},{19,3},{4,20},{20... | collective-permute-start | bytes 589832 | tf_op jit(solution)/shard_map/ppermute | solution.py:1274
  159.3 16.1 %collective-permute-start = (bf16[384,512]{1,0:T(8,128)(2,1)S(1)}, bf16[384,512]{1,0:T(8,128)(2,1)S(1)}, u32[]{:S(2)}, u32[]{:S(2)}) collective-permute-start(bf16[384,512]{1,0:T(8,128)(2,1)S(1)} %copy-done.11), channel_id=1, source_target_pairs={{0,8},{8,0},{1,9},{9,1},{2,10},{10,2},{3,11},{11,3},{4,12},{12,4},... | collective-permute-start | bytes 1179656 | tf_op jit(solution)/shard_map/ppermute | solution.py:1274
  159.3 17.4 %collective-permute-start.2 = (bf16[384,512]{1,0:T(8,128)(2,1)}, bf16[384,512]{1,0:T(8,128)(2,1)}, u32[]{:S(2)}, u32[]{:S(2)}) collective-permute-start(bf16[384,512]{1,0:T(8,128)(2,1)} %collective-permute-done.1.refs_15_), channel_id=1, source_target_pairs={{0,8},{8,0},{1,9},{9,1},{2,10},{10,2},{3,11},{11,3},{4,12},{12,4},... | collective-permute-start | bytes 1179656 | tf_op jit(solution)/shard_map/ppermute | solution.py:1274
  159.8 11.1 %collective-permute-start.3 = (bf16[96,1024]{1,0:T(8,128)(2,1)S(1)}, bf16[96,1024]{1,0:T(8,128)(2,1)S(1)}, u32[]{:S(2)}, u32[]{:S(2)}) collective-permute-start(bf16[96,1024]{1,0:T(8,128)(2,1)S(1)} %copy-done.8), channel_id=1, source_target_pairs={{0,8},{8,0},{1,9},{9,1},{2,10},{10,2},{3,11},{11,3},{4,12},{12,4},... | collective-permute-start | bytes 589832 | tf_op jit(solution)/shard_map/ppermute | solution.py:1274
  166.4 10.3 %all-to-all-start.9 = ((f32[32,8,128]{2,1,0:T(8,128)}), f32[32,8,128]{2,1,0:T(8,128)S(1)}, u32[]{:S(2)}, u32[]{:S(2)}) async-start(f32[32,8,128]{2,1,0:T(8,128)} %shard_map.416), calls=%async_computation.9 | async-start | bytes 262144 | tf_op jit(solution)/shard_map/all_to_all | solution.py:1268
  169.0 6.4 %collective-permute-start.5 = (bf16[96,1024]{1,0:T(8,128)(2,1)S(1)}, bf16[96,1024]{1,0:T(8,128)(2,1)S(1)}, u32[]{:S(2)}, u32[]{:S(2)}) collective-permute-start(bf16[96,1024]{1,0:T(8,128)(2,1)S(1)} %collective-permute-done.4.refs_19_), channel_id=1, source_target_pairs={{0,8},{8,0},{1,9},{9,1},{2,10},{10,2},{3,11},{11,3},{4,12},{12,4},... | collective-permute-start | bytes 589832 | tf_op jit(solution)/shard_map/ppermute | solution.py:1274
  169.2 6.2 %collective-permute-start.7 = (bf16[96,512]{1,0:T(8,128)(2,1)}, bf16[96,512]{1,0:T(8,128)(2,1)S(1)}, u32[]{:S(2)}, u32[]{:S(2)}) collective-permute-start(bf16[96,512]{1,0:T(8,128)(2,1)} %get-tuple-element.171.refs_21_), channel_id=1, source_target_pairs={{0,16},{16,0},{1,17},{17,1},{2,18},{18,2},{3,19},{19,3},{4,20},{20... | collective-permute-start | bytes 294920 | tf_op jit(solution)/shard_map/ppermute | solution.py:1274
  170.9 5.4 %collective-permute-start.6 = (bf16[96,512]{1,0:T(8,128)(2,1)}, bf16[96,512]{1,0:T(8,128)(2,1)S(1)}, u32[]{:S(2)}, u32[]{:S(2)}) collective-permute-start(bf16[96,512]{1,0:T(8,128)(2,1)} %get-tuple-element.171.refs_21_), channel_id=1, source_target_pairs={{0,8},{8,0},{1,9},{9,1},{2,10},{10,2},{3,11},{11,3},{4,12},{12,4},... | collective-permute-start | bytes 294920 | tf_op jit(solution)/shard_map/ppermute | solution.py:1274
  175.4 1.3 collective-permute-start.8
  181.8 18.7 %all-to-all-start.10 = ((bf16[32,24,128]{2,1,0:T(8,128)(2,1)}), bf16[32,24,128]{2,1,0:T(8,128)(2,1)S(1)}, u32[]{:S(2)}, u32[]{:S(2)}) async-start(bf16[32,24,128]{2,1,0:T(8,128)(2,1)} %get-tuple-element.172), calls=%async_computation.10 | async-start | bytes 393216 | tf_op jit(solution)/shard_map/all_to_all | solution.py:1268
  187.0 6.5 %collective-permute-start.9 = (bf16[96,1024]{1,0:T(8,128)(2,1)}, bf16[96,1024]{1,0:T(8,128)(2,1)S(1)}, u32[]{:S(2)}, u32[]{:S(2)}) collective-permute-start(bf16[96,1024]{1,0:T(8,128)(2,1)} %get-tuple-element.176), channel_id=1, source_target_pairs={{0,8},{8,0},{16,24},{24,16},{1,9},{9,1},{17,25},{25,17},{2,10},{10... | collective-permute-start | bytes 589832 | tf_op jit(solution)/shard_map/ppermute | solution.py:1278
  187.4 9.6 %collective-permute-start.10 = (bf16[96,1024]{1,0:T(8,128)(2,1)}, bf16[96,1024]{1,0:T(8,128)(2,1)S(1)}, u32[]{:S(2)}, u32[]{:S(2)}) collective-permute-start(bf16[96,1024]{1,0:T(8,128)(2,1)} %get-tuple-element.177), channel_id=1, source_target_pairs={{0,16},{8,24},{16,0},{24,8},{1,17},{9,25},{17,1},{25,9},{2,18},{10... | collective-permute-start | bytes 589832 | tf_op jit(solution)/shard_map/ppermute | solution.py:1278
  189.0 11.5 %collective-permute-start.11 = (bf16[96,1024]{1,0:T(8,128)(2,1)}, bf16[96,1024]{1,0:T(8,128)(2,1)S(1)}, u32[]{:S(2)}, u32[]{:S(2)}) collective-permute-start(bf16[96,1024]{1,0:T(8,128)(2,1)} %get-tuple-element.178), channel_id=1, source_target_pairs={{0,24},{8,16},{16,8},{24,0},{1,25},{9,17},{17,9},{25,1},{2,26},{10... | collective-permute-start | bytes 589832 | tf_op jit(solution)/shard_map/ppermute | solution.py:1278
  207.5 13.2 %all-to-all-start.11 = ((bf16[32,24,128]{2,1,0:T(8,128)(2,1)}), bf16[32,24,128]{2,1,0:T(8,128)(2,1)S(1)}, u32[]{:S(2)}, u32[]{:S(2)}) async-start(bf16[32,24,128]{2,1,0:T(8,128)(2,1)} %get-tuple-element.180), calls=%async_computation.11 | async-start | bytes 393216 | tf_op jit(solution)/shard_map/all_to_all | solution.py:1268
  212.2 46.3 %reduce-scatter.4.cloned.1.call-start = ((), (), s32[]{:S(2)}) async-start(), calls=%async_computation.19 | async-start | bytes 2359296 | tf_op jit(solution)/shard_map/reduce_scatter | solution.py:1373
  212.2 5.9 %collective-permute-start.12 = (bf16[96,128]{1,0:T(8,128)(2,1)}, bf16[96,128]{1,0:T(8,128)(2,1)S(1)}, u32[]{:S(2)}, u32[]{:S(2)}) collective-permute-start(bf16[96,128]{1,0:T(8,128)(2,1)} %get-tuple-element.198), channel_id=1, source_target_pairs={{0,8},{8,0},{16,24},{24,16},{1,9},{9,1},{17,25},{25,17},{2,10},{10... | collective-permute-start | bytes 73736 | tf_op jit(solution)/shard_map/ppermute | solution.py:1278
  212.5 5.6 %collective-permute-start.13 = (bf16[96,128]{1,0:T(8,128)(2,1)}, bf16[96,128]{1,0:T(8,128)(2,1)S(1)}, u32[]{:S(2)}, u32[]{:S(2)}) collective-permute-start(bf16[96,128]{1,0:T(8,128)(2,1)} %get-tuple-element.199), channel_id=1, source_target_pairs={{0,16},{8,24},{16,0},{24,8},{1,17},{9,25},{17,1},{25,9},{2,18},{10... | collective-permute-start | bytes 73736 | tf_op jit(solution)/shard_map/ppermute | solution.py:1278
  214.2 3.9 %collective-permute-start.14 = (bf16[96,128]{1,0:T(8,128)(2,1)}, bf16[96,128]{1,0:T(8,128)(2,1)S(1)}, u32[]{:S(2)}, u32[]{:S(2)}) collective-permute-start(bf16[96,128]{1,0:T(8,128)(2,1)} %get-tuple-element.200), channel_id=1, source_target_pairs={{0,24},{8,16},{16,8},{24,0},{1,25},{9,17},{17,9},{25,1},{2,26},{10... | collective-permute-start | bytes 73736 | tf_op jit(solution)/shard_map/ppermute | solution.py:1278
  226.3 16.8 %all-to-all-start.12 = ((bf16[32,48,128]{2,1,0:T(8,128)(2,1)}), bf16[32,48,128]{2,1,0:T(8,128)(2,1)S(1)}, u32[]{:S(2)}, u32[]{:S(2)}) async-start(bf16[32,48,128]{2,1,0:T(8,128)(2,1)} %get-tuple-element.201), calls=%async_computation.12 | async-start | bytes 786432 | tf_op jit(solution)/shard_map/all_to_all | solution.py:1268
  229.6 51.2 %reduce-scatter.6.cloned.1.call-start = ((), (), s32[]{:S(2)}) async-start(), calls=%async_computation.20 | async-start | bytes 1769472 | tf_op jit(solution)/shard_map/reduce_scatter | solution.py:1381
  248.0 10.5 %all-to-all-start.13 = ((bf16[32,12,128]{2,1,0:T(8,128)(2,1)}), bf16[32,12,128]{2,1,0:T(8,128)(2,1)S(1)}, u32[]{:S(2)}, u32[]{:S(2)}) async-start(bf16[32,12,128]{2,1,0:T(8,128)(2,1)} %get-tuple-element.212), calls=%async_computation.13 | async-start | bytes 262144 | tf_op jit(solution)/shard_map/all_to_all | solution.py:1268
  262.7 11.5 %collective-permute-start.15 = (bf16[4,2,2,96,256]{4,3,2,1,0:T(8,128)(2,1)}, bf16[4,2,2,96,256]{4,3,2,1,0:T(8,128)(2,1)S(1)}, u32[]{:S(2)}, u32[]{:S(2)}) collective-permute-start(bf16[4,2,2,96,256]{4,3,2,1,0:T(8,128)(2,1)} %get-tuple-element.226), channel_id=1, source_target_pairs={{0,8},{8,0},{1,9},{9,1},{2,10},{10,2},{3,11},{11,3},{4,12},{12,4},... | collective-permute-start | bytes 2359304 | tf_op jit(solution)/shard_map/ppermute | solution.py:1274
  262.9 11.3 %all-to-all-start.14 = ((bf16[32,12,128]{2,1,0:T(8,128)(2,1)}), bf16[32,12,128]{2,1,0:T(8,128)(2,1)S(1)}, u32[]{:S(2)}, u32[]{:S(2)}) async-start(bf16[32,12,128]{2,1,0:T(8,128)(2,1)} %get-tuple-element.221), calls=%async_computation.15 | async-start | bytes 262144 | tf_op jit(solution)/shard_map/all_to_all | solution.py:1268
  266.4 52.4 %reduce-scatter.8.cloned.1.call-start = ((), (), s32[]{:S(2)}) async-start(), calls=%async_computation.21 | async-start | bytes 1720320 | tf_op jit(solution)/shard_map/reduce_scatter | solution.py:1420
  278.1 2.7 collective-permute-start.16
  278.3 2.5 collective-permute-start.17
  286.4 12.6 %collective-permute-start.18 = (bf16[4,200,256]{2,1,0:T(8,128)(2,1)}, bf16[4,200,256]{2,1,0:T(8,128)(2,1)S(1)}, u32[]{:S(2)}, u32[]{:S(2)}) collective-permute-start(bf16[4,200,256]{2,1,0:T(8,128)(2,1)} %get-tuple-element.238), channel_id=1, source_target_pairs={{0,1},{1,0},{16,17},{17,16},{2,3},{3,2},{18,19},{19,18},{4,5},{5,4... | collective-permute-start | bytes 1228808 | tf_op jit(solution)/shard_map/ppermute | solution.py:1404
  287.7 20.2 %collective-permute-start.19 = (bf16[4,200,256]{2,1,0:T(8,128)(2,1)}, bf16[4,200,256]{2,1,0:T(8,128)(2,1)S(1)}, u32[]{:S(2)}, u32[]{:S(2)}) collective-permute-start(bf16[4,200,256]{2,1,0:T(8,128)(2,1)} %get-tuple-element.239), channel_id=1, source_target_pairs={{0,16},{1,17},{16,0},{17,1},{2,18},{3,19},{18,2},{19,3},{4,20},{5,... | collective-permute-start | bytes 1228808 | tf_op jit(solution)/shard_map/ppermute | solution.py:1404
  288.5 19.4 %collective-permute-start.20 = (bf16[4,200,256]{2,1,0:T(8,128)(2,1)}, bf16[4,200,256]{2,1,0:T(8,128)(2,1)}, u32[]{:S(2)}, u32[]{:S(2)}) collective-permute-start(bf16[4,200,256]{2,1,0:T(8,128)(2,1)} %get-tuple-element.240), channel_id=1, source_target_pairs={{0,17},{1,16},{16,1},{17,0},{2,19},{3,18},{18,3},{19,2},{4,21},{5,... | collective-permute-start | bytes 1228808 | tf_op jit(solution)/shard_map/ppermute | solution.py:1404
  311.5 38.4 %all-to-all-start.15 = ((bf16[8,3,16,1024]{3,2,1,0:T(8,128)(2,1)}), bf16[8,3,16,1024]{3,2,1,0:T(8,128)(2,1)S(1)}, u32[]{:S(2)}, u32[]{:S(2)}) async-start(bf16[8,3,16,1024]{3,2,1,0:T(8,128)(2,1)} %get-tuple-element.241), calls=%async_computation.17 | async-start | bytes 1572864 | tf_op jit(solution)/shard_map/all_to_all | solution.py:1271
  321.9 9.9 %collective-permute-start.25 = (bf16[336,512]{1,0:T(8,128)(2,1)}, bf16[336,512]{1,0:T(8,128)(2,1)S(1)}, u32[]{:S(2)}, u32[]{:S(2)}) collective-permute-start(bf16[336,512]{1,0:T(8,128)(2,1)} %bitcast.61), channel_id=1, source_target_pairs={{0,16},{16,0},{1,17},{17,1},{2,18},{18,2},{3,19},{19,3},{4,20},{20... | collective-permute-start | bytes 1032200 | tf_op jit(solution)/shard_map/ppermute | solution.py:1274
  323.5 12.7 %collective-permute-start.24 = (bf16[336,512]{1,0:T(8,128)(2,1)}, bf16[336,512]{1,0:T(8,128)(2,1)S(1)}, u32[]{:S(2)}, u32[]{:S(2)}) collective-permute-start(bf16[336,512]{1,0:T(8,128)(2,1)} %bitcast.62), channel_id=1, source_target_pairs={{0,8},{8,0},{1,9},{9,1},{2,10},{10,2},{3,11},{11,3},{4,12},{12,4},... | collective-permute-start | bytes 1032200 | tf_op jit(solution)/shard_map/ppermute | solution.py:1274
  331.8 4.4 %collective-permute-start.26 = (bf16[336,512]{1,0:T(8,128)(2,1)S(1)}, bf16[336,512]{1,0:T(8,128)(2,1)S(1)}, u32[]{:S(2)}, u32[]{:S(2)}) collective-permute-start(bf16[336,512]{1,0:T(8,128)(2,1)S(1)} %collective-permute-done.25.refs_3_), channel_id=1, source_target_pairs={{0,8},{8,0},{1,9},{9,1},{2,10},{10,2},{3,11},{11,3},{4,12},{12,4},... | collective-permute-start | bytes 1032200 | tf_op jit(solution)/shard_map/ppermute | solution.py:1274
  331.8 7.8 %collective-permute-start.21 = (bf16[200,256]{1,0:T(8,128)(2,1)}, bf16[200,256]{1,0:T(8,128)(2,1)S(1)}, u32[]{:S(2)}, u32[]{:S(2)}) collective-permute-start(bf16[200,256]{1,0:T(8,128)(2,1)} %get-tuple-element.248), channel_id=1, source_target_pairs={{0,2},{2,0},{4,6},{6,4},{1,3},{3,1},{5,7},{7,5},{8,10},{10,8},{12,... | collective-permute-start | bytes 307208 | tf_op jit(solution)/shard_map/ppermute | solution.py:1274
  331.8 11.3 %collective-permute-start.22 = (bf16[200,256]{1,0:T(8,128)(2,1)}, bf16[200,256]{1,0:T(8,128)(2,1)}, u32[]{:S(2)}, u32[]{:S(2)}) collective-permute-start(bf16[200,256]{1,0:T(8,128)(2,1)} %get-tuple-element.249), channel_id=1, source_target_pairs={{0,4},{2,6},{4,0},{6,2},{1,5},{3,7},{5,1},{7,3},{8,12},{10,14},{12... | collective-permute-start | bytes 307208 | tf_op jit(solution)/shard_map/ppermute | solution.py:1274
  333.9 9.2 %collective-permute-start.23 = (bf16[200,256]{1,0:T(8,128)(2,1)}, bf16[200,256]{1,0:T(8,128)(2,1)}, u32[]{:S(2)}, u32[]{:S(2)}) collective-permute-start(bf16[200,256]{1,0:T(8,128)(2,1)} %get-tuple-element.250), channel_id=1, source_target_pairs={{0,6},{2,4},{4,2},{6,0},{1,7},{3,5},{5,3},{7,1},{8,14},{10,12},{12... | collective-permute-start | bytes 307208 | tf_op jit(solution)/shard_map/ppermute | solution.py:1274
  344.9 4.9 %collective-permute-start.28 = (bf16[200,256]{1,0:T(8,128)(2,1)}, bf16[200,256]{1,0:T(8,128)(2,1)S(1)}, u32[]{:S(2)}, u32[]{:S(2)}) collective-permute-start(bf16[200,256]{1,0:T(8,128)(2,1)} %get-tuple-element.255.refs_1_), channel_id=1, source_target_pairs={{0,16},{16,0},{1,17},{17,1},{2,18},{18,2},{3,19},{19,3},{4,20},{20... | collective-permute-start | bytes 307208 | tf_op jit(solution)/shard_map/ppermute | solution.py:1274
  346.5 4.4 %collective-permute-start.27 = (bf16[200,256]{1,0:T(8,128)(2,1)}, bf16[200,256]{1,0:T(8,128)(2,1)S(1)}, u32[]{:S(2)}, u32[]{:S(2)}) collective-permute-start(bf16[200,256]{1,0:T(8,128)(2,1)} %get-tuple-element.255.refs_1_), channel_id=1, source_target_pairs={{0,8},{8,0},{1,9},{9,1},{2,10},{10,2},{3,11},{11,3},{4,12},{12,4},... | collective-permute-start | bytes 307208 | tf_op jit(solution)/shard_map/ppermute | solution.py:1274
  349.9 1.3 collective-permute-start.29
  (35 other events, 109.1 us)
Sparse Core Ops, SparseCore 0:
  226.4 28.3 reduce-scatter.3
  257.7 23.0 reduce-scatter.5
  286.5 32.2 reduce-scatter.7

commit v4 on v3

--- a/solution.py
+++ b/solution.py
@@ -81,7 +81,7 @@
         self.flying.append(copy)
 
 
-def kernel_call(body, outs, args, weights=(), scratch=(), flops=0, raw=(), n_raw=0, scalars=(), passes=(), stacks=(), limit=63, chunks=1):
+def kernel_call(body, outs, args, weights=(), scratch=(), flops=0, raw=(), n_raw=0, scalars=(), passes=(), stacks=(), limit=63, chunks=1, late=0):
     n_s, n_in, n_w, n_p = len(scalars), len(args), len(weights), len(passes)
     n_k = sum(map(len, stacks))
     n_out, n_r = len(outs), len(raw)
@@ -115,7 +115,8 @@
             copy.start()
         k = Kernel(v_in, v_w, v_out, raw_refs, s, v_k, refs, w_copies, sem[n_out:])
         k.out_pairs = {j: (v_out[j], out[j], sem[j]) for j in range(n_out)}
-        for copy in in_copies:
+        k.coming = in_copies[len(in_copies) - late :]
+        for copy in in_copies[: len(in_copies) - late]:
             copy.wait()
         body(k)
         for j in range(n_out):
@@ -1098,10 +1099,6 @@
 
     def body(k):
         (held,) = k.x
-        top = 0
-        for e, r in zip(k.i[2 * len(groups) :], tall):
-            k.copy(e, k.raw[-1].at[:, pl.ds(top, r)])
-            top += r
         at = 0
         for j, r in enumerate(rows):
             both = k.i[2 * j][...].astype(F32) + k.i[2 * j + 1][...].astype(F32)
@@ -1110,6 +1107,12 @@
         for i in range(high):
             for j in range(z.slo):
                 k.copy(held.at[:, k.s[0][0] ^ j, k.s[0][1] ^ i], k.raw[z.slo * i + j])
+        top = 0
+        for copy in k.coming:
+            copy.wait()
+        for e, r in zip(k.i[2 * len(groups) :], tall):
+            k.copy(e, k.raw[-1].at[:, pl.ds(top, r)])
+            top += r
 
     total = sum(rows)
     return kernel_call(
@@ -1121,6 +1124,7 @@
         + ([arr(hi, sum(tall), early[0].shape[2], dtype=BF)] if early else []),
         n_raw=z.slo * high + len(early),
         scalars=[where],
+        late=len(early),
     )
 
 

time: 361 us -> 361 us (level)
  no operation moved by 1% of the time
where the time goes in v4:
time: 361 us; the launch traced here: 359 us
  waiting for transfers between devices  127 us (35%)
  Pallas kernels  93 us (26%)
  starting transfers between devices  69.7 us (19%)
  blocking collectives  34 us (9%)
  local copies, waits for them, and re-layouts  18.4 us (5%)
  between operations  14.4 us (4%)
    pallas_call x27, Pallas kernels, kernel_call(): pl.pallas_call(run, out_shape=tuple((jax.ShapeDtypeStruct(o.shape, o.dtyp...  93 us
    all_to_all x11, waiting for transfers between devices, share(): return lax.all_to_all(pay, ALL, 0, 0, tiled=True)  56.6 us
    all_to_all x11, starting transfers between devices, share(): return lax.all_to_all(pay, ALL, 0, 0, tiled=True)  36.1 us
    all_to_all x3, blocking collectives, share(): return lax.all_to_all(pay, ALL, 0, 0, tiled=True)  34 us
    ppermute x21, waiting for transfers between devices, swap(): lax.ppermute(block, axis, [(i, i ^ distance) for i in range(lax.axis_size...  20.6 us
    all_to_all x2, waiting for transfers between devices, exchange(): return lax.all_to_all(block, SPACE, 0, 0, tiled=True)  20 us
    ppermute x3, waiting for transfers between devices, over_plane(): came.append(lax.ppermute(part, ('bhi', 'slo'), pairs) if i or j else part)  18 us
    ppermute x21, starting transfers between devices, swap(): lax.ppermute(block, axis, [(i, i ^ distance) for i in range(lax.axis_size...  14.1 us
  transfers between devices with their start and end apart: 46, of which 22 were waited for; matrix products, arithmetic and copies ran while one was open for 2% of the time, Pallas kernels for 14%

profile of v4, /device:TPU:0, one launch (start us, length us, event | category | flops | bytes accessed | tf_op | source)
XLA Modules:
  0.0 359.2 jit_solution(669837711976545691)
XLA Ops:
  9.4 7.3 %all-to-all-start = ((bf16[8,3,16,1024]{3,2,1,0:T(8,128)(2,1)}), bf16[8,3,16,1024]{3,2,1,0:T(8,128)(2,1)S(1)}, u32[]{:S(2)}, u32[]{:S(2)}) async-start(bf16[8,3,16,1024]{3,2,1,0:T(8,128)(2,1)} %bitcast.60), calls=%async_computation | async-start | bytes 1572864 | tf_op jit(solution)/shard_map/all_to_all | solution.py:1275
  16.8 20.0 %all-to-all-done.refs_1_ = bf16[8,3,16,1024]{3,2,1,0:T(8,128)(2,1)S(1)} async-done(((bf16[8,3,16,1024]{3,2,1,0:T(8,128)(2,1)}), bf16[8,3,16,1024]{3,2,1,0:T(8,128)(2,1)S(1)}, u32[]{:S(2)}, u32[]{:S(2)}) %all-to-all-start) | async-done | bytes 786464 | tf_op jit(solution)/shard_map/all_to_all | solution.py:1275
  39.6 12.1 %all_to_all.80.refs_1_ = bf16[32,24,128]{2,1,0:T(8,128)(2,1)} all-to-all(bf16[32,24,128]{2,1,0:T(8,128)(2,1)S(1)} %get-tuple-element.150), channel_id=1, replica_groups=mesh['bhi'=2,'core'=2,'shi'=4,'slo'=2] {'bhi','core','shi','slo'}, dimensions={0} | all-to-all | bytes 393216 | tf_op jit(solution)/shard_map/all_to_all | solution.py:1272
  51.7 3.8 %shard_map.408 = (bf16[384,2304]{1,0:T(8,128)(2,1)}, f32[384,256]{1,0:T(8,128)}, bf16[32,18,128]{2,1,0:T(8,128)(2,1)}, f32[12,128]{1,0:T(8,128)}, f32[32,6,128]{2,1,0:T(8,128)}) custom-call(f32[3]{0:T(128)} %copy-done.4, bf16[32,24,128]{2,1,0:T(8,128)(2,1)} %all_to_all.80.refs_1_, f32[384,256]{1,0:T(8,128)} %copy-done, f32[1,256]{1,0:T(1,128)} %bitcast.85, ...), custom_call_target="tpu_custom_call" | custom-call | flops 452984832 | bytes 4186112 | tf_op jit(solution)/shard_map/pallas_call | solution.py:136
  55.5 11.8 %all_to_all.81.refs_0_ = bf16[32,18,128]{2,1,0:T(8,128)(2,1)} all-to-all(bf16[32,18,128]{2,1,0:T(8,128)(2,1)} %get-tuple-element.152), channel_id=1, replica_groups=mesh['bhi'=2,'core'=2,'shi'=4,'slo'=2] {'bhi','core','shi','slo'}, dimensions={0} | all-to-all | bytes 294912 | tf_op jit(solution)/shard_map/all_to_all | solution.py:1272
  67.4 3.2 shard_map.409
  70.6 3.3 all-to-all-start.3
  77.7 8.4 %all-to-all-done.3.refs_0_ = bf16[32,40,128]{2,1,0:T(8,128)(2,1)} async-done(((bf16[32,40,128]{2,1,0:T(8,128)(2,1)}), bf16[32,40,128]{2,1,0:T(8,128)(2,1)}, u32[]{:S(2)}, u32[]{:S(2)}) %all-to-all-start.3) | async-done | bytes 327712 | tf_op jit(solution)/shard_map/all_to_all | solution.py:1272
  86.1 5.7 %shard_map.410 = (bf16[384,1024]{1,0:T(8,128)(2,1)}, bf16[384,1024]{1,0:T(8,128)(2,1)}, bf16[96,1024]{1,0:T(8,128)(2,1)}, f32[384,512]{1,0:T(8,128)}, bf16[32,36,128]{2,1,0:T(8,128)(2,1)}, /*index=5*/f32[48,128]{1,0:T(8,128)}) custom-call(bf16[32,40,128]{2,1,0:T(8,128)(2,1)} %all-to-all-done.3.refs_0_, f32[32,24,128]{2,1,0:T(8,128)} %broadcast_bitcast_fusion.refs_1_, ...), custom_call_target="tpu_custom_call" | custom-call | flops 402653184 | bytes 7585792 | tf_op jit(solution)/shard_map/pallas_call | solution.py:136
  95.3 11.3 %all-to-all-done.4.refs_0_ = bf16[32,36,128]{2,1,0:T(8,128)(2,1)S(1)} async-done(((bf16[32,36,128]{2,1,0:T(8,128)(2,1)}), bf16[32,36,128]{2,1,0:T(8,128)(2,1)S(1)}, u32[]{:S(2)}, u32[]{:S(2)}) %all-to-all-start.4) | async-done | bytes 294944 | tf_op jit(solution)/shard_map/all_to_all | solution.py:1272
  107.3 4.0 %shard_map.411 = (bf16[384,512]{1,0:T(8,128)(2,1)}, f32[96,512]{1,0:T(8,128)}, bf16[32,36,128]{2,1,0:T(8,128)(2,1)}, f32[24,128]{1,0:T(8,128)}) custom-call(bf16[32,36,128]{2,1,0:T(8,128)(2,1)} %copy-done.15, f32[32,12,128]{2,1,0:T(8,128)} %copy.93.refs_1_.refs_2_, f32[384,512]{1,0:T(8,128)} %get-tuple-element.158.refs_2_.refs_7_.refs_3_, ...), custom_call_target="tpu_custom_call" | custom-call | flops 452984832 | bytes 6897664 | tf_op jit(solution)/shard_map/pallas_call | solution.py:136
  114.0 3.6 %shard_map.412 = (f32[96,2048]{1,0:T(8,128)}, f32[16,8,128]{2,1,0:T(8,128)}) custom-call(bf16[96,1024]{1,0:T(8,128)(2,1)} %get-tuple-element.161.refs_0_.refs_17_, bf16[1024,2048]{1,0:T(8,128)(2,1)} %refs_1_.3), custom_call_target="tpu_custom_call" | custom-call | flops 402653184 | bytes 5242880 | tf_op jit(solution)/shard_map/pallas_call | solution.py:136
  117.6 8.5 %all-to-all-done.5.refs_0_ = bf16[32,36,128]{2,1,0:T(8,128)(2,1)S(1)} async-done(((bf16[32,36,128]{2,1,0:T(8,128)(2,1)}), bf16[32,36,128]{2,1,0:T(8,128)(2,1)S(1)}, u32[]{:S(2)}, u32[]{:S(2)}) %all-to-all-start.5) | async-done | bytes 294944 | tf_op jit(solution)/shard_map/all_to_all | solution.py:1272
  126.7 3.4 shard_map.413
  135.5 5.1 %all-to-all-done.6.refs_0_ = f32[32,8,128]{2,1,0:T(8,128)S(1)} async-done(((f32[32,8,128]{2,1,0:T(8,128)}), f32[32,8,128]{2,1,0:T(8,128)S(1)}, u32[]{:S(2)}, u32[]{:S(2)}) %all-to-all-start.6) | async-done | bytes 131104 | tf_op jit(solution)/shard_map/all_to_all | solution.py:1272
  141.2 10.1 %all_to_all.82.refs_0_.refs_1_ = f32[32,8,128]{2,1,0:T(8,128)} all-to-all(f32[32,8,128]{2,1,0:T(8,128)S(1)} %shard_map.414), channel_id=1, replica_groups=mesh['bhi'=2,'core'=2,'shi'=4,'slo'=2] {'bhi','core','shi','slo'}, dimensions={0} | all-to-all | bytes 262144 | tf_op jit(solution)/shard_map/all_to_all | solution.py:1272
  151.3 3.5 shard_map.415
  159.8 5.5 %all-to-all-done.8.refs_0_ = f32[32,8,128]{2,1,0:T(8,128)S(1)} async-done(((f32[32,8,128]{2,1,0:T(8,128)}), f32[32,8,128]{2,1,0:T(8,128)S(1)}, u32[]{:S(2)}, u32[]{:S(2)}) %all-to-all-start.8) | async-done | bytes 131104 | tf_op jit(solution)/shard_map/all_to_all | solution.py:1272
  171.0 4.4 %collective-permute-done.7.refs_23_ = bf16[96,512]{1,0:T(8,128)(2,1)S(1)} collective-permute-done((bf16[96,512]{1,0:T(8,128)(2,1)}, bf16[96,512]{1,0:T(8,128)(2,1)S(1)}, u32[]{:S(2)}, u32[]{:S(2)}) %collective-permute-start.7) | collective-permute-done | bytes 98336 | tf_op jit(solution)/shard_map/ppermute | solution.py:1278
  177.4 4.4 %shard_map.417 = (bf16[96,2048]{1,0:T(8,128)(2,1)}, f32[16,128]{1,0:T(8,128)}, f32[16,128]{1,0:T(8,128)}, f32[16,128]{1,0:T(8,128)}, f32[16,128]{1,0:T(8,128)}, ...) custom-call(s32[1]{0:T(128)} %bitcast.24.refs_0_, ...), custom_call_target="tpu_custom_call", output_to_operand_aliasing={{11}: (13, {}), {12}: (14, {}), {13}: (15, {}), {14}: (16, ... | custom-call | flops 201326592 | bytes 5767168 | tf_op jit(solution)/shard_map/pallas_call | solution.py:136
  181.8 5.2 %all-to-all-start.10 = ((bf16[32,24,128]{2,1,0:T(8,128)(2,1)}), bf16[32,24,128]{2,1,0:T(8,128)(2,1)S(1)}, u32[]{:S(2)}, u32[]{:S(2)}) async-start(bf16[32,24,128]{2,1,0:T(8,128)(2,1)} %get-tuple-element.172), calls=%async_computation.10 | async-start | bytes 393216 | tf_op jit(solution)/shard_map/all_to_all | solution.py:1272
  189.0 4.5 %shard_map.418.refs_16_ = f32[96,1024]{1,0:T(8,128)} custom-call(bf16[96,2048]{1,0:T(8,128)(2,1)} %get-tuple-element.179.refs_0_, bf16[1024,2048]{1,0:T(8,128)(2,1)} %refs_1_.3), custom_call_target="tpu_custom_call" | custom-call | flops 402653184 | bytes 4980736 | tf_op jit(solution)/shard_map/pallas_call | solution.py:136
  193.6 3.4 collective-permute-done.10.refs_14_
  197.0 3.5 collective-permute-done.11.refs_15_
  201.2 6.3 %shard_map.419 = (f32[4,128]{1,0:T(4,128)}, f32[4,128]{1,0:T(4,128)}, f32[384,512]{1,0:T(8,128)}, bf16[32,24,128]{2,1,0:T(8,128)(2,1)}, bf16[96,128]{1,0:T(8,128...) custom-call(s32[1]{0:T(128)} %bitcast.24.refs_0_, ...), custom_call_target="tpu_custom_call", output_to_operand_aliasing={{8}: (12, {}), {9}: (13, {}), {10}: (14, {}), {11}: (15, {}... | custom-call | flops 452984832 | bytes 7309312 | tf_op jit(solution)/shard_map/pallas_call | solution.py:136
  207.5 4.7 %all-to-all-start.11 = ((bf16[32,24,128]{2,1,0:T(8,128)(2,1)}), bf16[32,24,128]{2,1,0:T(8,128)(2,1)S(1)}, u32[]{:S(2)}, u32[]{:S(2)}) async-start(bf16[32,24,128]{2,1,0:T(8,128)(2,1)} %get-tuple-element.180), calls=%async_computation.11 | async-start | bytes 393216 | tf_op jit(solution)/shard_map/all_to_all | solution.py:1272
  214.2 3.8 %shard_map.420.refs_11_ = bf16[2,4,192,512]{3,2,1,0:T(8,128)(2,1)} custom-call(bf16[96,512]{1,0:T(8,128)(2,1)} %get-tuple-element.185.refs_0_, bf16[96,512]{1,0:T(8,128)(2,1)} %get-tuple-element.186.refs_1_, bf16[96,512]{1,0:T(8,128)(2,1)} %get-tuple-element.187.refs_2_, bf16[96,512]{1,0:T(8,128)(2,1)} %get-tuple-element.188.refs_3_, ...), custom_call_target="tpu_custom_call" | custom-call | flops 603979776 | bytes 1966080 | tf_op jit(solution)/shard_map/pallas_call | solution.py:136
  221.4 4.9 %shard_map.421 = (bf16[384,512]{1,0:T(8,128)(2,1)}, f32[4,128]{1,0:T(4,128)}, f32[4,128]{1,0:T(4,128)}, bf16[384,1024]{1,0:T(8,128)(2,1)}, bf16[32,48,128]{2,1,0...) custom-call(bf16[32,24,128]{2,1,0:T(8,128)(2,1)} %copy-done.22, ...), custom_call_target="tpu_custom_call", output_to_operand_aliasing={{5}: (11, {}), {6}: (12, {}), {7}: (13, {}), {8}: (14, {}),... | custom-call | flops 402653184 | bytes 7383040 | tf_op jit(solution)/shard_map/pallas_call | solution.py:136
  226.3 3.2 all-to-all-start.12
  229.6 4.1 %shard_map.422.refs_11_ = bf16[2,4,144,512]{3,2,1,0:T(8,128)(2,1)} custom-call(bf16[384,512]{1,0:T(8,128)(2,1)} %get-tuple-element.204.refs_0_, bf16[384,512]{1,0:T(8,128)(2,1)} %get-tuple-element.205.refs_1_, bf16[384,512]{1,0:T(8,128)(2,1)} %get-tuple-element.206.refs_2_, bf16[384,512]{1,0:T(8,128)(2,1)} %get-tuple-element.207.refs_3_, ...), custom_call_target="tpu_custom_call" | custom-call | flops 452984832 | bytes 1671168 | tf_op jit(solution)/shard_map/pallas_call | solution.py:136
  233.7 9.4 %all-to-all-done.12.refs_0_ = bf16[32,48,128]{2,1,0:T(8,128)(2,1)S(1)} async-done(((bf16[32,48,128]{2,1,0:T(8,128)(2,1)}), bf16[32,48,128]{2,1,0:T(8,128)(2,1)S(1)}, u32[]{:S(2)}, u32[]{:S(2)}) %all-to-all-start.12) | async-done | bytes 393248 | tf_op jit(solution)/shard_map/all_to_all | solution.py:1272
  243.8 4.1 %shard_map.423 = (bf16[384,1024]{1,0:T(8,128)(2,1)}, f32[8,128]{1,0:T(8,128)}, f32[8,128]{1,0:T(8,128)}, f32[384,256]{1,0:T(8,128)}, bf16[32,12,128]{2,1,0:T(8,128)(2,1)}, /*index=5*/bf16[2,4,144,512]{3,2,1,0:T(8,128)(2,1)}) custom-call(bf16[32,48,128]{2,1,0:T(8,128)(2,1)} %copy-done.13, ...), custom_call_target="tpu_custom_call", output_to_operand_aliasing={{5}: (11, {})} | custom-call | flops 201326592 | bytes 5386240 | tf_op jit(solution)/shard_map/pallas_call | solution.py:136
  248.0 2.9 all-to-all-start.13
  252.5 3.8 %shard_map.424 = (bf16[4,2,2,96,256]{4,3,2,1,0:T(8,128)(2,1)}, bf16[4,2,2,96,256]{4,3,2,1,0:T(8,128)(2,1)}) custom-call(s32[1]{0:T(128)} %bitcast.24.refs_0_, bf16[384,1024]{1,0:T(8,128)(2,1)} %get-tuple-element.215.refs_1_, bf16[384,512]{1,0:T(8,128)(2,1)} %get-tuple-element.216.refs_2_, bf16[384,256]{1,0:T(8,128)(2,1)} %get-tuple-element.217.refs_3_, ...), custom_call_target="tpu_custom_call" | custom-call | flops 603979776 | bytes 2162688 | tf_op jit(solution)/shard_map/pallas_call | solution.py:136
  259.1 3.6 shard_map.425
  262.9 3.5 all-to-all-start.14
  267.1 3.4 shard_map.426
  270.4 3.8 %all-to-all-done.14.refs_1_ = bf16[32,12,128]{2,1,0:T(8,128)(2,1)S(1)} async-done(((bf16[32,12,128]{2,1,0:T(8,128)(2,1)}), bf16[32,12,128]{2,1,0:T(8,128)(2,1)S(1)}, u32[]{:S(2)}, u32[]{:S(2)}) %all-to-all-start.14) | async-done | bytes 98336 | tf_op jit(solution)/shard_map/all_to_all | solution.py:1272
  275.1 3.0 shard_map.427
  281.7 4.6 %shard_map.428 = (bf16[4,200,256]{2,1,0:T(8,128)(2,1)}, bf16[4,200,256]{2,1,0:T(8,128)(2,1)}, bf16[4,200,256]{2,1,0:T(8,128)(2,1)}, bf16[4,200,256]{2,1,0:T(8,128)(2,1)}, bf16[4,336,512]{2,1,0:T(8,128)(2,1)}) custom-call(s32[3]{0:T(128)} %get-tuple-element.228.refs_0_, bf16[4,2,2,96,256]{4,3,2,1,0:T(8,128)(2,1)} %get-tuple-element.229.refs_1_, ...), custom_call_target="tpu_custom_call" | custom-call | bytes 4653056 | tf_op jit(solution)/shard_map/pallas_call | solution.py:136
  289.9 9.0 %collective-permute-done.18.refs_4_ = bf16[4,200,256]{2,1,0:T(8,128)(2,1)S(1)} collective-permute-done((bf16[4,200,256]{2,1,0:T(8,128)(2,1)}, bf16[4,200,256]{2,1,0:T(8,128)(2,1)S(1)}, u32[]{:S(2)}, u32[]{:S(2)}) %collective-permute-start.18) | collective-permute-done | bytes 409632 | tf_op jit(solution)/shard_map/ppermute | solution.py:1408
  298.9 8.9 %collective-permute-done.19.refs_5_ = bf16[4,200,256]{2,1,0:T(8,128)(2,1)S(1)} collective-permute-done((bf16[4,200,256]{2,1,0:T(8,128)(2,1)}, bf16[4,200,256]{2,1,0:T(8,128)(2,1)S(1)}, u32[]{:S(2)}, u32[]{:S(2)}) %collective-permute-start.19) | collective-permute-done | bytes 409632 | tf_op jit(solution)/shard_map/ppermute | solution.py:1408
  308.6 2.8 shard_map.429
  311.4 4.6 %all-to-all-start.15 = ((bf16[8,3,16,1024]{3,2,1,0:T(8,128)(2,1)}), bf16[8,3,16,1024]{3,2,1,0:T(8,128)(2,1)S(1)}, u32[]{:S(2)}, u32[]{:S(2)}) async-start(bf16[8,3,16,1024]{3,2,1,0:T(8,128)(2,1)} %get-tuple-element.241), calls=%async_computation.17 | async-start | bytes 1572864 | tf_op jit(solution)/shard_map/all_to_all | solution.py:1275
  318.8 3.0 shard_map.430
  323.4 8.3 %collective-permute-done.25.refs_3_ = bf16[336,512]{1,0:T(8,128)(2,1)S(1)} collective-permute-done((bf16[336,512]{1,0:T(8,128)(2,1)}, bf16[336,512]{1,0:T(8,128)(2,1)S(1)}, u32[]{:S(2)}, u32[]{:S(2)}) %collective-permute-start.25) | collective-permute-done | bytes 344096 | tf_op jit(solution)/shard_map/ppermute | solution.py:1278
  339.5 3.5 collective-permute-done.22.refs_2_
  346.4 3.4 collective-permute-done.28.refs_3_
  (168 shorter events, 76.0 us)
Async XLA Ops:
  7.2 29.6 %copy-start.1 = (bf16[1024,256]{1,0:T(8,128)(2,1)S(1)}, bf16[1024,256]{1,0:T(8,128)(2,1)}, u32[]{:S(2)}) copy-start(bf16[1024,256]{1,0:T(8,128)(2,1)} %refs_2_.3) | copy-start | bytes 1572868
  9.4 27.4 %all-to-all-start = ((bf16[8,3,16,1024]{3,2,1,0:T(8,128)(2,1)}), bf16[8,3,16,1024]{3,2,1,0:T(8,128)(2,1)S(1)}, u32[]{:S(2)}, u32[]{:S(2)}) async-start(bf16[8,3,16,1024]{3,2,1,0:T(8,128)(2,1)} %bitcast.60), calls=%async_computation | async-start | bytes 1572864 | tf_op jit(solution)/shard_map/all_to_all | solution.py:1275
  16.8 34.9 %copy-start.4 = (f32[3]{0:T(128)}, f32[3]{0:T(128)S(1)}, u32[]{:S(2)}) copy-start(f32[3]{0:T(128)S(1)} %convert_reduce_fusion.refs_0_) | copy-start | bytes 40
  70.6 15.5 %all-to-all-start.3 = ((bf16[32,40,128]{2,1,0:T(8,128)(2,1)}), bf16[32,40,128]{2,1,0:T(8,128)(2,1)}, u32[]{:S(2)}, u32[]{:S(2)}) async-start(bf16[32,40,128]{2,1,0:T(8,128)(2,1)} %get-tuple-element.155), calls=%async_computation.3 | async-start | bytes 655360 | tf_op jit(solution)/shard_map/all_to_all | solution.py:1272
  91.8 14.8 %all-to-all-start.4 = ((bf16[32,36,128]{2,1,0:T(8,128)(2,1)}), bf16[32,36,128]{2,1,0:T(8,128)(2,1)S(1)}, u32[]{:S(2)}, u32[]{:S(2)}) async-start(bf16[32,36,128]{2,1,0:T(8,128)(2,1)} %get-tuple-element.157), calls=%async_computation.4 | async-start | bytes 655360 | tf_op jit(solution)/shard_map/all_to_all | solution.py:1272
  111.3 14.8 %all-to-all-start.5 = ((bf16[32,36,128]{2,1,0:T(8,128)(2,1)}), bf16[32,36,128]{2,1,0:T(8,128)(2,1)S(1)}, u32[]{:S(2)}, u32[]{:S(2)}) async-start(bf16[32,36,128]{2,1,0:T(8,128)(2,1)} %get-tuple-element.159), calls=%async_computation.5 | async-start | bytes 655360 | tf_op jit(solution)/shard_map/all_to_all | solution.py:1272
  130.2 10.3 %all-to-all-start.6 = ((f32[32,8,128]{2,1,0:T(8,128)}), f32[32,8,128]{2,1,0:T(8,128)S(1)}, u32[]{:S(2)}, u32[]{:S(2)}) async-start(f32[32,8,128]{2,1,0:T(8,128)} %get-tuple-element.163), calls=%async_computation.6 | async-start | bytes 262144 | tf_op jit(solution)/shard_map/all_to_all | solution.py:1272
  133.7 25.7 %collective-permute-start.1 = (bf16[384,512]{1,0:T(8,128)(2,1)S(1)}, bf16[384,512]{1,0:T(8,128)(2,1)}, u32[]{:S(2)}, u32[]{:S(2)}) collective-permute-start(bf16[384,512]{1,0:T(8,128)(2,1)S(1)} %copy-done.11), channel_id=1, source_target_pairs={{0,16},{16,0},{1,17},{17,1},{2,18},{18,2},{3,19},{19,3},{4,20},{20... | collective-permute-start | bytes 1179656 | tf_op jit(solution)/shard_map/ppermute | solution.py:1278
  154.8 10.5 %all-to-all-start.8 = ((f32[32,8,128]{2,1,0:T(8,128)}), f32[32,8,128]{2,1,0:T(8,128)S(1)}, u32[]{:S(2)}, u32[]{:S(2)}) async-start(f32[32,8,128]{2,1,0:T(8,128)} %get-tuple-element.167), calls=%async_computation.8 | async-start | bytes 262144 | tf_op jit(solution)/shard_map/all_to_all | solution.py:1272
  157.6 11.4 %collective-permute-start.4 = (bf16[96,1024]{1,0:T(8,128)(2,1)S(1)}, bf16[96,1024]{1,0:T(8,128)(2,1)S(1)}, u32[]{:S(2)}, u32[]{:S(2)}) collective-permute-start(bf16[96,1024]{1,0:T(8,128)(2,1)S(1)} %copy-done.8), channel_id=1, source_target_pairs={{0,16},{16,0},{1,17},{17,1},{2,18},{18,2},{3,19},{19,3},{4,20},{20... | collective-permute-start | bytes 589832 | tf_op jit(solution)/shard_map/ppermute | solution.py:1278
  159.3 16.1 %collective-permute-start = (bf16[384,512]{1,0:T(8,128)(2,1)S(1)}, bf16[384,512]{1,0:T(8,128)(2,1)S(1)}, u32[]{:S(2)}, u32[]{:S(2)}) collective-permute-start(bf16[384,512]{1,0:T(8,128)(2,1)S(1)} %copy-done.11), channel_id=1, source_target_pairs={{0,8},{8,0},{1,9},{9,1},{2,10},{10,2},{3,11},{11,3},{4,12},{12,4},... | collective-permute-start | bytes 1179656 | tf_op jit(solution)/shard_map/ppermute | solution.py:1278
  159.3 17.4 %collective-permute-start.2 = (bf16[384,512]{1,0:T(8,128)(2,1)}, bf16[384,512]{1,0:T(8,128)(2,1)}, u32[]{:S(2)}, u32[]{:S(2)}) collective-permute-start(bf16[384,512]{1,0:T(8,128)(2,1)} %collective-permute-done.1.refs_15_), channel_id=1, source_target_pairs={{0,8},{8,0},{1,9},{9,1},{2,10},{10,2},{3,11},{11,3},{4,12},{12,4},... | collective-permute-start | bytes 1179656 | tf_op jit(solution)/shard_map/ppermute | solution.py:1278
  159.8 11.1 %collective-permute-start.3 = (bf16[96,1024]{1,0:T(8,128)(2,1)S(1)}, bf16[96,1024]{1,0:T(8,128)(2,1)S(1)}, u32[]{:S(2)}, u32[]{:S(2)}) collective-permute-start(bf16[96,1024]{1,0:T(8,128)(2,1)S(1)} %copy-done.8), channel_id=1, source_target_pairs={{0,8},{8,0},{1,9},{9,1},{2,10},{10,2},{3,11},{11,3},{4,12},{12,4},... | collective-permute-start | bytes 589832 | tf_op jit(solution)/shard_map/ppermute | solution.py:1278
  166.4 10.3 %all-to-all-start.9 = ((f32[32,8,128]{2,1,0:T(8,128)}), f32[32,8,128]{2,1,0:T(8,128)S(1)}, u32[]{:S(2)}, u32[]{:S(2)}) async-start(f32[32,8,128]{2,1,0:T(8,128)} %shard_map.416), calls=%async_computation.9 | async-start | bytes 262144 | tf_op jit(solution)/shard_map/all_to_all | solution.py:1272
  169.0 6.4 %collective-permute-start.5 = (bf16[96,1024]{1,0:T(8,128)(2,1)S(1)}, bf16[96,1024]{1,0:T(8,128)(2,1)S(1)}, u32[]{:S(2)}, u32[]{:S(2)}) collective-permute-start(bf16[96,1024]{1,0:T(8,128)(2,1)S(1)} %collective-permute-done.4.refs_19_), channel_id=1, source_target_pairs={{0,8},{8,0},{1,9},{9,1},{2,10},{10,2},{3,11},{11,3},{4,12},{12,4},... | collective-permute-start | bytes 589832 | tf_op jit(solution)/shard_map/ppermute | solution.py:1278
  169.2 6.2 %collective-permute-start.7 = (bf16[96,512]{1,0:T(8,128)(2,1)}, bf16[96,512]{1,0:T(8,128)(2,1)S(1)}, u32[]{:S(2)}, u32[]{:S(2)}) collective-permute-start(bf16[96,512]{1,0:T(8,128)(2,1)} %get-tuple-element.171.refs_21_), channel_id=1, source_target_pairs={{0,16},{16,0},{1,17},{17,1},{2,18},{18,2},{3,19},{19,3},{4,20},{20... | collective-permute-start | bytes 294920 | tf_op jit(solution)/shard_map/ppermute | solution.py:1278
  170.9 5.4 %collective-permute-start.6 = (bf16[96,512]{1,0:T(8,128)(2,1)}, bf16[96,512]{1,0:T(8,128)(2,1)S(1)}, u32[]{:S(2)}, u32[]{:S(2)}) collective-permute-start(bf16[96,512]{1,0:T(8,128)(2,1)} %get-tuple-element.171.refs_21_), channel_id=1, source_target_pairs={{0,8},{8,0},{1,9},{9,1},{2,10},{10,2},{3,11},{11,3},{4,12},{12,4},... | collective-permute-start | bytes 294920 | tf_op jit(solution)/shard_map/ppermute | solution.py:1278
  175.4 1.3 collective-permute-start.8
  181.8 18.7 %all-to-all-start.10 = ((bf16[32,24,128]{2,1,0:T(8,128)(2,1)}), bf16[32,24,128]{2,1,0:T(8,128)(2,1)S(1)}, u32[]{:S(2)}, u32[]{:S(2)}) async-start(bf16[32,24,128]{2,1,0:T(8,128)(2,1)} %get-tuple-element.172), calls=%async_computation.10 | async-start | bytes 393216 | tf_op jit(solution)/shard_map/all_to_all | solution.py:1272
  187.0 6.5 %collective-permute-start.9 = (bf16[96,1024]{1,0:T(8,128)(2,1)}, bf16[96,1024]{1,0:T(8,128)(2,1)S(1)}, u32[]{:S(2)}, u32[]{:S(2)}) collective-permute-start(bf16[96,1024]{1,0:T(8,128)(2,1)} %get-tuple-element.176), channel_id=1, source_target_pairs={{0,8},{8,0},{16,24},{24,16},{1,9},{9,1},{17,25},{25,17},{2,10},{10... | collective-permute-start | bytes 589832 | tf_op jit(solution)/shard_map/ppermute | solution.py:1282
  187.4 9.6 %collective-permute-start.10 = (bf16[96,1024]{1,0:T(8,128)(2,1)}, bf16[96,1024]{1,0:T(8,128)(2,1)S(1)}, u32[]{:S(2)}, u32[]{:S(2)}) collective-permute-start(bf16[96,1024]{1,0:T(8,128)(2,1)} %get-tuple-element.177), channel_id=1, source_target_pairs={{0,16},{8,24},{16,0},{24,8},{1,17},{9,25},{17,1},{25,9},{2,18},{10... | collective-permute-start | bytes 589832 | tf_op jit(solution)/shard_map/ppermute | solution.py:1282
  189.0 11.5 %collective-permute-start.11 = (bf16[96,1024]{1,0:T(8,128)(2,1)}, bf16[96,1024]{1,0:T(8,128)(2,1)S(1)}, u32[]{:S(2)}, u32[]{:S(2)}) collective-permute-start(bf16[96,1024]{1,0:T(8,128)(2,1)} %get-tuple-element.178), channel_id=1, source_target_pairs={{0,24},{8,16},{16,8},{24,0},{1,25},{9,17},{17,9},{25,1},{2,26},{10... | collective-permute-start | bytes 589832 | tf_op jit(solution)/shard_map/ppermute | solution.py:1282
  207.5 13.2 %all-to-all-start.11 = ((bf16[32,24,128]{2,1,0:T(8,128)(2,1)}), bf16[32,24,128]{2,1,0:T(8,128)(2,1)S(1)}, u32[]{:S(2)}, u32[]{:S(2)}) async-start(bf16[32,24,128]{2,1,0:T(8,128)(2,1)} %get-tuple-element.180), calls=%async_computation.11 | async-start | bytes 393216 | tf_op jit(solution)/shard_map/all_to_all | solution.py:1272
  212.2 46.3 %reduce-scatter.4.cloned.1.call-start = ((), (), s32[]{:S(2)}) async-start(), calls=%async_computation.19 | async-start | bytes 2359296 | tf_op jit(solution)/shard_map/reduce_scatter | solution.py:1377
  212.2 5.9 %collective-permute-start.12 = (bf16[96,128]{1,0:T(8,128)(2,1)}, bf16[96,128]{1,0:T(8,128)(2,1)S(1)}, u32[]{:S(2)}, u32[]{:S(2)}) collective-permute-start(bf16[96,128]{1,0:T(8,128)(2,1)} %get-tuple-element.198), channel_id=1, source_target_pairs={{0,8},{8,0},{16,24},{24,16},{1,9},{9,1},{17,25},{25,17},{2,10},{10... | collective-permute-start | bytes 73736 | tf_op jit(solution)/shard_map/ppermute | solution.py:1282
  212.5 5.6 %collective-permute-start.13 = (bf16[96,128]{1,0:T(8,128)(2,1)}, bf16[96,128]{1,0:T(8,128)(2,1)S(1)}, u32[]{:S(2)}, u32[]{:S(2)}) collective-permute-start(bf16[96,128]{1,0:T(8,128)(2,1)} %get-tuple-element.199), channel_id=1, source_target_pairs={{0,16},{8,24},{16,0},{24,8},{1,17},{9,25},{17,1},{25,9},{2,18},{10... | collective-permute-start | bytes 73736 | tf_op jit(solution)/shard_map/ppermute | solution.py:1282
  214.2 3.9 %collective-permute-start.14 = (bf16[96,128]{1,0:T(8,128)(2,1)}, bf16[96,128]{1,0:T(8,128)(2,1)S(1)}, u32[]{:S(2)}, u32[]{:S(2)}) collective-permute-start(bf16[96,128]{1,0:T(8,128)(2,1)} %get-tuple-element.200), channel_id=1, source_target_pairs={{0,24},{8,16},{16,8},{24,0},{1,25},{9,17},{17,9},{25,1},{2,26},{10... | collective-permute-start | bytes 73736 | tf_op jit(solution)/shard_map/ppermute | solution.py:1282
  226.3 16.8 %all-to-all-start.12 = ((bf16[32,48,128]{2,1,0:T(8,128)(2,1)}), bf16[32,48,128]{2,1,0:T(8,128)(2,1)S(1)}, u32[]{:S(2)}, u32[]{:S(2)}) async-start(bf16[32,48,128]{2,1,0:T(8,128)(2,1)} %get-tuple-element.201), calls=%async_computation.12 | async-start | bytes 786432 | tf_op jit(solution)/shard_map/all_to_all | solution.py:1272
  229.6 51.2 %reduce-scatter.6.cloned.1.call-start = ((), (), s32[]{:S(2)}) async-start(), calls=%async_computation.20 | async-start | bytes 1769472 | tf_op jit(solution)/shard_map/reduce_scatter | solution.py:1385
  248.0 10.5 %all-to-all-start.13 = ((bf16[32,12,128]{2,1,0:T(8,128)(2,1)}), bf16[32,12,128]{2,1,0:T(8,128)(2,1)S(1)}, u32[]{:S(2)}, u32[]{:S(2)}) async-start(bf16[32,12,128]{2,1,0:T(8,128)(2,1)} %get-tuple-element.212), calls=%async_computation.13 | async-start | bytes 262144 | tf_op jit(solution)/shard_map/all_to_all | solution.py:1272
  262.7 11.5 %collective-permute-start.15 = (bf16[4,2,2,96,256]{4,3,2,1,0:T(8,128)(2,1)}, bf16[4,2,2,96,256]{4,3,2,1,0:T(8,128)(2,1)S(1)}, u32[]{:S(2)}, u32[]{:S(2)}) collective-permute-start(bf16[4,2,2,96,256]{4,3,2,1,0:T(8,128)(2,1)} %get-tuple-element.226), channel_id=1, source_target_pairs={{0,8},{8,0},{1,9},{9,1},{2,10},{10,2},{3,11},{11,3},{4,12},{12,4},... | collective-permute-start | bytes 2359304 | tf_op jit(solution)/shard_map/ppermute | solution.py:1278
  262.9 11.3 %all-to-all-start.14 = ((bf16[32,12,128]{2,1,0:T(8,128)(2,1)}), bf16[32,12,128]{2,1,0:T(8,128)(2,1)S(1)}, u32[]{:S(2)}, u32[]{:S(2)}) async-start(bf16[32,12,128]{2,1,0:T(8,128)(2,1)} %get-tuple-element.221), calls=%async_computation.15 | async-start | bytes 262144 | tf_op jit(solution)/shard_map/all_to_all | solution.py:1272
  266.4 52.3 %reduce-scatter.8.cloned.1.call-start = ((), (), s32[]{:S(2)}) async-start(), calls=%async_computation.21 | async-start | bytes 1720320 | tf_op jit(solution)/shard_map/reduce_scatter | solution.py:1424
  278.1 2.7 collective-permute-start.16
  278.3 2.5 collective-permute-start.17
  286.4 12.6 %collective-permute-start.18 = (bf16[4,200,256]{2,1,0:T(8,128)(2,1)}, bf16[4,200,256]{2,1,0:T(8,128)(2,1)S(1)}, u32[]{:S(2)}, u32[]{:S(2)}) collective-permute-start(bf16[4,200,256]{2,1,0:T(8,128)(2,1)} %get-tuple-element.238), channel_id=1, source_target_pairs={{0,1},{1,0},{16,17},{17,16},{2,3},{3,2},{18,19},{19,18},{4,5},{5,4... | collective-permute-start | bytes 1228808 | tf_op jit(solution)/shard_map/ppermute | solution.py:1408
  287.7 20.2 %collective-permute-start.19 = (bf16[4,200,256]{2,1,0:T(8,128)(2,1)}, bf16[4,200,256]{2,1,0:T(8,128)(2,1)S(1)}, u32[]{:S(2)}, u32[]{:S(2)}) collective-permute-start(bf16[4,200,256]{2,1,0:T(8,128)(2,1)} %get-tuple-element.239), channel_id=1, source_target_pairs={{0,16},{1,17},{16,0},{17,1},{2,18},{3,19},{18,2},{19,3},{4,20},{5,... | collective-permute-start | bytes 1228808 | tf_op jit(solution)/shard_map/ppermute | solution.py:1408
  288.5 19.4 %collective-permute-start.20 = (bf16[4,200,256]{2,1,0:T(8,128)(2,1)}, bf16[4,200,256]{2,1,0:T(8,128)(2,1)}, u32[]{:S(2)}, u32[]{:S(2)}) collective-permute-start(bf16[4,200,256]{2,1,0:T(8,128)(2,1)} %get-tuple-element.240), channel_id=1, source_target_pairs={{0,17},{1,16},{16,1},{17,0},{2,19},{3,18},{18,3},{19,2},{4,21},{5,... | collective-permute-start | bytes 1228808 | tf_op jit(solution)/shard_map/ppermute | solution.py:1408
  311.4 38.4 %all-to-all-start.15 = ((bf16[8,3,16,1024]{3,2,1,0:T(8,128)(2,1)}), bf16[8,3,16,1024]{3,2,1,0:T(8,128)(2,1)S(1)}, u32[]{:S(2)}, u32[]{:S(2)}) async-start(bf16[8,3,16,1024]{3,2,1,0:T(8,128)(2,1)} %get-tuple-element.241), calls=%async_computation.17 | async-start | bytes 1572864 | tf_op jit(solution)/shard_map/all_to_all | solution.py:1275
  321.8 9.9 %collective-permute-start.25 = (bf16[336,512]{1,0:T(8,128)(2,1)}, bf16[336,512]{1,0:T(8,128)(2,1)S(1)}, u32[]{:S(2)}, u32[]{:S(2)}) collective-permute-start(bf16[336,512]{1,0:T(8,128)(2,1)} %bitcast.61), channel_id=1, source_target_pairs={{0,16},{16,0},{1,17},{17,1},{2,18},{18,2},{3,19},{19,3},{4,20},{20... | collective-permute-start | bytes 1032200 | tf_op jit(solution)/shard_map/ppermute | solution.py:1278
  323.4 12.7 %collective-permute-start.24 = (bf16[336,512]{1,0:T(8,128)(2,1)}, bf16[336,512]{1,0:T(8,128)(2,1)S(1)}, u32[]{:S(2)}, u32[]{:S(2)}) collective-permute-start(bf16[336,512]{1,0:T(8,128)(2,1)} %bitcast.62), channel_id=1, source_target_pairs={{0,8},{8,0},{1,9},{9,1},{2,10},{10,2},{3,11},{11,3},{4,12},{12,4},... | collective-permute-start | bytes 1032200 | tf_op jit(solution)/shard_map/ppermute | solution.py:1278
  331.7 4.4 %collective-permute-start.26 = (bf16[336,512]{1,0:T(8,128)(2,1)S(1)}, bf16[336,512]{1,0:T(8,128)(2,1)S(1)}, u32[]{:S(2)}, u32[]{:S(2)}) collective-permute-start(bf16[336,512]{1,0:T(8,128)(2,1)S(1)} %collective-permute-done.25.refs_3_), channel_id=1, source_target_pairs={{0,8},{8,0},{1,9},{9,1},{2,10},{10,2},{3,11},{11,3},{4,12},{12,4},... | collective-permute-start | bytes 1032200 | tf_op jit(solution)/shard_map/ppermute | solution.py:1278
  331.7 7.8 %collective-permute-start.21 = (bf16[200,256]{1,0:T(8,128)(2,1)}, bf16[200,256]{1,0:T(8,128)(2,1)S(1)}, u32[]{:S(2)}, u32[]{:S(2)}) collective-permute-start(bf16[200,256]{1,0:T(8,128)(2,1)} %get-tuple-element.248), channel_id=1, source_target_pairs={{0,2},{2,0},{4,6},{6,4},{1,3},{3,1},{5,7},{7,5},{8,10},{10,8},{12,... | collective-permute-start | bytes 307208 | tf_op jit(solution)/shard_map/ppermute | solution.py:1278
  331.7 11.3 %collective-permute-start.22 = (bf16[200,256]{1,0:T(8,128)(2,1)}, bf16[200,256]{1,0:T(8,128)(2,1)}, u32[]{:S(2)}, u32[]{:S(2)}) collective-permute-start(bf16[200,256]{1,0:T(8,128)(2,1)} %get-tuple-element.249), channel_id=1, source_target_pairs={{0,4},{2,6},{4,0},{6,2},{1,5},{3,7},{5,1},{7,3},{8,12},{10,14},{12... | collective-permute-start | bytes 307208 | tf_op jit(solution)/shard_map/ppermute | solution.py:1278
  333.8 9.2 %collective-permute-start.23 = (bf16[200,256]{1,0:T(8,128)(2,1)}, bf16[200,256]{1,0:T(8,128)(2,1)}, u32[]{:S(2)}, u32[]{:S(2)}) collective-permute-start(bf16[200,256]{1,0:T(8,128)(2,1)} %get-tuple-element.250), channel_id=1, source_target_pairs={{0,6},{2,4},{4,2},{6,0},{1,7},{3,5},{5,3},{7,1},{8,14},{10,12},{12... | collective-permute-start | bytes 307208 | tf_op jit(solution)/shard_map/ppermute | solution.py:1278
  344.9 4.9 %collective-permute-start.28 = (bf16[200,256]{1,0:T(8,128)(2,1)}, bf16[200,256]{1,0:T(8,128)(2,1)S(1)}, u32[]{:S(2)}, u32[]{:S(2)}) collective-permute-start(bf16[200,256]{1,0:T(8,128)(2,1)} %get-tuple-element.255.refs_1_), channel_id=1, source_target_pairs={{0,16},{16,0},{1,17},{17,1},{2,18},{18,2},{3,19},{19,3},{4,20},{20... | collective-permute-start | bytes 307208 | tf_op jit(solution)/shard_map/ppermute | solution.py:1278
  346.4 4.4 %collective-permute-start.27 = (bf16[200,256]{1,0:T(8,128)(2,1)}, bf16[200,256]{1,0:T(8,128)(2,1)S(1)}, u32[]{:S(2)}, u32[]{:S(2)}) collective-permute-start(bf16[200,256]{1,0:T(8,128)(2,1)} %get-tuple-element.255.refs_1_), channel_id=1, source_target_pairs={{0,8},{8,0},{1,9},{9,1},{2,10},{10,2},{3,11},{11,3},{4,12},{12,4},... | collective-permute-start | bytes 307208 | tf_op jit(solution)/shard_map/ppermute | solution.py:1278
  349.8 1.3 collective-permute-start.29
  (35 other events, 109.1 us)
Sparse Core Ops, SparseCore 0:
  226.4 28.3 reduce-scatter.3
  257.7 23.0 reduce-scatter.5
  286.5 32.2 reduce-scatter.7
